TPU v7x, 32 devices: a whole 2x2x4 slice. The times are simulated.
32 devices in a mesh: gx: 4 (over x, core), gy: 2 (over y), gz: 4 (over z).
Axes of the slice: x: 2, y: 2, z: 4, core: 2. Of those that a mesh axis runs over, the one named last changes fastest.
Arguments:
- solution: float32 [3, 32, 32, 512], P(None, 'gx', 'gy', 'gz'), may hold values from -6 to 6
- residual: float32 [3, 32, 32, 512], P(None, 'gx', 'gy', 'gz'), may hold values from -18 to 18
- direction: float32 [3, 32, 32, 512], P(None, 'gx', 'gy', 'gz'), may hold values from -18 to 18
- density: float32 [32, 32, 512], P('gx', 'gy', 'gz'), may hold values from 0.2 to 1
- labels: int32 [32, 32, 512], P('gx', 'gy', 'gz'), may hold values from 0 to 2
Outputs:
- new_solution: float32 [3, 32, 32, 512], P(None, 'gx', 'gy', 'gz')
- new_residual: float32 [3, 32, 32, 512], P(None, 'gx', 'gy', 'gz')
- new_direction: float32 [3, 32, 32, 512], P(None, 'gx', 'gy', 'gz')
- sensitivity: float32 [32, 32, 512], P('gx', 'gy', 'gz')
All inputs are finite; a program needn't handle non-finite values.
Results may differ from a plain program's by a relative error of at most 0.0003.
Values sent between devices are 32-bit elements; how exact they have to be, the bound alone decides.
No kernel may reach another device: no remote copies, remote signals or barrier semaphores. Data moves between devices by JAX's collectives and lax.ppermute only.
A program may use at most 64 MiB of HBM per device.

v0:
```python
import math

import jax
import jax.numpy as jnp
from jax import lax
from jax.sharding import PartitionSpec as P

RAD = 3


stiff_floor = 0.001
penalty = 3.0
neighbour_offsets = [
    (off_x, off_y, off_z)
    for off_x in (-1, 0, 1)
    for off_y in (-1, 0, 1)
    for off_z in (-1, 0, 1)
    if (off_x, off_y, off_z) != (0, 0, 0)
]


def with_halo(block, sides, width):
    for axis, dim in sides:
        count = lax.axis_size(axis)
        forward = [(i, i + 1) for i in range(count - 1)]
        backward = [(target, source) for source, target in forward]
        low = lax.ppermute(
            lax.slice_in_dim(block, block.shape[dim] - width, None, axis=dim), axis, forward
        )
        high = lax.ppermute(lax.slice_in_dim(block, 0, width, axis=dim), axis, backward)
        block = jnp.concatenate([low, block, high], axis=dim)
    return block


def filter_table(reach):
    table = []
    for off_x in range(-reach, reach + 1):
        for off_y in range(-reach, reach + 1):
            for off_z in range(-reach, reach + 1):
                distance = math.sqrt(off_x * off_x + off_y * off_y + off_z * off_z)
                weight = reach + 0.5 - distance
                if weight > 0:
                    table.append((off_x, off_y, off_z, weight))
    return table


def shifted(padded, shift_x, shift_y, shift_z, depth):
    size_x = padded.shape[-3] - 2 * depth
    size_y = padded.shape[-2] - 2 * depth
    size_z = padded.shape[-1] - 2 * depth
    return padded[
        ...,
        depth + shift_x : depth + shift_x + size_x,
        depth + shift_y : depth + shift_y + size_y,
        depth + shift_z : depth + shift_z + size_z,
    ]


def pull(differ, off_x, off_y, off_z):
    norm_sq = float(off_x * off_x + off_y * off_y + off_z * off_z)
    along = (off_x * differ[0] + off_y * differ[1] + off_z * differ[2]) / (norm_sq * norm_sq)
    return jnp.stack(
        [
            differ[0] / norm_sq + off_x * along,
            differ[1] / norm_sq + off_y * along,
            differ[2] / norm_sq + off_z * along,
        ]
    )


def corner_entries(off_x, off_y, off_z):
    norm_sq = float(off_x * off_x + off_y * off_y + off_z * off_z)
    values = [
        1.0 / norm_sq + off_x * off_x / (norm_sq * norm_sq),
        1.0 / norm_sq + off_y * off_y / (norm_sq * norm_sq),
        1.0 / norm_sq + off_z * off_z / (norm_sq * norm_sq),
    ]
    return jnp.array(values, dtype=jnp.float32).reshape(3, 1, 1, 1)


def couple(padded, stiff_pad):
    center = shifted(padded, 0, 0, 0, 1)
    stiff_mid = shifted(stiff_pad, 0, 0, 0, 1)
    total = jnp.zeros_like(center)
    diagonal = jnp.zeros_like(center)
    for off_x, off_y, off_z in neighbour_offsets:
        weight = 0.5 * (stiff_mid + shifted(stiff_pad, off_x, off_y, off_z, 1))
        differ = center - shifted(padded, off_x, off_y, off_z, 1)
        total = total + weight[None] * pull(differ, off_x, off_y, off_z)
        diagonal = diagonal + weight[None] * corner_entries(off_x, off_y, off_z)
    return (total, diagonal)


def energy(padded):
    center = shifted(padded, 0, 0, 0, 1)
    total = jnp.zeros_like(center[0])
    for off_x, off_y, off_z in neighbour_offsets:
        differ = center - shifted(padded, off_x, off_y, off_z, 1)
        total = total + 0.5 * jnp.sum(differ * pull(differ, off_x, off_y, off_z), axis=0)
    return total


def masks(labels):
    clamped = labels == 1
    roller = labels == 2
    first = jnp.where(clamped, 0.0, 1.0).astype(jnp.float32)
    last = jnp.where(clamped | roller, 0.0, 1.0).astype(jnp.float32)
    return jnp.stack([first, first, last])


def spread(table, padded, depth):
    total = jnp.zeros_like(shifted(padded, 0, 0, 0, depth))
    for off_x, off_y, off_z, weight in table:
        total = total + weight * shifted(padded, off_x, off_y, off_z, depth)
    return total


def inside_line(place, devices, count):
    start = place * count - RAD
    positions = start + jnp.arange(count + 2 * RAD, dtype=jnp.int32)
    limit = count * devices
    return ((positions >= 0) & (positions < limit)).astype(jnp.float32)


def per_device(solution, residual, direction, density, labels):
    stiffness = stiff_floor + (1.0 - stiff_floor) * density * density * density
    free_mask = masks(labels)
    masked = free_mask * direction
    stacked = jnp.concatenate([masked, stiffness[None], solution], axis=0)
    padded = with_halo(stacked, (("gx", 1), ("gy", 2), ("gz", 3)), 1)
    image_raw, diag_raw = couple(padded[0:3], padded[3])
    image = free_mask * image_raw
    precond = free_mask * diag_raw + (1.0 - free_mask)
    zeta = residual / precond
    norm_now, curvature = lax.psum(
        (jnp.sum(residual * zeta), jnp.sum(masked * image)), ("gx", "gy", "gz")
    )
    alpha = norm_now / curvature
    new_residual = residual - alpha * image
    new_zeta = new_residual / precond
    norm_next = lax.psum(jnp.sum(new_residual * new_zeta), ("gx", "gy", "gz"))
    new_solution = solution + alpha * masked
    new_direction = new_zeta + norm_next / norm_now * direction
    solution_pad = padded[4:7] + alpha * padded[0:3]
    compliance = -penalty * (1.0 - stiff_floor) * density * density * energy(solution_pad)
    table = filter_table(RAD)
    line_x = inside_line(lax.axis_index("gx"), lax.axis_size("gx"), density.shape[0])
    line_y = inside_line(lax.axis_index("gy"), lax.axis_size("gy"), density.shape[1])
    line_z = inside_line(lax.axis_index("gz"), lax.axis_size("gz"), density.shape[2])
    inside = line_x[:, None, None] * line_y[None, :, None] * line_z[None, None, :]
    hsum = spread(table, inside, RAD)
    scaled = compliance / hsum
    scaled_pad = with_halo(scaled, (("gx", 0), ("gy", 1), ("gz", 2)), RAD)
    sensitivity = spread(table, scaled_pad, RAD)
    return (new_solution, new_residual, new_direction, sensitivity)


def solution(mesh):
    return jax.shard_map(
        per_device,
        mesh=mesh,
        in_specs=(
            P(None, "gx", "gy", "gz"),
            P(None, "gx", "gy", "gz"),
            P(None, "gx", "gy", "gz"),
            P("gx", "gy", "gz"),
            P("gx", "gy", "gz"),
        ),
        out_specs=(
            P(None, "gx", "gy", "gz"),
            P(None, "gx", "gy", "gz"),
            P(None, "gx", "gy", "gz"),
            P("gx", "gy", "gz"),
        ),
        check_vma=False,
    )
```

profile of v0, /device:TPU:0, one launch (start us, length us, event | category | flops | bytes accessed | tf_op | source)
XLA Modules:
  0.0 168.9 jit_solution(1654854704304491295)
XLA Ops:
  0.6 0.9 select_bitcast_fusion.1
  1.5 0.9 fusion.148
  2.4 1.0 fusion.58
  3.4 0.8 pad_maximum_fusion.27
  4.1 2.4 %collective-permute-start = (f32[7,1,16,128]{3,2,1,0:T(8,128)S(1)}, f32[7,1,16,128]{3,2,1,0:T(8,128)S(1)}, u32[]{:S(2)}, u32[]{:S(2)}) collective-permute-start(f32[7,1,16,128]{3,2,1,0:T(8,128)S(1)} %get-tuple-element.179), channel_id=1, source_target_pairs={{0,8},{8,16},{16,24},{1,9},{9,17},{17,25},{2,10},{10,18},{18,26},{... | collective-permute-start | bytes 172040 | tf_op jit(solution)/shard_map/ppermute | solution.py:27
  6.5 1.3 collective-permute-start.1
  7.8 0.1 broadcast_multiply_fusion.17
  7.9 3.8 %collective-permute-done.1 = f32[7,1,16,128]{3,2,1,0:T(8,128)S(1)} collective-permute-done((f32[7,1,16,128]{3,2,1,0:T(8,128)S(1)}, f32[7,1,16,128]{3,2,1,0:T(8,128)S(1)}, u32[]{:S(2)}, u32[]{:S(2)}) %collective-permute-start.1) | collective-permute-done | bytes 57376 | tf_op jit(solution)/shard_map/ppermute | solution.py:30
  11.7 1.0 pad_maximum_fusion.32
  12.7 3.4 %collective-permute-start.2 = (f32[7,10,1,128]{3,2,1,0:T(1,128)S(1)}, f32[7,10,1,128]{3,2,1,0:T(1,128)S(1)}, u32[]{:S(2)}, u32[]{:S(2)}) collective-permute-start(f32[7,10,1,128]{3,2,1,0:T(1,128)S(1)} %get-tuple-element.175), channel_id=1, source_target_pairs={{0,4},{1,5},{2,6},{3,7},{8,12},{9,13},{10,14},{11,15},{16,20},{17,... | collective-permute-start | bytes 107528 | tf_op jit(solution)/shard_map/ppermute | solution.py:27
  16.2 1.3 collective-permute-start.3
  17.5 0.1 broadcast_multiply_fusion
  17.6 0.2 collective-permute-done.2
  17.8 4.2 %collective-permute-done.3 = f32[7,10,1,128]{3,2,1,0:T(1,128)S(1)} collective-permute-done((f32[7,10,1,128]{3,2,1,0:T(1,128)S(1)}, f32[7,10,1,128]{3,2,1,0:T(1,128)S(1)}, u32[]{:S(2)}, u32[]{:S(2)}) %collective-permute-start.3) | collective-permute-done | bytes 35872 | tf_op jit(solution)/shard_map/ppermute | solution.py:30
  22.0 0.1 pad_maximum_fusion.2
  22.1 0.3 fusion.448
  22.4 0.6 copy.59
  23.0 3.5 %collective-permute-start.4 = (f32[7,10,18,1]{2,0,3,1:T(8,128)S(1)}, f32[7,10,18,1]{2,0,3,1:T(8,128)S(1)}, u32[]{:S(2)}, u32[]{:S(2)}) collective-permute-start(f32[7,10,18,1]{2,0,3,1:T(8,128)S(1)} %copy.59), channel_id=1, source_target_pairs={{0,1},{1,2},{2,3},{4,5},{5,6},{6,7},{8,9},{9,10},{10,11},{12,13},{... | collective-permute-start | bytes 15128 | tf_op jit(solution)/shard_map/ppermute | solution.py:27
  26.5 0.6 copy.60
  27.1 1.3 collective-permute-start.5
  28.6 0.6 slice_add_fusion.53
  29.2 0.6 multiply_add_fusion.91
  29.9 0.6 multiply_add_fusion.138
  30.5 0.7 multiply_add_fusion.158
  31.2 0.7 multiply_add_fusion.108
  32.0 0.7 multiply_add_fusion.89
  32.7 0.5 copy.61
  33.2 0.5 copy.62
  33.8 1.0 pad_maximum_fusion
  34.9 0.2 broadcast_multiply_fusion.16
  35.0 0.2 broadcast_multiply_fusion.15
  35.2 0.2 broadcast_multiply_fusion.14
  35.4 0.7 copy-done.1
  36.1 0.2 broadcast_multiply_fusion.13
  36.3 2.1 %maximum_maximum_fusion = (f32[7,10,18,129]{3,2,1,0:T(8,128)S(1)}, f32[7,10,18,129]{3,2,1,0:T(8,128)S(1)}) fusion(f32[7,10,1,128]{3,2,1,0:T(1,128)S(1)} %collective-permute-done.3, f32[7,1,16,128]{3,2,1,0:T(8,128)S(1)} %collective-permute-done.1, f32[3,8,16,128]{3,2,1,0:T(8,128)S(1)} %copy-done, f32[1,8,16,128]{3,2,1,0:T(8,128)S(1)} %fusion.148, ...), kind=kLoop, calls=%fused_computation.1 | loop fusion | flops 2275560 | bytes 1955520 | tf_op jit(solution)/shard_map/concatenate | solution.py:31
  38.4 0.2 slice_subtract_fusion.43
  38.7 0.6 copy-done.3
  39.3 0.5 slice_subtract_fusion.42
  41.0 0.5 copy-done.4
  41.5 1.0 fusion.57
  42.7 1.6 multiply_reduce_fusion.1
  44.2 41.8 %all-reduce = (f32[]{:T(128)}, f32[]{:T(128)}) all-reduce(f32[]{:T(128)} %get-tuple-element.119, f32[]{:T(128)} %get-tuple-element.65), channel_id=1, replica_groups=mesh['gx'=4,'gy'=2,'gz'=4] {'gx','gy','gz'}, use_global_device_ids=true, to_apply=%region_1.2 | all-reduce | flops 2 | bytes 16 | tf_op jit(solution)/shard_map/psum | solution.py:135
  87.3 0.1 fusion
  87.4 0.4 slice_subtract_fusion.24
  87.9 0.4 slice_subtract_fusion.25
  88.3 0.4 slice_subtract_fusion.23
  91.0 0.6 copy-done.5
  91.6 3.0 %fusion.150 = f32[8,16,128]{2,1,0:T(8,128)S(1)} fusion(f32[8,16,128]{2,1,0:T(8,128)S(1)} %copy-done.5, f32[14,22,134]{2,1,0:T(8,128)S(1)} %broadcast_multiply_fusion, f32[8,16,128]{2,1,0:T(8,128)S(1)} %fusion.56, f32[8,16,128]{2,1,0:T(8,128)S(1)} %fusion.55, f32[8,16,128]{2,1,0:T(8,128)S(1)} %fusion.54, f32[8,16,128]{2,1,0:T(8,128)S(1)} %fusion.53, ...), kind=kLoop, calls=%fused_computation.296 | loop fusion | flops 6340608 | bytes 13565952 | tf_op jit(solution)/shard_map/div | solution.py:152
  94.7 1.3 collective-permute-start.6
  96.0 1.3 collective-permute-start.7
  97.3 1.3 multiply_reduce_fusion
  98.6 0.7 multiply_add_fusion.1
  99.3 44.8 %psum.23 = f32[]{:T(128)} all-reduce(f32[]{:T(128)} %get-tuple-element.62), channel_id=1, replica_groups=mesh['gx'=4,'gy'=2,'gz'=4] {'gx','gy','gz'}, use_global_device_ids=true, to_apply=%region_5.6 | all-reduce | flops 1 | bytes 8 | tf_op jit(solution)/shard_map/psum | solution.py:141
  145.5 4.4 %collective-permute-start.8 = (f32[14,3,128]{2,1,0:T(4,128)S(1)}, f32[14,3,128]{2,1,0:T(4,128)S(1)}, u32[]{:S(2)}, u32[]{:S(2)}) collective-permute-start(f32[14,3,128]{2,1,0:T(4,128)S(1)} %get-tuple-element.327), channel_id=1, source_target_pairs={{0,4},{1,5},{2,6},{3,7},{8,12},{9,13},{10,14},{11,15},{16,20},{17,... | collective-permute-start | bytes 64520 | tf_op jit(solution)/shard_map/ppermute | solution.py:27
  149.9 1.3 collective-permute-start.9
  151.2 0.7 multiply_add_fusion
  151.9 3.8 %collective-permute-done.9 = f32[14,3,128]{2,1,0:T(4,128)S(1)} collective-permute-done((f32[14,3,128]{2,1,0:T(4,128)S(1)}, f32[14,3,128]{2,1,0:T(4,128)S(1)}, u32[]{:S(2)}, u32[]{:S(2)}) %collective-permute-start.9) | collective-permute-done | bytes 21536 | tf_op jit(solution)/shard_map/ppermute | solution.py:30
  155.7 0.1 fusion.449
  155.8 2.5 %collective-permute-start.10 = (f32[14,22,3]{2,1,0:T(8,128)S(1)}, f32[14,22,3]{2,1,0:T(8,128)S(1)}, u32[]{:S(2)}, u32[]{:S(2)}) collective-permute-start(f32[14,22,3]{2,1,0:T(8,128)S(1)} %get-tuple-element.323), channel_id=1, source_target_pairs={{0,1},{1,2},{2,3},{4,5},{5,6},{6,7},{8,9},{9,10},{10,11},{12,13},{... | collective-permute-start | bytes 11096 | tf_op jit(solution)/shard_map/ppermute | solution.py:27
  158.3 1.3 collective-permute-start.11
  159.6 1.6 collective-permute-done.10
  161.2 4.4 %collective-permute-done.11 = f32[14,22,3]{2,1,0:T(8,128)S(1)} collective-permute-done((f32[14,22,3]{2,1,0:T(8,128)S(1)}, f32[14,22,3]{2,1,0:T(8,128)S(1)}, u32[]{:S(2)}, u32[]{:S(2)}) %collective-permute-start.11) | collective-permute-done | bytes 3728 | tf_op jit(solution)/shard_map/ppermute | solution.py:30
  165.6 0.2 maximum_maximum_fusion.1
  165.8 3.1 %fusion.151 = f32[8,16,128]{2,1,0:T(8,128)} fusion(f32[14,22,131]{2,1,0:T(8,128)S(1)} %get-tuple-element.322, f32[14,19,128]{2,1,0:T(8,128)S(1)} %get-tuple-element.326, f32[14,22,131]{2,1,0:T(8,128)S(1)} %get-tuple-element.321, f32[3,16,128]{2,1,0:T(8,128)S(1)} %collective-permute-done.7, f32[8,16,128]{2,1,0:T(8,128)S(1)} %fusion.150, ...), kind=kLoop, calls=%fused_computation.298 | loop fusion | flops 5947392 | bytes 11452416 | tf_op jit(solution)/shard_map/add | solution.py:114
  (177 shorter events, 3.0 us)
Async XLA Ops:
  0.6 21.4 %copy-start = (f32[3,8,16,128]{3,2,1,0:T(8,128)S(1)}, f32[3,8,16,128]{3,2,1,0:T(8,128)}, u32[]{:S(2)}) copy-start(f32[3,8,16,128]{3,2,1,0:T(8,128)} %param.31) | copy-start | bytes 589828
  4.1 3.8 %collective-permute-start = (f32[7,1,16,128]{3,2,1,0:T(8,128)S(1)}, f32[7,1,16,128]{3,2,1,0:T(8,128)S(1)}, u32[]{:S(2)}, u32[]{:S(2)}) collective-permute-start(f32[7,1,16,128]{3,2,1,0:T(8,128)S(1)} %get-tuple-element.179), channel_id=1, source_target_pairs={{0,8},{8,16},{16,24},{1,9},{9,17},{17,25},{2,10},{10,18},{18,26},{... | collective-permute-start | bytes 172040 | tf_op jit(solution)/shard_map/ppermute | solution.py:27
  6.5 5.2 %collective-permute-start.1 = (f32[7,1,16,128]{3,2,1,0:T(8,128)S(1)}, f32[7,1,16,128]{3,2,1,0:T(8,128)S(1)}, u32[]{:S(2)}, u32[]{:S(2)}) collective-permute-start(f32[7,1,16,128]{3,2,1,0:T(8,128)S(1)} %get-tuple-element.180), channel_id=1, source_target_pairs={{8,0},{16,8},{24,16},{9,1},{17,9},{25,17},{10,2},{18,10},{26,18},{... | collective-permute-start | bytes 172040 | tf_op jit(solution)/shard_map/ppermute | solution.py:30
  12.7 5.0 %collective-permute-start.2 = (f32[7,10,1,128]{3,2,1,0:T(1,128)S(1)}, f32[7,10,1,128]{3,2,1,0:T(1,128)S(1)}, u32[]{:S(2)}, u32[]{:S(2)}) collective-permute-start(f32[7,10,1,128]{3,2,1,0:T(1,128)S(1)} %get-tuple-element.175), channel_id=1, source_target_pairs={{0,4},{1,5},{2,6},{3,7},{8,12},{9,13},{10,14},{11,15},{16,20},{17,... | collective-permute-start | bytes 107528 | tf_op jit(solution)/shard_map/ppermute | solution.py:27
  16.2 5.8 %collective-permute-start.3 = (f32[7,10,1,128]{3,2,1,0:T(1,128)S(1)}, f32[7,10,1,128]{3,2,1,0:T(1,128)S(1)}, u32[]{:S(2)}, u32[]{:S(2)}) collective-permute-start(f32[7,10,1,128]{3,2,1,0:T(1,128)S(1)} %get-tuple-element.176), channel_id=1, source_target_pairs={{4,0},{5,1},{6,2},{7,3},{12,8},{13,9},{14,10},{15,11},{20,16},{21,... | collective-permute-start | bytes 107528 | tf_op jit(solution)/shard_map/ppermute | solution.py:30
  23.0 9.7 %collective-permute-start.4 = (f32[7,10,18,1]{2,0,3,1:T(8,128)S(1)}, f32[7,10,18,1]{2,0,3,1:T(8,128)S(1)}, u32[]{:S(2)}, u32[]{:S(2)}) collective-permute-start(f32[7,10,18,1]{2,0,3,1:T(8,128)S(1)} %copy.59), channel_id=1, source_target_pairs={{0,1},{1,2},{2,3},{4,5},{5,6},{6,7},{8,9},{9,10},{10,11},{12,13},{... | collective-permute-start | bytes 15128 | tf_op jit(solution)/shard_map/ppermute | solution.py:27
  27.1 6.1 %collective-permute-start.5 = (f32[7,10,18,1]{2,0,3,1:T(8,128)S(1)}, f32[7,10,18,1]{2,0,3,1:T(8,128)S(1)}, u32[]{:S(2)}, u32[]{:S(2)}) collective-permute-start(f32[7,10,18,1]{2,0,3,1:T(8,128)S(1)} %copy.60), channel_id=1, source_target_pairs={{1,0},{2,1},{3,2},{5,4},{6,5},{7,6},{9,8},{10,9},{11,10},{13,12},{... | collective-permute-start | bytes 15128 | tf_op jit(solution)/shard_map/ppermute | solution.py:30
  34.8 1.2 copy-start.1
  38.4 0.9 copy-start.3
  40.5 0.9 copy-start.4
  40.5 0.9 copy-start.21
  40.5 0.9 copy-start.22
  40.6 0.9 copy-start.23
  40.6 0.9 copy-start.24
  40.6 0.9 copy-start.25
  40.6 0.9 copy-start.26
  40.7 1.8 %copy-start.6 = (f32[1,8,16,128]{3,2,1,0:T(8,128)S(1)}, f32[1,8,16,128]{3,2,1,0:T(8,128)}, u32[]{:S(2)}) copy-start(f32[1,8,16,128]{3,2,1,0:T(8,128)} %get-tuple-element.87) | copy-start | bytes 196612
  40.7 1.8 %copy-start.7 = (f32[1,8,16,128]{3,2,1,0:T(8,128)S(1)}, f32[1,8,16,128]{3,2,1,0:T(8,128)}, u32[]{:S(2)}) copy-start(f32[1,8,16,128]{3,2,1,0:T(8,128)} %get-tuple-element.115) | copy-start | bytes 196612
  40.8 1.8 %copy-start.8 = (f32[1,8,16,128]{3,2,1,0:T(8,128)S(1)}, f32[1,8,16,128]{3,2,1,0:T(8,128)}, u32[]{:S(2)}) copy-start(f32[1,8,16,128]{3,2,1,0:T(8,128)} %get-tuple-element.81) | copy-start | bytes 196612
  40.8 1.8 %copy-start.9 = (f32[1,8,16,128]{3,2,1,0:T(8,128)S(1)}, f32[1,8,16,128]{3,2,1,0:T(8,128)}, u32[]{:S(2)}) copy-start(f32[1,8,16,128]{3,2,1,0:T(8,128)} %get-tuple-element.235) | copy-start | bytes 196612
  40.8 1.8 %copy-start.10 = (f32[1,8,16,128]{3,2,1,0:T(8,128)S(1)}, f32[1,8,16,128]{3,2,1,0:T(8,128)}, u32[]{:S(2)}) copy-start(f32[1,8,16,128]{3,2,1,0:T(8,128)} %get-tuple-element.236) | copy-start | bytes 196612
  40.8 1.8 %copy-start.11 = (f32[1,8,16,128]{3,2,1,0:T(8,128)S(1)}, f32[1,8,16,128]{3,2,1,0:T(8,128)}, u32[]{:S(2)}) copy-start(f32[1,8,16,128]{3,2,1,0:T(8,128)} %get-tuple-element.355) | copy-start | bytes 196612
  40.8 1.8 %copy-start.12 = (f32[1,8,16,128]{3,2,1,0:T(8,128)S(1)}, f32[1,8,16,128]{3,2,1,0:T(8,128)}, u32[]{:S(2)}) copy-start(f32[1,8,16,128]{3,2,1,0:T(8,128)} %get-tuple-element.356) | copy-start | bytes 196612
  40.8 1.8 %copy-start.13 = (f32[1,8,16,128]{3,2,1,0:T(8,128)S(1)}, f32[1,8,16,128]{3,2,1,0:T(8,128)}, u32[]{:S(2)}) copy-start(f32[1,8,16,128]{3,2,1,0:T(8,128)} %get-tuple-element.269) | copy-start | bytes 196612
  40.8 1.8 %copy-start.14 = (f32[1,8,16,128]{3,2,1,0:T(8,128)S(1)}, f32[1,8,16,128]{3,2,1,0:T(8,128)}, u32[]{:S(2)}) copy-start(f32[1,8,16,128]{3,2,1,0:T(8,128)} %get-tuple-element.270) | copy-start | bytes 196612
  40.8 1.8 %copy-start.15 = (f32[1,8,16,128]{3,2,1,0:T(8,128)S(1)}, f32[1,8,16,128]{3,2,1,0:T(8,128)}, u32[]{:S(2)}) copy-start(f32[1,8,16,128]{3,2,1,0:T(8,128)} %get-tuple-element.353) | copy-start | bytes 196612
  40.8 1.8 %copy-start.16 = (f32[1,8,16,128]{3,2,1,0:T(8,128)S(1)}, f32[1,8,16,128]{3,2,1,0:T(8,128)}, u32[]{:S(2)}) copy-start(f32[1,8,16,128]{3,2,1,0:T(8,128)} %get-tuple-element.354) | copy-start | bytes 196612
  40.8 1.8 %copy-start.17 = (f32[1,8,16,128]{3,2,1,0:T(8,128)S(1)}, f32[1,8,16,128]{3,2,1,0:T(8,128)}, u32[]{:S(2)}) copy-start(f32[1,8,16,128]{3,2,1,0:T(8,128)} %get-tuple-element.281) | copy-start | bytes 196612
  40.9 1.8 %copy-start.18 = (f32[1,8,16,128]{3,2,1,0:T(8,128)S(1)}, f32[1,8,16,128]{3,2,1,0:T(8,128)}, u32[]{:S(2)}) copy-start(f32[1,8,16,128]{3,2,1,0:T(8,128)} %get-tuple-element.282) | copy-start | bytes 196612
  40.9 1.8 %copy-start.19 = (f32[1,8,16,128]{3,2,1,0:T(8,128)S(1)}, f32[1,8,16,128]{3,2,1,0:T(8,128)}, u32[]{:S(2)}) copy-start(f32[1,8,16,128]{3,2,1,0:T(8,128)} %get-tuple-element.341) | copy-start | bytes 196612
  40.9 1.8 %copy-start.20 = (f32[1,8,16,128]{3,2,1,0:T(8,128)S(1)}, f32[1,8,16,128]{3,2,1,0:T(8,128)}, u32[]{:S(2)}) copy-start(f32[1,8,16,128]{3,2,1,0:T(8,128)} %get-tuple-element.342) | copy-start | bytes 196612
  42.6 44.7 %copy-start.2 = (f32[7,10,18,130]{3,2,1,0:T(8,128)S(1)}, f32[7,10,18,130]{3,2,1,0:T(8,128)}, u32[]{:S(2)}) copy-start(f32[7,10,18,130]{3,2,1,0:T(8,128)} %copy-done.1) | copy-start | bytes 1965604
  90.8 0.8 copy-start.5
  94.7 50.8 %collective-permute-start.6 = (f32[3,16,128]{2,1,0:T(8,128)S(1)}, f32[3,16,128]{2,1,0:T(8,128)S(1)}, u32[]{:S(2)}, u32[]{:S(2)}) collective-permute-start(f32[3,16,128]{2,1,0:T(8,128)S(1)} %get-tuple-element.329), channel_id=1, source_target_pairs={{0,8},{8,16},{16,24},{1,9},{9,17},{17,25},{2,10},{10,18},{18,26},{... | collective-permute-start | bytes 73736 | tf_op jit(solution)/shard_map/ppermute | solution.py:27
  96.0 49.5 %collective-permute-start.7 = (f32[3,16,128]{2,1,0:T(8,128)S(1)}, f32[3,16,128]{2,1,0:T(8,128)S(1)}, u32[]{:S(2)}, u32[]{:S(2)}) collective-permute-start(f32[3,16,128]{2,1,0:T(8,128)S(1)} %get-tuple-element.330), channel_id=1, source_target_pairs={{8,0},{16,8},{24,16},{9,1},{17,9},{25,17},{10,2},{18,10},{26,18},{... | collective-permute-start | bytes 73736 | tf_op jit(solution)/shard_map/ppermute | solution.py:30
  145.5 6.4 %collective-permute-start.8 = (f32[14,3,128]{2,1,0:T(4,128)S(1)}, f32[14,3,128]{2,1,0:T(4,128)S(1)}, u32[]{:S(2)}, u32[]{:S(2)}) collective-permute-start(f32[14,3,128]{2,1,0:T(4,128)S(1)} %get-tuple-element.327), channel_id=1, source_target_pairs={{0,4},{1,5},{2,6},{3,7},{8,12},{9,13},{10,14},{11,15},{16,20},{17,... | collective-permute-start | bytes 64520 | tf_op jit(solution)/shard_map/ppermute | solution.py:27
  149.9 5.8 %collective-permute-start.9 = (f32[14,3,128]{2,1,0:T(4,128)S(1)}, f32[14,3,128]{2,1,0:T(4,128)S(1)}, u32[]{:S(2)}, u32[]{:S(2)}) collective-permute-start(f32[14,3,128]{2,1,0:T(4,128)S(1)} %get-tuple-element.328), channel_id=1, source_target_pairs={{4,0},{5,1},{6,2},{7,3},{12,8},{13,9},{14,10},{15,11},{20,16},{21,... | collective-permute-start | bytes 64520 | tf_op jit(solution)/shard_map/ppermute | solution.py:30
  155.8 5.4 %collective-permute-start.10 = (f32[14,22,3]{2,1,0:T(8,128)S(1)}, f32[14,22,3]{2,1,0:T(8,128)S(1)}, u32[]{:S(2)}, u32[]{:S(2)}) collective-permute-start(f32[14,22,3]{2,1,0:T(8,128)S(1)} %get-tuple-element.323), channel_id=1, source_target_pairs={{0,1},{1,2},{2,3},{4,5},{5,6},{6,7},{8,9},{9,10},{10,11},{12,13},{... | collective-permute-start | bytes 11096 | tf_op jit(solution)/shard_map/ppermute | solution.py:27
  158.3 7.3 %collective-permute-start.11 = (f32[14,22,3]{2,1,0:T(8,128)S(1)}, f32[14,22,3]{2,1,0:T(8,128)S(1)}, u32[]{:S(2)}, u32[]{:S(2)}) collective-permute-start(f32[14,22,3]{2,1,0:T(8,128)S(1)} %get-tuple-element.324), channel_id=1, source_target_pairs={{1,0},{2,1},{3,2},{5,4},{6,5},{7,6},{9,8},{10,9},{11,10},{13,12},{... | collective-permute-start | bytes 11096 | tf_op jit(solution)/shard_map/ppermute | solution.py:30
where the time goes:
time: 170 us; the launch traced here: 169 us
  blocking collectives  86.6 us (51%)
  other arithmetic  29.3 us (17%)
  starting transfers between devices  25.1 us (15%)
  waiting for transfers between devices  18 us (11%)
  local copies, waits for them, and re-layouts  5.12 us (3%)
  between operations  4.73 us (3%)
    psum x1, blocking collectives, per_device(): norm_next = lax.psum(jnp.sum(new_residual * new_zeta), ('gx', 'gy', 'gz'))  44.8 us
    psum x1, blocking collectives, per_device(): lax.psum((jnp.sum(residual * zeta), jnp.sum(masked * image)), ('gx', 'gy'...  41.8 us
    ppermute x6, starting transfers between devices, with_halo(): lax.ppermute(lax.slice_in_dim(block, block.shape[dim] - width, None, axis...  17.4 us
    ppermute x6, waiting for transfers between devices, with_halo(): lax.ppermute(lax.slice_in_dim(block, 0, width, axis=dim), axis, backward)  16.2 us
    ppermute x6, starting transfers between devices, with_halo(): lax.ppermute(lax.slice_in_dim(block, 0, width, axis=dim), axis, backward)  7.74 us
    concatenate x6, other arithmetic, with_halo(): block = jnp.concatenate([low, block, high], axis=dim)  3.58 us
  transfers between devices with their start and end apart: 12, of which 6 were waited for; matrix products, arithmetic and copies ran while one was open for 5% of the time, Pallas kernels for 0%

commit v1 on v0

v1 whole, which is shorter than its diff:
```python
import functools
import math

import jax
import jax.numpy as jnp
from jax import lax
from jax.experimental import pallas as pl
from jax.experimental.pallas import tpu as pltpu
from jax.sharding import PartitionSpec as P

RAD = 3
HALO = RAD + 1
stiff_floor = 0.001
penalty = 3.0
f32 = jnp.float32
neighbour_offsets = [
    (off_x, off_y, off_z)
    for off_x in (-1, 0, 1)
    for off_y in (-1, 0, 1)
    for off_z in (-1, 0, 1)
    if (off_x, off_y, off_z) != (0, 0, 0)
]
AXES = ("gx", "gy", "gz")


def cone(a, b, k):
    return max(0.0, RAD + 0.5 - math.sqrt(a * a + b * b + k * k))


def lanes_of(shape):
    return lax.broadcasted_iota(jnp.int32, shape, len(shape) - 1)


def rows_of(shape):
    return lax.broadcasted_iota(jnp.int32, shape, len(shape) - 2)


def roll(value, amount, axis):
    size = value.shape[axis]
    amount = amount % size
    return value if amount == 0 else pltpu.roll(value, amount, axis)


def call(body, outs, *args, scratch=(), cost=20000):
    return pl.pallas_call(
        body,
        out_shape=[jax.ShapeDtypeStruct(shape, f32) for shape in outs],
        in_specs=[pl.BlockSpec(memory_space=pltpu.VMEM)] * len(args),
        out_specs=[pl.BlockSpec(memory_space=pltpu.VMEM)] * len(outs),
        scratch_shapes=list(scratch),
        compiler_params=pltpu.CompilerParams(vmem_limit_bytes=24 * 1024 * 1024),
        cost_estimate=pl.CostEstimate(flops=cost * 1000, bytes_accessed=cost, transcendentals=0),
    )(*args)


def pack_faces(two, sol, dire, den, lab, lo, hi, *sides):
    sub = rows_of((8, 128))
    first = (lax.axis_index("gy") == 0) if two else None
    for t in range(4):
        planes = []
        for x in (2 * t, 2 * t + 1):
            label = lab[x]
            keep = jnp.where(label == 1, 0.0, 1.0).astype(f32)
            keep_last = jnp.where(label >= 1, 0.0, 1.0).astype(f32)
            fields = [dire[0, x] * keep, dire[1, x] * keep, dire[2, x] * keep_last]
            fields += [sol[0, x], sol[1, x], sol[2, x], den[x]]
            target, at = (lo, x) if x < 4 else (hi, x - 4)
            for f in range(7):
                target[f, at] = fields[f]
            planes.append(fields)
        for f in range(7):
            p, q = planes[0][f], planes[1][f]
            low = jnp.where(sub < 4, p[0:8], roll(q[0:8], 4, 0))
            high = jnp.where(sub < 4, roll(p[8:16], 4, 0), q[8:16])
            tiles = [jnp.where(first, high, low)] if two else [low, high]
            for s, tile in enumerate(tiles):
                sides[3 * s][f, t] = tile
                sides[3 * s + 1 + t // 2][f, t % 2] = tile


def extend(two, lo, hi, xl, xh, y0, c0l, c0h, y1, c1l, c1h, ext, ends):
    sub = rows_of((8, 128))
    lane = lanes_of((24, 128))
    if two:
        gy = lax.axis_index("gy")
        has_low = (gy == 1).astype(f32)
        has_high = (gy == 0).astype(f32)
    for f in range(7):
        packed = None
        for X in range(16):
            src = (xl, lo, hi, xh)[X // 4]
            own = src[f, X % 4]
            a, b = roll(own[0:8], 4, 0), roll(own[8:16], 4, 0)
            if X < 4:
                low, high = c0l[f, X // 2], c1l[f, X // 2]
            elif X < 12:
                low, high = y0[f, (X - 4) // 2], y1[f, (X - 4) // 2]
            else:
                low, high = c0h[f, (X - 12) // 2], c1h[f, (X - 12) // 2]
            if two:
                low, high = low * has_low, high * has_high
            if X % 2 == 0:
                high = roll(high, 4, 0)
            else:
                low = roll(low, 4, 0)
            plane = jnp.concatenate(
                [jnp.where(sub < 4, low, a), jnp.where(sub < 4, a, b), jnp.where(sub < 4, b, high)],
                axis=0,
            )
            ext[f, X] = plane
            turned = roll(plane, 8 * X + 4, 1)
            packed = turned if X == 0 else jnp.where(lane >= 8 * X, turned, packed)
        ends[f] = packed


def inverse_sums(counts, main, side):
    shape = (24, 128)
    row, lane = rows_of(shape), lanes_of(shape)
    nx, ny, nz = counts
    base_x = lax.axis_index("gx") * 8 - HALO
    base_y = lax.axis_index("gy") * 16 - HALO
    base_z = lax.axis_index("gz") * 128

    def folded(place, limit):
        def inside(p):
            return jnp.where((p >= 0) & (p < limit), 1.0, 0.0).astype(f32)

        return [inside(place)] + [inside(place - k) + inside(place + k) for k in range(1, RAD + 1)]

    along_y = folded(row + base_y, ny * 16)

    def partial(along_z):
        table = []
        for a in range(RAD + 1):
            total = jnp.zeros(shape, f32)
            for b in range(RAD + 1):
                line = None
                for k in range(RAD + 1):
                    w = cone(a, b, k)
                    if w > 0:
                        line = w * along_z[k] if line is None else line + w * along_z[k]
                if line is not None:
                    total = total + along_y[b] * line
            table.append(total)
        return table

    def finish(total, along_x, along_z):
        inner = along_x[0] * along_y[0] * along_z[0] > 0
        return jnp.where(inner, 1.0 / jnp.where(inner, total, 1.0), 0.0)

    along_z = folded(lane + base_z, nz * 128)
    table = partial(along_z)
    for X in range(16):
        along_x = folded(jnp.full(shape, X, jnp.int32) + base_x, nx * 8)
        total = sum(along_x[a] * table[a] for a in range(RAD + 1))
        main[X] = finish(total, along_x, along_z)
    place = lane % 8
    along_x = folded(lane // 8 + base_x, nx * 8)
    for s, shift in enumerate((-4, 124)):
        along_z = folded(place + (base_z + shift), nz * 128)
        table = partial(along_z)
        total = sum(along_x[a] * table[a] for a in range(RAD + 1))
        side[s] = finish(total, along_x, along_z)


def apply_operator(ext, ends, from_low, from_high, res, lab, image, inverse, sums, shifts):
    lane = lanes_of((24, 128))
    lane2 = lanes_of((16, 128))
    fields = (0, 1, 2, 6)
    del lane2
    for g, f in enumerate(fields):
        halo = jnp.where(lane % 8 < 4, from_low[f], from_high[f])
        for n in range(10):
            X = n + 3
            value = ext[f, X]
            near = roll(halo, 124 - 8 * X, 1)
            if g == 3:
                value = stiff_floor + (1.0 - stiff_floor) * value * value * value
                value = jnp.where(ext[f, X] > 0, value, 0.0)
                near_stiff = stiff_floor + (1.0 - stiff_floor) * near * near * near
                near = jnp.where(near > 0, near_stiff, 0.0)
            up = roll(jnp.where(lane == 0, near, value), -1, 1)
            down = roll(jnp.where(lane == 127, near, value), 1, 1)
            for z, plane in enumerate((down, value, up)):
                for y in range(3):
                    shifts[g, y, z, n] = roll(plane, -(HALO - 1 + y), 0)[0:16]
    parts = [jnp.zeros((16, 128), f32) for _ in range(4)]
    for x in range(8):
        n = x + 1
        mid = [shifts[g, 1, 1, n] for g in range(4)]
        classes = {1: [None] * 3, 2: [None] * 3, 3: [None] * 3}
        faces = [None] * 3
        edges = [None] * 3
        corners = None

        def add(old, new):
            return new if old is None else old + new

        for o in neighbour_offsets:
            near = [shifts[g, 1 + o[1], 1 + o[2], n + o[0]] for g in range(4)]
            norm = sum(abs(c) for c in o)
            weight = mid[3] + near[3]
            d = [mid[c] - near[c] for c in range(3)]
            acc = classes[norm]
            if norm == 1:
                c0 = [c for c in range(3) if o[c] != 0][0]
                faces[c0] = add(faces[c0], near[3])
                for c in range(3):
                    acc[c] = add(acc[c], weight * (d[c] + d[c] if c == c0 else d[c]))
            else:
                along = None
                for c in range(3):
                    if o[c] != 0:
                        term = d[c]
                        if along is None:
                            along, sign = term, o[c]
                        else:
                            along = along + term if o[c] == sign else along - term
                along = along * (1.0 / norm)
                for c in range(3):
                    if o[c] == 0:
                        pulled = d[c]
                    elif o[c] == sign:
                        pulled = d[c] + along
                    else:
                        pulled = d[c] - along
                    acc[c] = add(acc[c], weight * pulled)
                if norm == 2:
                    c0 = [c for c in range(3) if o[c] == 0][0]
                    edges[c0] = add(edges[c0], near[3])
                else:
                    corners = add(corners, near[3])
        s0 = mid[3]
        all_faces = faces[0] + faces[1] + faces[2]
        all_edges = edges[0] + edges[1] + edges[2]
        common = (all_faces + 6.0 * s0) + 0.75 * (all_edges + 12.0 * s0) + (4.0 / 9.0) * (corners + 8.0 * s0)
        label = lab[x]
        for c in range(3):
            diag = 0.5 * (common + (faces[c] + 2.0 * s0) - 0.25 * (edges[c] + 4.0 * s0))
            fixed = (label == 1) if c < 2 else (label >= 1)
            total = 0.5 * classes[1][c] + 0.25 * classes[2][c] + (1.0 / 6.0) * classes[3][c]
            total = jnp.where(fixed, 0.0, total)
            inv = 1.0 / jnp.where(fixed, 1.0, diag)
            r = res[c, x]
            zeta = r * inv
            scaled = total * inv
            image[c, x] = total
            inverse[c, x] = inv
            parts[0] = parts[0] + r * zeta
            parts[1] = parts[1] + mid[c] * total
            parts[2] = parts[2] + r * scaled
            parts[3] = parts[3] + total * scaled
    sub = rows_of((8, 128))
    out = jnp.zeros((8, 128), f32)
    for k in range(4):
        part = parts[k][0:8] + parts[k][8:16]
        out = jnp.where(sub == k, jnp.sum(part, axis=0, keepdims=True), out)
    sums[...] = out


def quadratic(d, o):
    norm = sum(abs(c) for c in o)
    square = d[0] * d[0] + d[1] * d[1] + d[2] * d[2]
    along, sign = None, 1
    for c in range(3):
        if o[c] != 0:
            if along is None:
                along, sign = d[c], o[c]
            else:
                along = along + d[c] if o[c] == sign else along - d[c]
    return (0.5 / norm) * square + (0.5 / (norm * norm)) * (along * along)


flat_half = [(1, -1, 0), (1, 0, 0), (1, 1, 0), (0, 1, 0)]
up_half = [(a, b, 1) for a in (-1, 0, 1) for b in (-1, 0, 1)]


def finish_step(
    ext, ends, from_low, from_high, total, image, inverse, res, dire, hinv, hside,
    new_sol, new_res, new_dir, sens, us, scaled,
):
    lane = lanes_of((24, 128))
    lows = lane % 8 < 4
    tot = jnp.sum(total[...], axis=1, keepdims=True)
    rz, pq, s2, s3 = tot[0:1], tot[1:2], tot[2:3], tot[3:4]
    alpha = rz / pq
    beta = (rz + alpha * (alpha * s3 - 2.0 * s2)) / rz

    for x in range(8):
        for c in range(3):
            r = res[c, x] - alpha * image[c, x]
            new_res[c, x] = r
            new_dir[c, x] = r * inverse[c, x] + beta * dire[c, x]

    halos = []
    lefts, rights = [], []
    for c in range(3):
        low_u = from_low[3 + c] + alpha * from_low[c]
        high_u = from_high[3 + c] + alpha * from_high[c]
        own_u = ends[3 + c] + alpha * ends[c]
        halos.append(jnp.where(lows, low_u, high_u))
        lefts.append(jnp.where(lows, low_u, own_u))
        rights.append(jnp.where(lows, own_u, high_u))
    for X in range(16):
        for c in range(3):
            u = ext[3 + c, X] + alpha * ext[c, X]
            if 4 <= X < 12:
                new_sol[c, X - 4] = roll(u, -HALO, 0)[0:16]
            near = roll(halos[c], 124 - 8 * X, 1)
            up = roll(jnp.where(lane == 0, near, u), -1, 1)
            for z, plane in enumerate((u, up)):
                us[3 * z, c, X] = roll(plane, 1, 0)
                us[3 * z + 1, c, X] = plane
                us[3 * z + 2, c, X] = roll(plane, -1, 0)

    sides, side_low = [], None
    den_left = jnp.where(lows, from_low[6], ends[6])
    den_right = jnp.where(lows, ends[6], from_high[6])
    for s, (u, den) in enumerate(((lefts, den_left), (rights, den_right))):
        turned = {oy: [roll(v, -oy, 0) for v in u] for oy in (-1, 0, 1)}
        forward = jnp.zeros((24, 128), f32)
        back = {(oy, oz): jnp.zeros((24, 128), f32) for oy in (-1, 0, 1) for oz in (0, 1)}
        for o in flat_half + up_half:
            move = 8 * o[0] + o[2]
            g = quadratic([u[c] - roll(turned[o[1]][c], -move, 1) for c in range(3)], o)
            forward = forward + g
            back[o[1], o[2]] = back[o[1], o[2]] + roll(g, 8 * o[0], 1)
        flat = back[0, 0] + roll(back[1, 0], 1, 0) + roll(back[-1, 0], -1, 0)
        up = back[0, 1] + roll(back[1, 1], 1, 0) + roll(back[-1, 1], -1, 0)
        if s == 0:
            side_low = up
        energy = forward + flat + roll(up, 1, 1)
        sides.append((-penalty * (1.0 - stiff_floor)) * (den * den) * energy * hside[s])
    ends_scaled = jnp.where(lows, sides[0], sides[1])

    zero = jnp.zeros((24, 128), f32)
    forward = [zero] * 16
    back = [{(oy, oz): None for oy in (-1, 0, 1) for oz in (0, 1)} for _ in range(16)]
    for X in range(0, 16):
        mine = [us[1, c, X] for c in range(3)]
        for o in flat_half + up_half:
            to = X + o[0]
            if not 0 <= to < 16:
                continue
            k = 3 * o[2] + o[1] + 1
            g = quadratic([mine[c] - us[k, c, to] for c in range(3)], o)
            forward[X] = forward[X] + g
            old = back[to][o[1], o[2]]
            back[to][o[1], o[2]] = g if old is None else old + g
        done = X - 1
        if done >= 1:
            bk = back[done]
            flat = bk[0, 0] + roll(bk[1, 0], 1, 0) + roll(bk[-1, 0], -1, 0)
            up = bk[0, 1] + roll(bk[1, 1], 1, 0) + roll(bk[-1, 1], -1, 0)
            below = roll(side_low, 127 - (8 * done + 3), 1)
            up = roll(jnp.where(lane == 127, below, up), 1, 1)
            den = ext[6, done]
            energy = forward[done] + flat + up
            scaled[done] = (-penalty * (1.0 - stiff_floor)) * (den * den) * energy * hinv[done]

    rows = [[None] * (RAD + 1) for _ in range(8)]
    for X in range(1, 15):
        s = scaled[X]
        near = roll(ends_scaled, 124 - 8 * X, 1)
        fold = [s]
        for k in range(1, RAD + 1):
            above = roll(jnp.where(lane < k, near, s), -k, 1)
            under = roll(jnp.where(lane >= 128 - k, near, s), k, 1)
            fold.append(above + under)
        made = {}
        for b in range(RAD + 1):
            for a in range(-RAD, RAD + 1):
                x = X - a - HALO
                if not 0 <= x < 8 or cone(a, b, 0) <= 0:
                    continue
                key = a * a + b * b
                if key not in made:
                    line = None
                    for k in range(RAD + 1):
                        w = cone(a, b, k)
                        if w > 0:
                            line = w * fold[k] if line is None else line + w * fold[k]
                    made[key] = line
                old = rows[x][b]
                rows[x][b] = made[key] if old is None else old + made[key]
        x = X - 2 * RAD - 1
        if x >= 0:
            value = rows[x][0]
            for b in range(1, RAD + 1):
                value = value + roll(rows[x][b], b, 0) + roll(rows[x][b], -b, 0)
            sens[x] = roll(value, -HALO, 0)[0:16]


def line_pairs(count, step):
    return [(i, i + step) for i in range(count) if 0 <= i + step < count]


def plane_pairs(nx, ny, step_x, step_y):
    pairs = []
    for ix in range(nx):
        for iy in range(ny):
            to_x, to_y = ix + step_x, (1 - iy if step_y is None else iy + step_y)
            if 0 <= to_x < nx and 0 <= to_y < ny:
                pairs.append((ix * ny + iy, to_x * ny + to_y))
    return pairs


def prime_factors(count):
    factors, p = [], 2
    while count > 1:
        while count % p == 0:
            factors.append(p)
            count //= p
        p += 1
    return factors


def total_over(value, mesh_shape):
    for axis in AXES:
        count = mesh_shape[axis]
        stride = 1
        for factor in prime_factors(count):
            block = stride * factor
            got = []
            for step in range(1, factor):
                pairs = []
                for i in range(count):
                    digit = (i // stride) % factor
                    to = i + (((digit + step) % factor) - digit) * stride
                    pairs.append((i, to))
                got.append(lax.ppermute(value, axis, pairs))
            for other in got:
                value = value + other
            stride = block
    return value


def per_device(mesh_shape, solution, residual, direction, density, labels):
    nx, ny, nz = (mesh_shape[a] for a in AXES)
    two = ny == 2
    half, full, corner = (7, 4, 16, 128), (7, 4, 8, 128), (7, 2, 8, 128)
    n_sides = 1 if two else 2
    packed = call(
        functools.partial(pack_faces, two),
        [half, half] + [full, corner, corner] * n_sides,
        solution, direction, density, labels,
    )
    lo, hi = packed[:2]
    plane = ("gx", "gy")
    xl = lax.ppermute(hi, "gx", line_pairs(nx, 1))
    xh = lax.ppermute(lo, "gx", line_pairs(nx, -1))
    received = []
    for s in range(n_sides):
        rows, first, second = packed[2 + 3 * s : 5 + 3 * s]
        step = None if two else (-1, 1)[s]
        received.append(
            [
                lax.ppermute(rows, plane, plane_pairs(nx, ny, 0, step)),
                lax.ppermute(second, plane, plane_pairs(nx, ny, 1, step)),
                lax.ppermute(first, plane, plane_pairs(nx, ny, -1, step)),
            ]
        )
    low_side, high_side = (received[0], received[0]) if two else (received[1], received[0])
    hinv, hside = call(functools.partial(inverse_sums, (nx, ny, nz)), [(16, 24, 128), (2, 24, 128)])
    ext, ends = call(
        functools.partial(extend, two),
        [(7, 16, 24, 128), (7, 24, 128)],
        lo, hi, xl, xh, *low_side, *high_side,
    )
    from_low = lax.ppermute(ends, "gz", line_pairs(nz, 1))
    from_high = lax.ppermute(ends, "gz", line_pairs(nz, -1))
    field = (3, 8, 16, 128)
    image, inverse, sums = call(
        apply_operator,
        [field, field, (8, 128)],
        ext, ends, from_low, from_high, residual, labels,
        scratch=[pltpu.VMEM((4, 3, 3, 10, 16, 128), f32)],
    )
    total = total_over(sums, mesh_shape)
    return tuple(
        call(
            finish_step,
            [field, field, field, (8, 16, 128)],
            ext, ends, from_low, from_high, total, image, inverse, residual, direction, hinv, hside,
            scratch=[pltpu.VMEM((6, 3, 16, 24, 128), f32), pltpu.VMEM((16, 24, 128), f32)],
        )
    )


def solution(mesh):
    wide, flat = P(None, "gx", "gy", "gz"), P("gx", "gy", "gz")
    return jax.shard_map(
        functools.partial(per_device, dict(mesh.shape)),
        mesh=mesh,
        in_specs=(wide, wide, wide, flat, flat),
        out_specs=(wide, wide, wide, flat),
        check_vma=False,
    )
```

time: 170 us -> 55.6 us (0.33)
  blocking collectives: 86.6 us -> 0 us
  other arithmetic: 29.3 us -> 0.02 us
  Pallas kernels: 0 us -> 9.58 us
  between operations: 4.73 us -> 0.73 us
  waiting for transfers between devices: 18 us -> 15.5 us
    psum x2 -> x0, blocking collectives: 86.6 us -> none  [the longest x1 44.8 us: per_device(): norm_next = lax.psum(jnp.sum(new_residual * new_zeta), ('gx', 'gy', 'gz'))]
    add x95 -> x5, other arithmetic: 10.6 us -> 0.02 us  [total_over(): value = value + other]
    pallas_call x0 -> x5, Pallas kernels: none -> 9.58 us  [call(): pl.pallas_call(body, out_shape=[jax.ShapeDtypeStruct(shape, f32) for shap...]
    reduce_sum x29 -> x0, other arithmetic: 4.7 us -> none  [the longest x1 1.55 us: per_device(): jnp.sum(masked * image)]
    concatenate x6 -> x0, other arithmetic: 3.58 us -> none  [with_halo(): block = jnp.concatenate([low, block, high], axis=dim)]
    div x1 -> x0, other arithmetic: 3.05 us -> none  [per_device(): scaled = compliance / hsum]
    ppermute x12, waiting for transfers between devices: 18 us -> 15.5 us  [the longest x5 8.61 us: total_over(): got.append(lax.ppermute(value, axis, pairs))]
    sub x7 -> x0, other arithmetic: 2.07 us -> none  [the longest x3 1.23 us: energy(): differ = center - shifted(padded, off_x, off_y, off_z, 1)]
  transfers between devices with their start and end apart: 12 -> 12, of which waited for: 6 -> 9; matrix products, arithmetic and copies ran while one was open for 5% -> 0% of each run, Pallas kernels for 0% -> 0%
where the time goes in v1:
time: 55.6 us; the launch traced here: 55.2 us
  starting transfers between devices  25.8 us (46%)
  waiting for transfers between devices  15.5 us (28%)
  Pallas kernels  9.58 us (17%)
  local copies, waits for them, and re-layouts  3.54 us (6%)
  between operations  0.73 us (1%)
    pallas_call x5, Pallas kernels, call(): pl.pallas_call(body, out_shape=[jax.ShapeDtypeStruct(shape, f32) for shap...  9.58 us
    ppermute x5, waiting for transfers between devices, total_over(): got.append(lax.ppermute(value, axis, pairs))  8.61 us
    ppermute x5, starting transfers between devices, total_over(): got.append(lax.ppermute(value, axis, pairs))  8.25 us
    ppermute x1, starting transfers between devices, per_device(): from_low = lax.ppermute(ends, 'gz', line_pairs(nz, 1))  4.55 us
    ppermute x1, waiting for transfers between devices, per_device(): lax.ppermute(first, plane, plane_pairs(nx, ny, -1, step))  3.84 us
    unnamed x14, local copies, waits for them, and re-layouts  3.54 us
    ppermute x1, starting transfers between devices, per_device(): xl = lax.ppermute(hi, 'gx', line_pairs(nx, 1))  3.04 us
    ppermute x1, starting transfers between devices, per_device(): lax.ppermute(rows, plane, plane_pairs(nx, ny, 0, step))  3.03 us
  transfers between devices with their start and end apart: 12, of which 9 were waited for; matrix products, arithmetic and copies ran while one was open for 0% of the time, Pallas kernels for 0%

profile of v1, /device:TPU:0, one launch (start us, length us, event | category | flops | bytes accessed | tf_op | source)
XLA Modules:
  0.0 55.2 jit_solution(17633821636608414733)
XLA Ops:
  0.6 0.0 copy-start
  0.6 0.9 %copy-done = f32[3,8,16,128]{3,2,1,0:T(8,128)S(1)} copy-done((f32[3,8,16,128]{3,2,1,0:T(8,128)S(1)}, f32[3,8,16,128]{3,2,1,0:T(8,128)}, u32[]{:S(2)}) %copy-start) | copy-done | bytes 196632
  1.6 0.0 copy-start.3
  1.6 0.8 %copy-done.3 = s32[8,16,128]{2,1,0:T(8,128)S(1)} copy-done((s32[8,16,128]{2,1,0:T(8,128)S(1)}, s32[8,16,128]{2,1,0:T(8,128)}, u32[]{:S(2)}) %copy-start.3) | copy-done | bytes 65560
  2.4 0.0 copy-start.5
  2.4 0.9 %copy-done.5 = f32[3,8,16,128]{3,2,1,0:T(8,128)S(1)} copy-done((f32[3,8,16,128]{3,2,1,0:T(8,128)S(1)}, f32[3,8,16,128]{3,2,1,0:T(8,128)}, u32[]{:S(2)}) %copy-start.5) | copy-done | bytes 196632
  3.3 0.0 copy-start.6
  3.3 0.8 %copy-done.6 = f32[8,16,128]{2,1,0:T(8,128)S(1)} copy-done((f32[8,16,128]{2,1,0:T(8,128)S(1)}, f32[8,16,128]{2,1,0:T(8,128)}, u32[]{:S(2)}) %copy-start.6) | copy-done | bytes 65560
  4.2 0.0 copy-start.2
  4.2 0.0 copy-start.4
  4.2 1.4 %collective-permute-start.1 = (f32[7,4,16,128]{3,2,1,0:T(8,128)S(1)}, f32[7,4,16,128]{3,2,1,0:T(8,128)S(1)}, u32[]{:S(2)}, u32[]{:S(2)}) collective-permute-start(f32[7,4,16,128]{3,2,1,0:T(8,128)S(1)} %get-tuple-element.16.lo), channel_id=1, source_target_pairs={{8,0},{16,8},{24,16},{9,1},{17,9},{25,17},{10,2},{18,10},{26,18},{... | collective-permute-start | bytes 688136 | tf_op jit(solution)/shard_map/ppermute | solution.py:451
  5.7 3.0 %collective-permute-start = (f32[7,4,16,128]{3,2,1,0:T(8,128)S(1)}, f32[7,4,16,128]{3,2,1,0:T(8,128)S(1)}, u32[]{:S(2)}, u32[]{:S(2)}) collective-permute-start(f32[7,4,16,128]{3,2,1,0:T(8,128)S(1)} %get-tuple-element.17.hi), channel_id=1, source_target_pairs={{0,8},{8,16},{16,24},{1,9},{9,17},{17,25},{2,10},{10,18},{18,26},{... | collective-permute-start | bytes 688136 | tf_op jit(solution)/shard_map/ppermute | solution.py:450
  8.7 3.0 %collective-permute-start.2 = (f32[7,4,8,128]{3,2,1,0:T(8,128)S(1)}, f32[7,4,8,128]{3,2,1,0:T(8,128)S(1)}, u32[]{:S(2)}, u32[]{:S(2)}) collective-permute-start(f32[7,4,8,128]{3,2,1,0:T(8,128)S(1)} %get-tuple-element.18), channel_id=1, source_target_pairs={{0,4},{4,0},{8,12},{12,8},{16,20},{20,16},{24,28},{28,24},{1,5},{5... | collective-permute-start | bytes 344072 | tf_op jit(solution)/shard_map/ppermute | solution.py:458
  11.7 2.8 %collective-permute-start.3 = (f32[7,2,8,128]{3,2,1,0:T(8,128)S(1)}, f32[7,2,8,128]{3,2,1,0:T(8,128)S(1)}, u32[]{:S(2)}, u32[]{:S(2)}) collective-permute-start(f32[7,2,8,128]{3,2,1,0:T(8,128)S(1)} %get-tuple-element.19), channel_id=1, source_target_pairs={{0,12},{4,8},{8,20},{12,16},{16,28},{20,24},{1,13},{5,9},{9,21},{1... | collective-permute-start | bytes 172040 | tf_op jit(solution)/shard_map/ppermute | solution.py:459
  14.6 0.0 copy-start.1
  14.6 1.4 %collective-permute-start.4 = (f32[7,2,8,128]{3,2,1,0:T(8,128)S(1)}, f32[7,2,8,128]{3,2,1,0:T(8,128)S(1)}, u32[]{:S(2)}, u32[]{:S(2)}) collective-permute-start(f32[7,2,8,128]{3,2,1,0:T(8,128)S(1)} %get-tuple-element.20), channel_id=1, source_target_pairs={{8,4},{12,0},{16,12},{20,8},{24,20},{28,16},{9,5},{13,1},{17,13},{... | collective-permute-start | bytes 172040 | tf_op jit(solution)/shard_map/ppermute | solution.py:460
  16.0 0.4 collective-permute-done.3.c0l.c1l
  16.4 3.8 %collective-permute-done.4.c0h.c1h = f32[7,2,8,128]{3,2,1,0:T(8,128)S(1)} collective-permute-done((f32[7,2,8,128]{3,2,1,0:T(8,128)S(1)}, f32[7,2,8,128]{3,2,1,0:T(8,128)S(1)}, u32[]{:S(2)}, u32[]{:S(2)}) %collective-permute-start.4) | collective-permute-done | bytes 57376 | tf_op jit(solution)/shard_map/ppermute | solution.py:460
  20.2 0.0 collective-permute-done.2.y0.y1
  20.2 0.0 collective-permute-done.1.xh
  20.2 0.0 collective-permute-done.xl
  20.2 0.4 shard_map.85
  20.7 1.3 %collective-permute-start.6 = (f32[7,24,128]{2,1,0:T(8,128)S(1)}, f32[7,24,128]{2,1,0:T(8,128)S(1)}, u32[]{:S(2)}, u32[]{:S(2)}) collective-permute-start(f32[7,24,128]{2,1,0:T(8,128)S(1)} %get-tuple-element.22.ends), channel_id=1, source_target_pairs={{1,0},{2,1},{3,2},{5,4},{6,5},{7,6},{9,8},{10,9},{11,10},{13,12},{... | collective-permute-start | bytes 258056 | tf_op jit(solution)/shard_map/ppermute | solution.py:471
  22.0 4.6 %collective-permute-start.5 = (f32[7,24,128]{2,1,0:T(8,128)S(1)}, f32[7,24,128]{2,1,0:T(8,128)S(1)}, u32[]{:S(2)}, u32[]{:S(2)}) collective-permute-start(f32[7,24,128]{2,1,0:T(8,128)S(1)} %get-tuple-element.22.ends), channel_id=1, source_target_pairs={{0,1},{1,2},{2,3},{4,5},{5,6},{6,7},{8,9},{9,10},{10,11},{12,13},{... | collective-permute-start | bytes 258056 | tf_op jit(solution)/shard_map/ppermute | solution.py:470
  26.5 1.0 %collective-permute-done.6.from_high = f32[7,24,128]{2,1,0:T(8,128)S(1)} collective-permute-done((f32[7,24,128]{2,1,0:T(8,128)S(1)}, f32[7,24,128]{2,1,0:T(8,128)S(1)}, u32[]{:S(2)}, u32[]{:S(2)}) %collective-permute-start.6) | collective-permute-done | bytes 86048 | tf_op jit(solution)/shard_map/ppermute | solution.py:471
  27.5 1.7 %collective-permute-done.5.from_low = f32[7,24,128]{2,1,0:T(8,128)S(1)} collective-permute-done((f32[7,24,128]{2,1,0:T(8,128)S(1)}, f32[7,24,128]{2,1,0:T(8,128)S(1)}, u32[]{:S(2)}, u32[]{:S(2)}) %collective-permute-start.5) | collective-permute-done | bytes 86048 | tf_op jit(solution)/shard_map/ppermute | solution.py:470
  29.2 0.0 copy-done.2
  29.2 0.0 copy-done.4
  29.2 2.6 %shard_map.86 = (f32[3,8,16,128]{3,2,1,0:T(8,128)S(1)}, f32[3,8,16,128]{3,2,1,0:T(8,128)S(1)}, f32[8,128]{1,0:T(8,128)S(1)}) custom-call(f32[7,16,24,128]{3,2,1,0:T(8,128)S(1)} %get-tuple-element.21.ext, f32[7,24,128]{2,1,0:T(8,128)S(1)} %get-tuple-element.22.ends, f32[7,24,128]{2,1,0:T(8,128)S(1)} %collective-permute-done.5.from_low, ...), custom_call_target="tpu_custom_call" | custom-call | flops 20000000 | bytes 20000 | tf_op jit(solution)/shard_map/pallas_call | solution.py:45
  31.8 0.4 collective-permute-start.7
  32.2 0.8 %collective-permute-done.7 = f32[8,128]{1,0:T(8,128)S(1)} collective-permute-done((f32[8,128]{1,0:T(8,128)S(1)}, f32[8,128]{1,0:T(8,128)S(1)}, u32[]{:S(2)}, u32[]{:S(2)}) %collective-permute-start.7) | collective-permute-done | bytes 4128 | tf_op jit(solution)/shard_map/ppermute | solution.py:431
  33.0 0.8 %collective-permute-start.8 = (f32[8,128]{1,0:T(8,128)S(1)}, f32[8,128]{1,0:T(8,128)S(1)}, u32[]{:S(2)}, u32[]{:S(2)}) collective-permute-start(f32[8,128]{1,0:T(8,128)S(1)} %add.15), channel_id=1, source_target_pairs={{0,16},{8,24},{16,0},{24,8},{1,17},{9,25},{17,1},{25,9},{2,18},{10... | collective-permute-start | bytes 12296 | tf_op jit(solution)/shard_map/ppermute | solution.py:431
  33.8 2.8 %collective-permute-done.8 = f32[8,128]{1,0:T(8,128)S(1)} collective-permute-done((f32[8,128]{1,0:T(8,128)S(1)}, f32[8,128]{1,0:T(8,128)S(1)}, u32[]{:S(2)}, u32[]{:S(2)}) %collective-permute-start.8) | collective-permute-done | bytes 4128 | tf_op jit(solution)/shard_map/ppermute | solution.py:431
  36.6 1.5 %collective-permute-start.9 = (f32[8,128]{1,0:T(8,128)S(1)}, f32[8,128]{1,0:T(8,128)S(1)}, u32[]{:S(2)}, u32[]{:S(2)}) collective-permute-start(f32[8,128]{1,0:T(8,128)S(1)} %add.16), channel_id=1, source_target_pairs={{0,4},{4,0},{1,5},{5,1},{2,6},{6,2},{3,7},{7,3},{8,12},{12,8},{9,1... | collective-permute-start | bytes 12296 | tf_op jit(solution)/shard_map/ppermute | solution.py:431
  38.1 2.1 %collective-permute-done.9 = f32[8,128]{1,0:T(8,128)S(1)} collective-permute-done((f32[8,128]{1,0:T(8,128)S(1)}, f32[8,128]{1,0:T(8,128)S(1)}, u32[]{:S(2)}, u32[]{:S(2)}) %collective-permute-start.9) | collective-permute-done | bytes 4128 | tf_op jit(solution)/shard_map/ppermute | solution.py:431
  40.2 2.4 %collective-permute-start.10 = (f32[8,128]{1,0:T(8,128)S(1)}, f32[8,128]{1,0:T(8,128)S(1)}, u32[]{:S(2)}, u32[]{:S(2)}) collective-permute-start(f32[8,128]{1,0:T(8,128)S(1)} %add.17), channel_id=1, source_target_pairs={{0,1},{1,0},{2,3},{3,2},{4,5},{5,4},{6,7},{7,6},{8,9},{9,8},{10,11... | collective-permute-start | bytes 12296 | tf_op jit(solution)/shard_map/ppermute | solution.py:431
  42.7 1.6 %collective-permute-done.10 = f32[8,128]{1,0:T(8,128)S(1)} collective-permute-done((f32[8,128]{1,0:T(8,128)S(1)}, f32[8,128]{1,0:T(8,128)S(1)}, u32[]{:S(2)}, u32[]{:S(2)}) %collective-permute-start.10) | collective-permute-done | bytes 4128 | tf_op jit(solution)/shard_map/ppermute | solution.py:431
  44.3 3.0 %collective-permute-start.11 = (f32[8,128]{1,0:T(8,128)S(1)}, f32[8,128]{1,0:T(8,128)S(1)}, u32[]{:S(2)}, u32[]{:S(2)}) collective-permute-start(f32[8,128]{1,0:T(8,128)S(1)} %add.18), channel_id=1, source_target_pairs={{0,2},{1,3},{2,0},{3,1},{4,6},{5,7},{6,4},{7,5},{8,10},{9,11},{10,... | collective-permute-start | bytes 12296 | tf_op jit(solution)/shard_map/ppermute | solution.py:431
  47.3 0.3 shard_map.87
  47.6 1.3 %collective-permute-done.11 = f32[8,128]{1,0:T(8,128)S(1)} collective-permute-done((f32[8,128]{1,0:T(8,128)S(1)}, f32[8,128]{1,0:T(8,128)S(1)}, u32[]{:S(2)}, u32[]{:S(2)}) %collective-permute-start.11) | collective-permute-done | bytes 4128 | tf_op jit(solution)/shard_map/ppermute | solution.py:431
  48.9 0.0 copy-done.1
  48.9 6.3 %shard_map.88 = (f32[3,8,16,128]{3,2,1,0:T(8,128)}, f32[3,8,16,128]{3,2,1,0:T(8,128)}, f32[3,8,16,128]{3,2,1,0:T(8,128)}, f32[8,16,128]{2,1,0:T(8,128)}) custom-call(f32[7,16,24,128]{3,2,1,0:T(8,128)S(1)} %get-tuple-element.21.ext, f32[7,24,128]{2,1,0:T(8,128)S(1)} %get-tuple-element.22.ends, f32[7,24,128]{2,1,0:T(8,128)S(1)} %collective-permute-done.5.from_low, ...), custom_call_target="tpu_custom_call" | custom-call | flops 20000000 | bytes 20000 | tf_op jit(solution)/shard_map/pallas_call | solution.py:45
  (6 shorter events, 0.1 us)
Async XLA Ops:
  0.6 0.9 %copy-start = (f32[3,8,16,128]{3,2,1,0:T(8,128)S(1)}, f32[3,8,16,128]{3,2,1,0:T(8,128)}, u32[]{:S(2)}) copy-start(f32[3,8,16,128]{3,2,1,0:T(8,128)} %dire.3) | copy-start | bytes 589828
  1.6 0.8 %copy-start.3 = (s32[8,16,128]{2,1,0:T(8,128)S(1)}, s32[8,16,128]{2,1,0:T(8,128)}, u32[]{:S(2)}) copy-start(s32[8,16,128]{2,1,0:T(8,128)} %lab.3) | copy-start | bytes 196612
  2.4 0.9 %copy-start.5 = (f32[3,8,16,128]{3,2,1,0:T(8,128)S(1)}, f32[3,8,16,128]{3,2,1,0:T(8,128)}, u32[]{:S(2)}) copy-start(f32[3,8,16,128]{3,2,1,0:T(8,128)} %sol.1) | copy-start | bytes 589828
  3.3 0.8 %copy-start.6 = (f32[8,16,128]{2,1,0:T(8,128)S(1)}, f32[8,16,128]{2,1,0:T(8,128)}, u32[]{:S(2)}) copy-start(f32[8,16,128]{2,1,0:T(8,128)} %den.1) | copy-start | bytes 196612
  4.2 25.0 %copy-start.2 = (f32[3,8,16,128]{3,2,1,0:T(8,128)S(1)}, f32[3,8,16,128]{3,2,1,0:T(8,128)}, u32[]{:S(2)}) copy-start(f32[3,8,16,128]{3,2,1,0:T(8,128)} %res.3) | copy-start | bytes 589828
  4.2 25.0 %copy-start.4 = (s32[8,16,128]{2,1,0:T(8,128)S(1)}, s32[8,16,128]{2,1,0:T(8,128)}, u32[]{:S(2)}) copy-start(s32[8,16,128]{2,1,0:T(8,128)} %lab.3) | copy-start | bytes 196612
  4.2 16.0 %collective-permute-start.1 = (f32[7,4,16,128]{3,2,1,0:T(8,128)S(1)}, f32[7,4,16,128]{3,2,1,0:T(8,128)S(1)}, u32[]{:S(2)}, u32[]{:S(2)}) collective-permute-start(f32[7,4,16,128]{3,2,1,0:T(8,128)S(1)} %get-tuple-element.16.lo), channel_id=1, source_target_pairs={{8,0},{16,8},{24,16},{9,1},{17,9},{25,17},{10,2},{18,10},{26,18},{... | collective-permute-start | bytes 688136 | tf_op jit(solution)/shard_map/ppermute | solution.py:451
  5.7 14.6 %collective-permute-start = (f32[7,4,16,128]{3,2,1,0:T(8,128)S(1)}, f32[7,4,16,128]{3,2,1,0:T(8,128)S(1)}, u32[]{:S(2)}, u32[]{:S(2)}) collective-permute-start(f32[7,4,16,128]{3,2,1,0:T(8,128)S(1)} %get-tuple-element.17.hi), channel_id=1, source_target_pairs={{0,8},{8,16},{16,24},{1,9},{9,17},{17,25},{2,10},{10,18},{18,26},{... | collective-permute-start | bytes 688136 | tf_op jit(solution)/shard_map/ppermute | solution.py:450
  8.7 11.5 %collective-permute-start.2 = (f32[7,4,8,128]{3,2,1,0:T(8,128)S(1)}, f32[7,4,8,128]{3,2,1,0:T(8,128)S(1)}, u32[]{:S(2)}, u32[]{:S(2)}) collective-permute-start(f32[7,4,8,128]{3,2,1,0:T(8,128)S(1)} %get-tuple-element.18), channel_id=1, source_target_pairs={{0,4},{4,0},{8,12},{12,8},{16,20},{20,16},{24,28},{28,24},{1,5},{5... | collective-permute-start | bytes 344072 | tf_op jit(solution)/shard_map/ppermute | solution.py:458
  11.7 4.6 %collective-permute-start.3 = (f32[7,2,8,128]{3,2,1,0:T(8,128)S(1)}, f32[7,2,8,128]{3,2,1,0:T(8,128)S(1)}, u32[]{:S(2)}, u32[]{:S(2)}) collective-permute-start(f32[7,2,8,128]{3,2,1,0:T(8,128)S(1)} %get-tuple-element.19), channel_id=1, source_target_pairs={{0,12},{4,8},{8,20},{12,16},{16,28},{20,24},{1,13},{5,9},{9,21},{1... | collective-permute-start | bytes 172040 | tf_op jit(solution)/shard_map/ppermute | solution.py:459
  14.6 34.3 %copy-start.1 = (f32[3,8,16,128]{3,2,1,0:T(8,128)S(1)}, f32[3,8,16,128]{3,2,1,0:T(8,128)}, u32[]{:S(2)}) copy-start(f32[3,8,16,128]{3,2,1,0:T(8,128)} %dire.3) | copy-start | bytes 589828
  14.6 5.6 %collective-permute-start.4 = (f32[7,2,8,128]{3,2,1,0:T(8,128)S(1)}, f32[7,2,8,128]{3,2,1,0:T(8,128)S(1)}, u32[]{:S(2)}, u32[]{:S(2)}) collective-permute-start(f32[7,2,8,128]{3,2,1,0:T(8,128)S(1)} %get-tuple-element.20), channel_id=1, source_target_pairs={{8,4},{12,0},{16,12},{20,8},{24,20},{28,16},{9,5},{13,1},{17,13},{... | collective-permute-start | bytes 172040 | tf_op jit(solution)/shard_map/ppermute | solution.py:460
  20.7 6.8 %collective-permute-start.6 = (f32[7,24,128]{2,1,0:T(8,128)S(1)}, f32[7,24,128]{2,1,0:T(8,128)S(1)}, u32[]{:S(2)}, u32[]{:S(2)}) collective-permute-start(f32[7,24,128]{2,1,0:T(8,128)S(1)} %get-tuple-element.22.ends), channel_id=1, source_target_pairs={{1,0},{2,1},{3,2},{5,4},{6,5},{7,6},{9,8},{10,9},{11,10},{13,12},{... | collective-permute-start | bytes 258056 | tf_op jit(solution)/shard_map/ppermute | solution.py:471
  22.0 7.2 %collective-permute-start.5 = (f32[7,24,128]{2,1,0:T(8,128)S(1)}, f32[7,24,128]{2,1,0:T(8,128)S(1)}, u32[]{:S(2)}, u32[]{:S(2)}) collective-permute-start(f32[7,24,128]{2,1,0:T(8,128)S(1)} %get-tuple-element.22.ends), channel_id=1, source_target_pairs={{0,1},{1,2},{2,3},{4,5},{5,6},{6,7},{8,9},{9,10},{10,11},{12,13},{... | collective-permute-start | bytes 258056 | tf_op jit(solution)/shard_map/ppermute | solution.py:470
  31.8 1.3 %collective-permute-start.7 = (f32[8,128]{1,0:T(8,128)S(1)}, f32[8,128]{1,0:T(8,128)S(1)}, u32[]{:S(2)}, u32[]{:S(2)}) collective-permute-start(f32[8,128]{1,0:T(8,128)S(1)} %get-tuple-element.23), channel_id=1, source_target_pairs={{0,8},{8,0},{16,24},{24,16},{1,9},{9,1},{17,25},{25,17},{2,10},{10... | collective-permute-start | bytes 12296 | tf_op jit(solution)/shard_map/ppermute | solution.py:431
  33.0 3.6 %collective-permute-start.8 = (f32[8,128]{1,0:T(8,128)S(1)}, f32[8,128]{1,0:T(8,128)S(1)}, u32[]{:S(2)}, u32[]{:S(2)}) collective-permute-start(f32[8,128]{1,0:T(8,128)S(1)} %add.15), channel_id=1, source_target_pairs={{0,16},{8,24},{16,0},{24,8},{1,17},{9,25},{17,1},{25,9},{2,18},{10... | collective-permute-start | bytes 12296 | tf_op jit(solution)/shard_map/ppermute | solution.py:431
  36.6 3.6 %collective-permute-start.9 = (f32[8,128]{1,0:T(8,128)S(1)}, f32[8,128]{1,0:T(8,128)S(1)}, u32[]{:S(2)}, u32[]{:S(2)}) collective-permute-start(f32[8,128]{1,0:T(8,128)S(1)} %add.16), channel_id=1, source_target_pairs={{0,4},{4,0},{1,5},{5,1},{2,6},{6,2},{3,7},{7,3},{8,12},{12,8},{9,1... | collective-permute-start | bytes 12296 | tf_op jit(solution)/shard_map/ppermute | solution.py:431
  40.2 4.0 %collective-permute-start.10 = (f32[8,128]{1,0:T(8,128)S(1)}, f32[8,128]{1,0:T(8,128)S(1)}, u32[]{:S(2)}, u32[]{:S(2)}) collective-permute-start(f32[8,128]{1,0:T(8,128)S(1)} %add.17), channel_id=1, source_target_pairs={{0,1},{1,0},{2,3},{3,2},{4,5},{5,4},{6,7},{7,6},{8,9},{9,8},{10,11... | collective-permute-start | bytes 12296 | tf_op jit(solution)/shard_map/ppermute | solution.py:431
  44.3 4.6 %collective-permute-start.11 = (f32[8,128]{1,0:T(8,128)S(1)}, f32[8,128]{1,0:T(8,128)S(1)}, u32[]{:S(2)}, u32[]{:S(2)}) collective-permute-start(f32[8,128]{1,0:T(8,128)S(1)} %add.18), channel_id=1, source_target_pairs={{0,2},{1,3},{2,0},{3,1},{4,6},{5,7},{6,4},{7,5},{8,10},{9,11},{10,... | collective-permute-start | bytes 12296 | tf_op jit(solution)/shard_map/ppermute | solution.py:431

commit v2 on v1

--- a/solution.py
+++ b/solution.py
@@ -41,11 +41,16 @@
     return value if amount == 0 else pltpu.roll(value, amount, axis)
 
 
-def call(body, outs, *args, scratch=(), cost=20000):
+def call(body, outs, *args, scratch=(), cost=20000, far=()):
+    args = [
+        pltpu.with_memory_space_constraint(a, pltpu.HBM) if i in far else a for i, a in enumerate(args)
+    ]
     return pl.pallas_call(
         body,
         out_shape=[jax.ShapeDtypeStruct(shape, f32) for shape in outs],
-        in_specs=[pl.BlockSpec(memory_space=pltpu.VMEM)] * len(args),
+        in_specs=[
+            pl.BlockSpec(memory_space=pl.ANY if i in far else pltpu.VMEM) for i in range(len(args))
+        ],
         out_specs=[pl.BlockSpec(memory_space=pltpu.VMEM)] * len(outs),
         scratch_shapes=list(scratch),
         compiler_params=pltpu.CompilerParams(vmem_limit_bytes=24 * 1024 * 1024),
@@ -53,64 +58,113 @@
     )(*args)
 
 
-def pack_faces(two, sol, dire, den, lab, lo, hi, *sides):
+def is_even(axis):
+    return lax.axis_index(axis) % 2 == 0
+
+
+def pack_faces(rounds_y, sol_any, dire_any, den_any, lab_any, *refs):
+    halves, packs = refs[:2], refs[2 : 2 + 3 * rounds_y]
+    sol, dire, den, lab, sems = refs[2 + 3 * rounds_y :]
+    copies = [
+        pltpu.make_async_copy(source, target, sems.at[i])
+        for i, (source, target) in enumerate(
+            ((dire_any, dire), (sol_any, sol), (den_any, den), (lab_any, lab))
+        )
+    ]
+    for copy in copies:
+        copy.start()
     sub = rows_of((8, 128))
-    first = (lax.axis_index("gy") == 0) if two else None
-    for t in range(4):
-        planes = []
-        for x in (2 * t, 2 * t + 1):
-            label = lab[x]
-            keep = jnp.where(label == 1, 0.0, 1.0).astype(f32)
-            keep_last = jnp.where(label >= 1, 0.0, 1.0).astype(f32)
-            fields = [dire[0, x] * keep, dire[1, x] * keep, dire[2, x] * keep_last]
-            fields += [sol[0, x], sol[1, x], sol[2, x], den[x]]
-            target, at = (lo, x) if x < 4 else (hi, x - 4)
-            for f in range(7):
-                target[f, at] = fields[f]
-            planes.append(fields)
+    even_x, even_y = is_even("gx"), is_even("gy")
+    for copy in copies:
+        copy.wait()
+
+    def masked(x):
+        label = lab[x]
+        keep = jnp.where(label == 1, 0.0, 1.0).astype(f32)
+        keep_last = jnp.where(label >= 1, 0.0, 1.0).astype(f32)
+        fields = [dire[0, x] * keep, dire[1, x] * keep, dire[2, x] * keep_last]
+        return fields + [sol[0, x], sol[1, x], sol[2, x], den[x]]
+
+    for t in range(2):
+        planes = {x: masked(x) for x in (2 * t, 2 * t + 1, 2 * t + 4, 2 * t + 5)}
         for f in range(7):
-            p, q = planes[0][f], planes[1][f]
-            low = jnp.where(sub < 4, p[0:8], roll(q[0:8], 4, 0))
-            high = jnp.where(sub < 4, roll(p[8:16], 4, 0), q[8:16])
-            tiles = [jnp.where(first, high, low)] if two else [low, high]
-            for s, tile in enumerate(tiles):
-                sides[3 * s][f, t] = tile
-                sides[3 * s + 1 + t // 2][f, t % 2] = tile
-
-
-def extend(two, lo, hi, xl, xh, y0, c0l, c0h, y1, c1l, c1h, ext, ends):
+            for i in (2 * t, 2 * t + 1):
+                low, high = planes[i][f], planes[i + 4][f]
+                halves[0][f, i] = jnp.where(even_x, high, low)
+                halves[1][f, i] = jnp.where(even_x, low, high)
+            tiles = []
+            for i in (2 * t, 2 * t + 4):
+                p, q = planes[i][f], planes[i + 1][f]
+                low = jnp.where(sub < 4, p[0:8], roll(q[0:8], 4, 0))
+                high = jnp.where(sub < 4, roll(p[8:16], 4, 0), q[8:16])
+                tiles.append((jnp.where(even_y, high, low), jnp.where(even_y, low, high)))
+            for s in range(rounds_y):
+                rows, corner0, corner1 = packs[3 * s : 3 * s + 3]
+                low, high = tiles[0][s], tiles[1][s]
+                rows[f, t] = low
+                rows[f, t + 2] = high
+                corner0[f, t] = jnp.where(even_x, high, low)
+                corner1[f, t] = jnp.where(even_x, low, high)
+
+
+def extend(counts, half0, half1, got0, got1, *refs):
+    nx, ny, nz = counts
+    sides, (ext, ends) = refs[:-2], refs[-2:]
     sub = rows_of((8, 128))
     lane = lanes_of((24, 128))
-    if two:
-        gy = lax.axis_index("gy")
-        has_low = (gy == 1).astype(f32)
-        has_high = (gy == 0).astype(f32)
-    for f in range(7):
-        packed = None
-        for X in range(16):
-            src = (xl, lo, hi, xh)[X // 4]
-            own = src[f, X % 4]
-            a, b = roll(own[0:8], 4, 0), roll(own[8:16], 4, 0)
-            if X < 4:
-                low, high = c0l[f, X // 2], c1l[f, X // 2]
-            elif X < 12:
-                low, high = y0[f, (X - 4) // 2], y1[f, (X - 4) // 2]
-            else:
-                low, high = c0h[f, (X - 12) // 2], c1h[f, (X - 12) // 2]
-            if two:
-                low, high = low * has_low, high * has_high
-            if X % 2 == 0:
-                high = roll(high, 4, 0)
-            else:
-                low = roll(low, 4, 0)
-            plane = jnp.concatenate(
-                [jnp.where(sub < 4, low, a), jnp.where(sub < 4, a, b), jnp.where(sub < 4, b, high)],
-                axis=0,
-            )
-            ext[f, X] = plane
-            turned = roll(plane, 8 * X + 4, 1)
-            packed = turned if X == 0 else jnp.where(lane >= 8 * X, turned, packed)
-        ends[f] = packed
+    ix, iy = lax.axis_index("gx"), lax.axis_index("gy")
+    even_y = is_even("gy")
+    x_ok = ((ix > 0).astype(f32), (ix < nx - 1).astype(f32))
+    y_ok = ((iy > 0).astype(f32), (iy < ny - 1).astype(f32))
+
+    def body(blocks, order):
+        def strip(which, f, t):
+            tiles = []
+            for s in range(len(sides) // 3):
+                rows, corner0, corner1 = sides[3 * s : 3 * s + 3]
+                ref = rows if which is None else (corner0, corner1)[order[which]]
+                tiles.append(ref[f, t])
+            keep = 1.0 if which is None else x_ok[which]
+            other = tiles[-1]
+            low = jnp.where(even_y, other, tiles[0]) * (y_ok[0] * keep)
+            high = jnp.where(even_y, tiles[0], other) * (y_ok[1] * keep)
+            return low, high
+
+        for f in range(7):
+            packed = None
+            for X in range(16):
+                own = blocks[X // 4][f, X % 4]
+                which = None
+                if X < 4:
+                    which, t = 0, X // 2
+                elif X >= 12:
+                    which, t = 1, (X - 12) // 2
+                else:
+                    t = (X - 4) // 2
+                if which is not None:
+                    own = own * x_ok[which]
+                low, high = strip(which, f, t)
+                a, b = roll(own[0:8], 4, 0), roll(own[8:16], 4, 0)
+                if X % 2 == 0:
+                    high = roll(high, 4, 0)
+                else:
+                    low = roll(low, 4, 0)
+                plane = jnp.concatenate(
+                    [jnp.where(sub < 4, low, a), jnp.where(sub < 4, a, b), jnp.where(sub < 4, b, high)],
+                    axis=0,
+                )
+                ext[f, X] = plane
+                turned = roll(plane, 8 * X + 4, 1)
+                packed = turned if X == 0 else jnp.where(lane >= 8 * X, turned, packed)
+            ends[f] = packed
+
+    @pl.when(ix % 2 == 0)
+    def _():
+        body((got1, half1, half0, got0), (1, 0))
+
+    @pl.when(ix % 2 == 1)
+    def _():
+        body((got0, half0, half1, got1), (0, 1))
 
 
 def inverse_sums(counts, main, side):
@@ -163,13 +217,17 @@
         side[s] = finish(total, along_x, along_z)
 
 
-def apply_operator(ext, ends, from_low, from_high, res, lab, image, inverse, sums, shifts):
+def apply_operator(nz, ext, got0, got1, res, lab, image, inverse, sums, around, shifts):
     lane = lanes_of((24, 128))
-    lane2 = lanes_of((16, 128))
     fields = (0, 1, 2, 6)
-    del lane2
+    iz = lax.axis_index("gz")
+    lows = lane % 8 < 4
+    from_zero = (lane // 4) % 2 == (iz + 1) % 2
+    keep = jnp.where(lows, (iz > 0).astype(f32), (iz < nz - 1).astype(f32))
+    for f in range(7):
+        around[f] = jnp.where(from_zero, got0[f], got1[f]) * keep
     for g, f in enumerate(fields):
-        halo = jnp.where(lane % 8 < 4, from_low[f], from_high[f])
+        halo = around[f]
         for n in range(10):
             X = n + 3
             value = ext[f, X]
@@ -276,7 +334,7 @@
 
 
 def finish_step(
-    ext, ends, from_low, from_high, total, image, inverse, res, dire, hinv, hside,
+    ext, ends, around, total, image, inverse, res, dire, hinv, hside,
     new_sol, new_res, new_dir, sens, us, scaled,
 ):
     lane = lanes_of((24, 128))
@@ -295,12 +353,11 @@
     halos = []
     lefts, rights = [], []
     for c in range(3):
-        low_u = from_low[3 + c] + alpha * from_low[c]
-        high_u = from_high[3 + c] + alpha * from_high[c]
+        halo_u = around[3 + c] + alpha * around[c]
         own_u = ends[3 + c] + alpha * ends[c]
-        halos.append(jnp.where(lows, low_u, high_u))
-        lefts.append(jnp.where(lows, low_u, own_u))
-        rights.append(jnp.where(lows, own_u, high_u))
+        halos.append(halo_u)
+        lefts.append(jnp.where(lows, halo_u, own_u))
+        rights.append(jnp.where(lows, own_u, halo_u))
     for X in range(16):
         for c in range(3):
             u = ext[3 + c, X] + alpha * ext[c, X]
@@ -314,8 +371,8 @@
                 us[3 * z + 2, c, X] = roll(plane, -1, 0)
 
     sides, side_low = [], None
-    den_left = jnp.where(lows, from_low[6], ends[6])
-    den_right = jnp.where(lows, ends[6], from_high[6])
+    den_left = jnp.where(lows, around[6], ends[6])
+    den_right = jnp.where(lows, ends[6], around[6])
     for s, (u, den) in enumerate(((lefts, den_left), (rights, den_right))):
         turned = {oy: [roll(v, -oy, 0) for v in u] for oy in (-1, 0, 1)}
         forward = jnp.zeros((24, 128), f32)
@@ -391,17 +448,25 @@
             sens[x] = roll(value, -HALO, 0)[0:16]
 
 
-def line_pairs(count, step):
-    return [(i, i + step) for i in range(count) if 0 <= i + step < count]
-
-
-def plane_pairs(nx, ny, step_x, step_y):
+def partner(place, turn, count):
+    other = (place ^ 1) if turn == 0 else ((place + 1) ^ 1) - 1
+    return other if 0 <= other < count else None
+
+
+def swap_pairs(counts, turns):
     pairs = []
-    for ix in range(nx):
-        for iy in range(ny):
-            to_x, to_y = ix + step_x, (1 - iy if step_y is None else iy + step_y)
-            if 0 <= to_x < nx and 0 <= to_y < ny:
-                pairs.append((ix * ny + iy, to_x * ny + to_y))
+    for flat in range(math.prod(counts)):
+        rest, place = flat, []
+        for count in reversed(counts):
+            place.insert(0, rest % count)
+            rest //= count
+        to = [p if t is None else partner(p, t, c) for p, t, c in zip(place, turns, counts)]
+        if None in to:
+            to = place
+        index = 0
+        for p, count in zip(to, counts):
+            index = index * count + p
+        pairs.append((flat, index))
     return pairs
 
 
@@ -437,51 +502,45 @@
 
 def per_device(mesh_shape, solution, residual, direction, density, labels):
     nx, ny, nz = (mesh_shape[a] for a in AXES)
-    two = ny == 2
     half, full, corner = (7, 4, 16, 128), (7, 4, 8, 128), (7, 2, 8, 128)
-    n_sides = 1 if two else 2
+    rounds_y = 1 if ny == 2 else 2
+    field, flat = (3, 8, 16, 128), (8, 16, 128)
     packed = call(
-        functools.partial(pack_faces, two),
-        [half, half] + [full, corner, corner] * n_sides,
+        functools.partial(pack_faces, rounds_y),
+        [half, half] + [full, corner, corner] * rounds_y,
         solution, direction, density, labels,
+        far=range(4),
+        scratch=[
+            pltpu.VMEM(field, f32), pltpu.VMEM(field, f32), pltpu.VMEM(flat, f32),
+            pltpu.VMEM(flat, jnp.int32), pltpu.SemaphoreType.DMA((4,)),
+        ],
     )
-    lo, hi = packed[:2]
+    halves = packed[:2]
     plane = ("gx", "gy")
-    xl = lax.ppermute(hi, "gx", line_pairs(nx, 1))
-    xh = lax.ppermute(lo, "gx", line_pairs(nx, -1))
-    received = []
-    for s in range(n_sides):
-        rows, first, second = packed[2 + 3 * s : 5 + 3 * s]
-        step = None if two else (-1, 1)[s]
-        received.append(
-            [
-                lax.ppermute(rows, plane, plane_pairs(nx, ny, 0, step)),
-                lax.ppermute(second, plane, plane_pairs(nx, ny, 1, step)),
-                lax.ppermute(first, plane, plane_pairs(nx, ny, -1, step)),
-            ]
-        )
-    low_side, high_side = (received[0], received[0]) if two else (received[1], received[0])
+    got = [lax.ppermute(halves[r], plane, swap_pairs((nx, ny), (r, None))) for r in (0, 1)]
+    strips = []
+    for s in range(rounds_y):
+        for array, turn in zip(packed[2 + 3 * s : 5 + 3 * s], (None, 0, 1)):
+            strips.append(lax.ppermute(array, plane, swap_pairs((nx, ny), (turn, s))))
     hinv, hside = call(functools.partial(inverse_sums, (nx, ny, nz)), [(16, 24, 128), (2, 24, 128)])
     ext, ends = call(
-        functools.partial(extend, two),
+        functools.partial(extend, (nx, ny, nz)),
         [(7, 16, 24, 128), (7, 24, 128)],
-        lo, hi, xl, xh, *low_side, *high_side,
+        *halves, *got, *strips,
     )
-    from_low = lax.ppermute(ends, "gz", line_pairs(nz, 1))
-    from_high = lax.ppermute(ends, "gz", line_pairs(nz, -1))
-    field = (3, 8, 16, 128)
-    image, inverse, sums = call(
-        apply_operator,
-        [field, field, (8, 128)],
-        ext, ends, from_low, from_high, residual, labels,
+    ends_got = [lax.ppermute(ends, "gz", swap_pairs((nz,), (r,))) for r in (0, 1)]
+    image, inverse, sums, around = call(
+        functools.partial(apply_operator, nz),
+        [field, field, (8, 128), (7, 24, 128)],
+        ext, *ends_got, residual, labels,
         scratch=[pltpu.VMEM((4, 3, 3, 10, 16, 128), f32)],
     )
     total = total_over(sums, mesh_shape)
     return tuple(
         call(
             finish_step,
-            [field, field, field, (8, 16, 128)],
-            ext, ends, from_low, from_high, total, image, inverse, residual, direction, hinv, hside,
+            [field, field, field, flat],
+            ext, ends, around, total, image, inverse, residual, direction, hinv, hside,
             scratch=[pltpu.VMEM((6, 3, 16, 24, 128), f32), pltpu.VMEM((16, 24, 128), f32)],
         )
     )

time: 55.6 us -> 47.1 us (0.85)
  local copies, waits for them, and re-layouts: 3.54 us -> 0.01 us
  starting transfers between devices: 25.8 us -> 22.6 us
  waiting for transfers between devices: 15.5 us -> 13 us
  Pallas kernels: 9.58 us -> 10.6 us
    ppermute x7, starting transfers between devices: 17.6 us -> 9.54 us  [the longest x3 6.06 us: per_device(): strips.append(lax.ppermute(array, plane, swap_pairs((nx, ny), (turn, s))))]
    ppermute x5, starting transfers between devices: 8.25 us -> 13 us  [total_over(): got.append(lax.ppermute(value, axis, pairs))]
    unnamed x14 -> x6, local copies, waits for them, and re-layouts: 3.54 us -> 0.01 us
    ppermute x7, waiting for transfers between devices: 6.85 us -> 4.55 us  [the longest x3 2.3 us: per_device(): strips.append(lax.ppermute(array, plane, swap_pairs((nx, ny), (turn, s))))]
    pallas_call x5, Pallas kernels: 9.58 us -> 10.6 us  [call(): pl.pallas_call(body, out_shape=[jax.ShapeDtypeStruct(shape, f32) for shap...]
  transfers between devices with their start and end apart: 12 -> 12, of which waited for: 9 -> 7; matrix products, arithmetic and copies ran while one was open for 0% -> 0% of each run, Pallas kernels for 0% -> 1%
where the time goes in v2:
time: 47.1 us; the launch traced here: 46.9 us
  starting transfers between devices  22.6 us (48%)
  waiting for transfers between devices  13 us (28%)
  Pallas kernels  10.6 us (23%)
  between operations  0.72 us (2%)
    ppermute x5, starting transfers between devices, total_over(): got.append(lax.ppermute(value, axis, pairs))  13 us
    pallas_call x5, Pallas kernels, call(): pl.pallas_call(body, out_shape=[jax.ShapeDtypeStruct(shape, f32) for shap...  10.6 us
    ppermute x5, waiting for transfers between devices, total_over(): got.append(lax.ppermute(value, axis, pairs))  8.47 us
    ppermute x3, starting transfers between devices, per_device(): strips.append(lax.ppermute(array, plane, swap_pairs((nx, ny), (turn, s))))  6.06 us
    ppermute x3, waiting for transfers between devices, per_device(): strips.append(lax.ppermute(array, plane, swap_pairs((nx, ny), (turn, s))))  2.3 us
    ppermute x2, starting transfers between devices, per_device(): lax.ppermute(ends, 'gz', swap_pairs((nz,), (r,)))  2.3 us
    ppermute x2, waiting for transfers between devices, per_device(): lax.ppermute(ends, 'gz', swap_pairs((nz,), (r,)))  2.25 us
    ppermute x2, starting transfers between devices, per_device(): lax.ppermute(halves[r], plane, swap_pairs((nx, ny), (r, None)))  1.18 us
  transfers between devices with their start and end apart: 12, of which 7 were waited for; matrix products, arithmetic and copies ran while one was open for 0% of the time, Pallas kernels for 1%

profile of v2, /device:TPU:0, one launch (start us, length us, event | category | flops | bytes accessed | tf_op | source)
XLA Modules:
  0.0 46.9 jit_solution(10837305525483282890)
XLA Ops:
  0.6 0.0 copy-start.2
  0.6 0.0 copy-start
  0.7 1.2 %shard_map.84 = (f32[7,4,16,128]{3,2,1,0:T(8,128)S(1)}, f32[7,4,16,128]{3,2,1,0:T(8,128)S(1)}, f32[7,4,8,128]{3,2,1,0:T(8,128)S(1)}, f32[7,2,8,128]{3,2,1,0:T(8,128)S(1)}, f32[7,2,8,128]{3,2,1,0:T(8,128)S(1)}) custom-call(f32[3,8,16,128]{3,2,1,0:T(8,128)} %sol_any.1, f32[3,8,16,128]{3,2,1,0:T(8,128)} %dire.1, f32[8,16,128]{2,1,0:T(8,128)} %den_any.1, ...), custom_call_target="tpu_custom_call" | custom-call | flops 20000000 | bytes 20000 | tf_op jit(solution)/shard_map/pallas_call | solution.py:48
  1.9 0.5 %collective-permute-start = (f32[7,4,16,128]{3,2,1,0:T(8,128)S(1)}, f32[7,4,16,128]{3,2,1,0:T(8,128)S(1)}, u32[]{:S(2)}, u32[]{:S(2)}) collective-permute-start(f32[7,4,16,128]{3,2,1,0:T(8,128)S(1)} %get-tuple-element.17.half0), channel_id=1, source_target_pairs={{0,8},{4,12},{8,0},{12,4},{16,24},{20,28},{24,16},{28,20},{1,9},{5... | collective-permute-start | bytes 688136 | tf_op jit(solution)/shard_map/ppermute | solution.py:520
  2.4 0.7 %collective-permute-start.1 = (f32[7,4,16,128]{3,2,1,0:T(8,128)S(1)}, f32[7,4,16,128]{3,2,1,0:T(8,128)S(1)}, u32[]{:S(2)}, u32[]{:S(2)}) collective-permute-start(f32[7,4,16,128]{3,2,1,0:T(8,128)S(1)} %get-tuple-element.18.half1), channel_id=1, source_target_pairs={{0,0},{4,4},{8,16},{12,20},{16,8},{20,12},{24,24},{28,28},{1,1},{5... | collective-permute-start | bytes 688136 | tf_op jit(solution)/shard_map/ppermute | solution.py:520
  3.0 2.6 %collective-permute-start.2 = (f32[7,4,8,128]{3,2,1,0:T(8,128)S(1)}, f32[7,4,8,128]{3,2,1,0:T(8,128)S(1)}, u32[]{:S(2)}, u32[]{:S(2)}) collective-permute-start(f32[7,4,8,128]{3,2,1,0:T(8,128)S(1)} %get-tuple-element.19), channel_id=1, source_target_pairs={{0,4},{4,0},{8,12},{12,8},{16,20},{20,16},{24,28},{28,24},{1,5},{5... | collective-permute-start | bytes 344072 | tf_op jit(solution)/shard_map/ppermute | solution.py:524
  5.6 2.7 %collective-permute-start.3 = (f32[7,2,8,128]{3,2,1,0:T(8,128)S(1)}, f32[7,2,8,128]{3,2,1,0:T(8,128)S(1)}, u32[]{:S(2)}, u32[]{:S(2)}) collective-permute-start(f32[7,2,8,128]{3,2,1,0:T(8,128)S(1)} %get-tuple-element.20), channel_id=1, source_target_pairs={{0,12},{4,8},{8,4},{12,0},{16,28},{20,24},{24,20},{28,16},{1,13},{... | collective-permute-start | bytes 172040 | tf_op jit(solution)/shard_map/ppermute | solution.py:524
  8.3 0.0 copy-start.1
  8.3 0.8 %collective-permute-start.4 = (f32[7,2,8,128]{3,2,1,0:T(8,128)S(1)}, f32[7,2,8,128]{3,2,1,0:T(8,128)S(1)}, u32[]{:S(2)}, u32[]{:S(2)}) collective-permute-start(f32[7,2,8,128]{3,2,1,0:T(8,128)S(1)} %get-tuple-element.21), channel_id=1, source_target_pairs={{0,0},{4,4},{8,20},{12,16},{16,12},{20,8},{24,24},{28,28},{1,1},{5... | collective-permute-start | bytes 172040 | tf_op jit(solution)/shard_map/ppermute | solution.py:524
  9.1 2.3 %collective-permute-done.3.refs_1_ = f32[7,2,8,128]{3,2,1,0:T(8,128)S(1)} collective-permute-done((f32[7,2,8,128]{3,2,1,0:T(8,128)S(1)}, f32[7,2,8,128]{3,2,1,0:T(8,128)S(1)}, u32[]{:S(2)}, u32[]{:S(2)}) %collective-permute-start.3) | collective-permute-done | bytes 57376 | tf_op jit(solution)/shard_map/ppermute | solution.py:524
  11.4 0.0 collective-permute-done.4.refs_2_
  11.4 0.0 collective-permute-done.2.refs_0_
  11.4 0.0 collective-permute-done.got0
  11.4 0.0 collective-permute-done.1.got1
  11.4 0.5 shard_map.85
  11.9 1.6 %collective-permute-start.5 = (f32[7,24,128]{2,1,0:T(8,128)S(1)}, f32[7,24,128]{2,1,0:T(8,128)S(1)}, u32[]{:S(2)}, u32[]{:S(2)}) collective-permute-start(f32[7,24,128]{2,1,0:T(8,128)S(1)} %get-tuple-element.23.ends), channel_id=1, source_target_pairs={{0,1},{1,0},{2,3},{3,2},{4,5},{5,4},{6,7},{7,6},{8,9},{9,8},{10,11... | collective-permute-start | bytes 258056 | tf_op jit(solution)/shard_map/ppermute | solution.py:531
  13.5 0.7 %collective-permute-start.6 = (f32[7,24,128]{2,1,0:T(8,128)S(1)}, f32[7,24,128]{2,1,0:T(8,128)S(1)}, u32[]{:S(2)}, u32[]{:S(2)}) collective-permute-start(f32[7,24,128]{2,1,0:T(8,128)S(1)} %get-tuple-element.23.ends), channel_id=1, source_target_pairs={{0,0},{1,2},{2,1},{3,3},{4,4},{5,6},{6,5},{7,7},{8,8},{9,10},{10,9... | collective-permute-start | bytes 258056 | tf_op jit(solution)/shard_map/ppermute | solution.py:531
  14.2 2.2 %collective-permute-done.5.got0 = f32[7,24,128]{2,1,0:T(8,128)S(1)} collective-permute-done((f32[7,24,128]{2,1,0:T(8,128)S(1)}, f32[7,24,128]{2,1,0:T(8,128)S(1)}, u32[]{:S(2)}, u32[]{:S(2)}) %collective-permute-start.5) | collective-permute-done | bytes 86048 | tf_op jit(solution)/shard_map/ppermute | solution.py:531
  16.4 0.0 collective-permute-done.6.got1
  16.4 0.0 copy-done.2
  16.4 0.0 copy-done
  16.5 2.4 %shard_map.86 = (f32[3,8,16,128]{3,2,1,0:T(8,128)S(1)}, f32[3,8,16,128]{3,2,1,0:T(8,128)S(1)}, f32[8,128]{1,0:T(8,128)S(1)}, f32[7,24,128]{2,1,0:T(8,128)S(1)}) custom-call(f32[7,16,24,128]{3,2,1,0:T(8,128)S(1)} %get-tuple-element.22.ext, f32[7,24,128]{2,1,0:T(8,128)S(1)} %collective-permute-done.5.got0, f32[7,24,128]{2,1,0:T(8,128)S(1)} %collective-permute-done.6.got1, ...), custom_call_target="tpu_custom_call" | custom-call | flops 20000000 | bytes 20000 | tf_op jit(solution)/shard_map/pallas_call | solution.py:48
  18.9 2.2 %collective-permute-start.7 = (f32[8,128]{1,0:T(8,128)S(1)}, f32[8,128]{1,0:T(8,128)S(1)}, u32[]{:S(2)}, u32[]{:S(2)}) collective-permute-start(f32[8,128]{1,0:T(8,128)S(1)} %get-tuple-element.25), channel_id=1, source_target_pairs={{0,8},{8,0},{16,24},{24,16},{1,9},{9,1},{17,25},{25,17},{2,10},{10... | collective-permute-start | bytes 12296 | tf_op jit(solution)/shard_map/ppermute | solution.py:496
  21.1 0.8 %collective-permute-done.7 = f32[8,128]{1,0:T(8,128)S(1)} collective-permute-done((f32[8,128]{1,0:T(8,128)S(1)}, f32[8,128]{1,0:T(8,128)S(1)}, u32[]{:S(2)}, u32[]{:S(2)}) %collective-permute-start.7) | collective-permute-done | bytes 4128 | tf_op jit(solution)/shard_map/ppermute | solution.py:496
  21.9 2.3 %collective-permute-start.8 = (f32[8,128]{1,0:T(8,128)S(1)}, f32[8,128]{1,0:T(8,128)S(1)}, u32[]{:S(2)}, u32[]{:S(2)}) collective-permute-start(f32[8,128]{1,0:T(8,128)S(1)} %add.15), channel_id=1, source_target_pairs={{0,16},{8,24},{16,0},{24,8},{1,17},{9,25},{17,1},{25,9},{2,18},{10... | collective-permute-start | bytes 12296 | tf_op jit(solution)/shard_map/ppermute | solution.py:496
  24.2 1.6 %collective-permute-done.8 = f32[8,128]{1,0:T(8,128)S(1)} collective-permute-done((f32[8,128]{1,0:T(8,128)S(1)}, f32[8,128]{1,0:T(8,128)S(1)}, u32[]{:S(2)}, u32[]{:S(2)}) %collective-permute-start.8) | collective-permute-done | bytes 4128 | tf_op jit(solution)/shard_map/ppermute | solution.py:496
  25.8 0.5 collective-permute-start.9
  26.3 3.2 %collective-permute-done.9 = f32[8,128]{1,0:T(8,128)S(1)} collective-permute-done((f32[8,128]{1,0:T(8,128)S(1)}, f32[8,128]{1,0:T(8,128)S(1)}, u32[]{:S(2)}, u32[]{:S(2)}) %collective-permute-start.9) | collective-permute-done | bytes 4128 | tf_op jit(solution)/shard_map/ppermute | solution.py:496
  29.4 4.6 %collective-permute-start.10 = (f32[8,128]{1,0:T(8,128)S(1)}, f32[8,128]{1,0:T(8,128)S(1)}, u32[]{:S(2)}, u32[]{:S(2)}) collective-permute-start(f32[8,128]{1,0:T(8,128)S(1)} %add.17), channel_id=1, source_target_pairs={{0,1},{1,0},{2,3},{3,2},{4,5},{5,4},{6,7},{7,6},{8,9},{9,8},{10,11... | collective-permute-start | bytes 12296 | tf_op jit(solution)/shard_map/ppermute | solution.py:496
  34.0 1.6 %collective-permute-done.10 = f32[8,128]{1,0:T(8,128)S(1)} collective-permute-done((f32[8,128]{1,0:T(8,128)S(1)}, f32[8,128]{1,0:T(8,128)S(1)}, u32[]{:S(2)}, u32[]{:S(2)}) %collective-permute-start.10) | collective-permute-done | bytes 4128 | tf_op jit(solution)/shard_map/ppermute | solution.py:496
  35.6 3.5 %collective-permute-start.11 = (f32[8,128]{1,0:T(8,128)S(1)}, f32[8,128]{1,0:T(8,128)S(1)}, u32[]{:S(2)}, u32[]{:S(2)}) collective-permute-start(f32[8,128]{1,0:T(8,128)S(1)} %add.18), channel_id=1, source_target_pairs={{0,2},{1,3},{2,0},{3,1},{4,6},{5,7},{6,4},{7,5},{8,10},{9,11},{10,... | collective-permute-start | bytes 12296 | tf_op jit(solution)/shard_map/ppermute | solution.py:496
  39.1 0.3 shard_map.87
  39.3 1.3 %collective-permute-done.11 = f32[8,128]{1,0:T(8,128)S(1)} collective-permute-done((f32[8,128]{1,0:T(8,128)S(1)}, f32[8,128]{1,0:T(8,128)S(1)}, u32[]{:S(2)}, u32[]{:S(2)}) %collective-permute-start.11) | collective-permute-done | bytes 4128 | tf_op jit(solution)/shard_map/ppermute | solution.py:496
  40.7 0.0 copy-done.1
  40.7 6.3 %shard_map.88 = (f32[3,8,16,128]{3,2,1,0:T(8,128)}, f32[3,8,16,128]{3,2,1,0:T(8,128)}, f32[3,8,16,128]{3,2,1,0:T(8,128)}, f32[8,16,128]{2,1,0:T(8,128)}) custom-call(f32[7,16,24,128]{3,2,1,0:T(8,128)S(1)} %get-tuple-element.22.ext, f32[7,24,128]{2,1,0:T(8,128)S(1)} %get-tuple-element.23.ends, f32[7,24,128]{2,1,0:T(8,128)S(1)} %get-tuple-element.24.around, ...), custom_call_target="tpu_custom_call" | custom-call | flops 20000000 | bytes 20000 | tf_op jit(solution)/shard_map/pallas_call | solution.py:48
  (5 shorter events, 0.0 us)
Async XLA Ops:
  0.6 15.8 %copy-start.2 = (s32[8,16,128]{2,1,0:T(8,128)S(1)}, s32[8,16,128]{2,1,0:T(8,128)}, u32[]{:S(2)}) copy-start(s32[8,16,128]{2,1,0:T(8,128)} %lab.1) | copy-start | bytes 196612
  0.6 15.8 %copy-start = (f32[3,8,16,128]{3,2,1,0:T(8,128)S(1)}, f32[3,8,16,128]{3,2,1,0:T(8,128)}, u32[]{:S(2)}) copy-start(f32[3,8,16,128]{3,2,1,0:T(8,128)} %res.3) | copy-start | bytes 589828
  1.9 9.6 %collective-permute-start = (f32[7,4,16,128]{3,2,1,0:T(8,128)S(1)}, f32[7,4,16,128]{3,2,1,0:T(8,128)S(1)}, u32[]{:S(2)}, u32[]{:S(2)}) collective-permute-start(f32[7,4,16,128]{3,2,1,0:T(8,128)S(1)} %get-tuple-element.17.half0), channel_id=1, source_target_pairs={{0,8},{4,12},{8,0},{12,4},{16,24},{20,28},{24,16},{28,20},{1,9},{5... | collective-permute-start | bytes 688136 | tf_op jit(solution)/shard_map/ppermute | solution.py:520
  2.4 9.0 %collective-permute-start.1 = (f32[7,4,16,128]{3,2,1,0:T(8,128)S(1)}, f32[7,4,16,128]{3,2,1,0:T(8,128)S(1)}, u32[]{:S(2)}, u32[]{:S(2)}) collective-permute-start(f32[7,4,16,128]{3,2,1,0:T(8,128)S(1)} %get-tuple-element.18.half1), channel_id=1, source_target_pairs={{0,0},{4,4},{8,16},{12,20},{16,8},{20,12},{24,24},{28,28},{1,1},{5... | collective-permute-start | bytes 688136 | tf_op jit(solution)/shard_map/ppermute | solution.py:520
  3.0 8.4 %collective-permute-start.2 = (f32[7,4,8,128]{3,2,1,0:T(8,128)S(1)}, f32[7,4,8,128]{3,2,1,0:T(8,128)S(1)}, u32[]{:S(2)}, u32[]{:S(2)}) collective-permute-start(f32[7,4,8,128]{3,2,1,0:T(8,128)S(1)} %get-tuple-element.19), channel_id=1, source_target_pairs={{0,4},{4,0},{8,12},{12,8},{16,20},{20,16},{24,28},{28,24},{1,5},{5... | collective-permute-start | bytes 344072 | tf_op jit(solution)/shard_map/ppermute | solution.py:524
  5.6 5.8 %collective-permute-start.3 = (f32[7,2,8,128]{3,2,1,0:T(8,128)S(1)}, f32[7,2,8,128]{3,2,1,0:T(8,128)S(1)}, u32[]{:S(2)}, u32[]{:S(2)}) collective-permute-start(f32[7,2,8,128]{3,2,1,0:T(8,128)S(1)} %get-tuple-element.20), channel_id=1, source_target_pairs={{0,12},{4,8},{8,4},{12,0},{16,28},{20,24},{24,20},{28,16},{1,13},{... | collective-permute-start | bytes 172040 | tf_op jit(solution)/shard_map/ppermute | solution.py:524
  8.3 32.3 %copy-start.1 = (f32[3,8,16,128]{3,2,1,0:T(8,128)S(1)}, f32[3,8,16,128]{3,2,1,0:T(8,128)}, u32[]{:S(2)}) copy-start(f32[3,8,16,128]{3,2,1,0:T(8,128)} %dire.1) | copy-start | bytes 589828
  8.3 3.1 %collective-permute-start.4 = (f32[7,2,8,128]{3,2,1,0:T(8,128)S(1)}, f32[7,2,8,128]{3,2,1,0:T(8,128)S(1)}, u32[]{:S(2)}, u32[]{:S(2)}) collective-permute-start(f32[7,2,8,128]{3,2,1,0:T(8,128)S(1)} %get-tuple-element.21), channel_id=1, source_target_pairs={{0,0},{4,4},{8,20},{12,16},{16,12},{20,8},{24,24},{28,28},{1,1},{5... | collective-permute-start | bytes 172040 | tf_op jit(solution)/shard_map/ppermute | solution.py:524
  11.9 4.6 %collective-permute-start.5 = (f32[7,24,128]{2,1,0:T(8,128)S(1)}, f32[7,24,128]{2,1,0:T(8,128)S(1)}, u32[]{:S(2)}, u32[]{:S(2)}) collective-permute-start(f32[7,24,128]{2,1,0:T(8,128)S(1)} %get-tuple-element.23.ends), channel_id=1, source_target_pairs={{0,1},{1,0},{2,3},{3,2},{4,5},{5,4},{6,7},{7,6},{8,9},{9,8},{10,11... | collective-permute-start | bytes 258056 | tf_op jit(solution)/shard_map/ppermute | solution.py:531
  13.5 2.9 %collective-permute-start.6 = (f32[7,24,128]{2,1,0:T(8,128)S(1)}, f32[7,24,128]{2,1,0:T(8,128)S(1)}, u32[]{:S(2)}, u32[]{:S(2)}) collective-permute-start(f32[7,24,128]{2,1,0:T(8,128)S(1)} %get-tuple-element.23.ends), channel_id=1, source_target_pairs={{0,0},{1,2},{2,1},{3,3},{4,4},{5,6},{6,5},{7,7},{8,8},{9,10},{10,9... | collective-permute-start | bytes 258056 | tf_op jit(solution)/shard_map/ppermute | solution.py:531
  18.9 3.1 %collective-permute-start.7 = (f32[8,128]{1,0:T(8,128)S(1)}, f32[8,128]{1,0:T(8,128)S(1)}, u32[]{:S(2)}, u32[]{:S(2)}) collective-permute-start(f32[8,128]{1,0:T(8,128)S(1)} %get-tuple-element.25), channel_id=1, source_target_pairs={{0,8},{8,0},{16,24},{24,16},{1,9},{9,1},{17,25},{25,17},{2,10},{10... | collective-permute-start | bytes 12296 | tf_op jit(solution)/shard_map/ppermute | solution.py:496
  21.9 3.9 %collective-permute-start.8 = (f32[8,128]{1,0:T(8,128)S(1)}, f32[8,128]{1,0:T(8,128)S(1)}, u32[]{:S(2)}, u32[]{:S(2)}) collective-permute-start(f32[8,128]{1,0:T(8,128)S(1)} %add.15), channel_id=1, source_target_pairs={{0,16},{8,24},{16,0},{24,8},{1,17},{9,25},{17,1},{25,9},{2,18},{10... | collective-permute-start | bytes 12296 | tf_op jit(solution)/shard_map/ppermute | solution.py:496
  25.8 3.6 %collective-permute-start.9 = (f32[8,128]{1,0:T(8,128)S(1)}, f32[8,128]{1,0:T(8,128)S(1)}, u32[]{:S(2)}, u32[]{:S(2)}) collective-permute-start(f32[8,128]{1,0:T(8,128)S(1)} %add.16), channel_id=1, source_target_pairs={{0,4},{4,0},{1,5},{5,1},{2,6},{6,2},{3,7},{7,3},{8,12},{12,8},{9,1... | collective-permute-start | bytes 12296 | tf_op jit(solution)/shard_map/ppermute | solution.py:496
  29.4 6.2 %collective-permute-start.10 = (f32[8,128]{1,0:T(8,128)S(1)}, f32[8,128]{1,0:T(8,128)S(1)}, u32[]{:S(2)}, u32[]{:S(2)}) collective-permute-start(f32[8,128]{1,0:T(8,128)S(1)} %add.17), channel_id=1, source_target_pairs={{0,1},{1,0},{2,3},{3,2},{4,5},{5,4},{6,7},{7,6},{8,9},{9,8},{10,11... | collective-permute-start | bytes 12296 | tf_op jit(solution)/shard_map/ppermute | solution.py:496
  35.6 5.1 %collective-permute-start.11 = (f32[8,128]{1,0:T(8,128)S(1)}, f32[8,128]{1,0:T(8,128)S(1)}, u32[]{:S(2)}, u32[]{:S(2)}) collective-permute-start(f32[8,128]{1,0:T(8,128)S(1)} %add.18), channel_id=1, source_target_pairs={{0,2},{1,3},{2,0},{3,1},{4,6},{5,7},{6,4},{7,5},{8,10},{9,11},{10,... | collective-permute-start | bytes 12296 | tf_op jit(solution)/shard_map/ppermute | solution.py:496

commit v3 on v2

--- a/solution.py
+++ b/solution.py
@@ -41,7 +41,7 @@
     return value if amount == 0 else pltpu.roll(value, amount, axis)
 
 
-def call(body, outs, *args, scratch=(), cost=20000, far=()):
+def call(body, outs, *args, scratch=(), cost=20000, far=(), far_out=False):
     args = [
         pltpu.with_memory_space_constraint(a, pltpu.HBM) if i in far else a for i, a in enumerate(args)
     ]
@@ -51,7 +51,7 @@
         in_specs=[
             pl.BlockSpec(memory_space=pl.ANY if i in far else pltpu.VMEM) for i in range(len(args))
         ],
-        out_specs=[pl.BlockSpec(memory_space=pltpu.VMEM)] * len(outs),
+        out_specs=[pl.BlockSpec(memory_space=pl.ANY if far_out else pltpu.VMEM)] * len(outs),
         scratch_shapes=list(scratch),
         compiler_params=pltpu.CompilerParams(vmem_limit_bytes=24 * 1024 * 1024),
         cost_estimate=pl.CostEstimate(flops=cost * 1000, bytes_accessed=cost, transcendentals=0),
@@ -326,19 +326,35 @@
                 along, sign = d[c], o[c]
             else:
                 along = along + d[c] if o[c] == sign else along - d[c]
-    return (0.5 / norm) * square + (0.5 / (norm * norm)) * (along * along)
-
-
-flat_half = [(1, -1, 0), (1, 0, 0), (1, 1, 0), (0, 1, 0)]
-up_half = [(a, b, 1) for a in (-1, 0, 1) for b in (-1, 0, 1)]
+    if norm == 1:
+        return square + along * along
+    return (1.0 / norm) * square + (1.0 / (norm * norm)) * (along * along)
+
+
+pairs = [((1, 0, 0), 0, 0, 0, 0)]
+pairs += [((a, 1, 0), 0, 0, 2, 2) for a in (-1, 0, 1)]
+pairs += [((a, 0, 1), 0, 0, 1, 1) for a in (-1, 0, 1)]
+pairs += [((a, 1, 1), 0, 0, 3, 3) for a in (-1, 0, 1)]
+pairs += [((a, -1, 1), 2, 2, 1, 1) for a in (-1, 0, 1)]
+energy_scale = -penalty * (1.0 - stiff_floor) * 0.5
+
+
+def plus(old, new):
+    return new if old is None else old + new
 
 
 def finish_step(
     ext, ends, around, total, image, inverse, res, dire, hinv, hside,
-    new_sol, new_res, new_dir, sens, us, scaled,
+    new_sol_any, new_res_any, new_dir_any, sens_any, us, scaled, new_sol, new_res, new_dir, sens, sems,
 ):
     lane = lanes_of((24, 128))
     lows = lane % 8 < 4
+    copies = [
+        pltpu.make_async_copy(source, target, sems.at[i])
+        for i, (source, target) in enumerate(
+            ((new_res, new_res_any), (new_dir, new_dir_any), (new_sol, new_sol_any), (sens, sens_any))
+        )
+    ]
     tot = jnp.sum(total[...], axis=1, keepdims=True)
     rz, pq, s2, s3 = tot[0:1], tot[1:2], tot[2:3], tot[3:4]
     alpha = rz / pq
@@ -349,9 +365,10 @@
             r = res[c, x] - alpha * image[c, x]
             new_res[c, x] = r
             new_dir[c, x] = r * inverse[c, x] + beta * dire[c, x]
-
-    halos = []
-    lefts, rights = [], []
+    copies[0].start()
+    copies[1].start()
+
+    halos, lefts, rights = [], [], []
     for c in range(3):
         halo_u = around[3 + c] + alpha * around[c]
         own_u = ends[3 + c] + alpha * ends[c]
@@ -365,55 +382,61 @@
                 new_sol[c, X - 4] = roll(u, -HALO, 0)[0:16]
             near = roll(halos[c], 124 - 8 * X, 1)
             up = roll(jnp.where(lane == 0, near, u), -1, 1)
-            for z, plane in enumerate((u, up)):
-                us[3 * z, c, X] = roll(plane, 1, 0)
-                us[3 * z + 1, c, X] = plane
-                us[3 * z + 2, c, X] = roll(plane, -1, 0)
+            us[0, c, X] = u
+            us[1, c, X] = up
+            us[2, c, X] = roll(u, -1, 0)
+            us[3, c, X] = roll(up, -1, 0)
+    copies[2].start()
 
     sides, side_low = [], None
     den_left = jnp.where(lows, around[6], ends[6])
     den_right = jnp.where(lows, ends[6], around[6])
     for s, (u, den) in enumerate(((lefts, den_left), (rights, den_right))):
-        turned = {oy: [roll(v, -oy, 0) for v in u] for oy in (-1, 0, 1)}
-        forward = jnp.zeros((24, 128), f32)
-        back = {(oy, oz): jnp.zeros((24, 128), f32) for oy in (-1, 0, 1) for oz in (0, 1)}
-        for o in flat_half + up_half:
-            move = 8 * o[0] + o[2]
-            g = quadratic([u[c] - roll(turned[o[1]][c], -move, 1) for c in range(3)], o)
-            forward = forward + g
-            back[o[1], o[2]] = back[o[1], o[2]] + roll(g, 8 * o[0], 1)
-        flat = back[0, 0] + roll(back[1, 0], 1, 0) + roll(back[-1, 0], -1, 0)
-        up = back[0, 1] + roll(back[1, 1], 1, 0) + roll(back[-1, 1], -1, 0)
+        up = [roll(v, -1, 1) for v in u]
+        moved = [u, up, [roll(v, -1, 0) for v in u], [roll(v, -1, 0) for v in up]]
+        far = {}
+        acc = {}
+        for o, field0, frame0, field1, frame1 in pairs:
+            key = (field1, o[0])
+            if key not in far:
+                far[key] = [roll(v, -8 * o[0], 1) for v in moved[field1]]
+            g = quadratic([moved[field0][c] - far[key][c] for c in range(3)], o)
+            acc[frame0, 0] = plus(acc.get((frame0, 0)), g)
+            acc[frame1, o[0]] = plus(acc.get((frame1, o[0])), g)
+        frames = []
+        for frame in range(4):
+            value = None
+            for a in (-1, 0, 1):
+                if (frame, a) in acc:
+                    value = plus(value, roll(acc[frame, a], 8 * a, 1))
+            frames.append(value)
+        up = frames[1] + roll(frames[3], 1, 0)
         if s == 0:
             side_low = up
-        energy = forward + flat + roll(up, 1, 1)
-        sides.append((-penalty * (1.0 - stiff_floor)) * (den * den) * energy * hside[s])
+        energy = frames[0] + roll(frames[2], 1, 0) + roll(up, 1, 1)
+        sides.append(energy_scale * (den * den) * energy * hside[s])
     ends_scaled = jnp.where(lows, sides[0], sides[1])
 
-    zero = jnp.zeros((24, 128), f32)
-    forward = [zero] * 16
-    back = [{(oy, oz): None for oy in (-1, 0, 1) for oz in (0, 1)} for _ in range(16)]
-    for X in range(0, 16):
-        mine = [us[1, c, X] for c in range(3)]
-        for o in flat_half + up_half:
+    acc = [[None] * 4 for _ in range(16)]
+    for X in range(16):
+        for o, field0, frame0, field1, frame1 in pairs:
             to = X + o[0]
-            if not 0 <= to < 16:
+            if not 0 <= to < 16 or not (1 <= X < 15 or 1 <= to < 15):
                 continue
-            k = 3 * o[2] + o[1] + 1
-            g = quadratic([mine[c] - us[k, c, to] for c in range(3)], o)
-            forward[X] = forward[X] + g
-            old = back[to][o[1], o[2]]
-            back[to][o[1], o[2]] = g if old is None else old + g
+            g = quadratic([us[field0, c, X] - us[field1, c, to] for c in range(3)], o)
+            if 1 <= X < 15:
+                acc[X][frame0] = plus(acc[X][frame0], g)
+            if 1 <= to < 15:
+                acc[to][frame1] = plus(acc[to][frame1], g)
         done = X - 1
         if done >= 1:
-            bk = back[done]
-            flat = bk[0, 0] + roll(bk[1, 0], 1, 0) + roll(bk[-1, 0], -1, 0)
-            up = bk[0, 1] + roll(bk[1, 1], 1, 0) + roll(bk[-1, 1], -1, 0)
+            frames = acc[done]
+            up = frames[1] + roll(frames[3], 1, 0)
             below = roll(side_low, 127 - (8 * done + 3), 1)
             up = roll(jnp.where(lane == 127, below, up), 1, 1)
             den = ext[6, done]
-            energy = forward[done] + flat + up
-            scaled[done] = (-penalty * (1.0 - stiff_floor)) * (den * den) * energy * hinv[done]
+            energy = frames[0] + roll(frames[2], 1, 0) + up
+            scaled[done] = energy_scale * (den * den) * energy * hinv[done]
 
     rows = [[None] * (RAD + 1) for _ in range(8)]
     for X in range(1, 15):
@@ -446,6 +469,9 @@
             for b in range(1, RAD + 1):
                 value = value + roll(rows[x][b], b, 0) + roll(rows[x][b], -b, 0)
             sens[x] = roll(value, -HALO, 0)[0:16]
+    copies[3].start()
+    for copy in copies:
+        copy.wait()
 
 
 def partner(place, turn, count):
@@ -481,23 +507,7 @@
 
 
 def total_over(value, mesh_shape):
-    for axis in AXES:
-        count = mesh_shape[axis]
-        stride = 1
-        for factor in prime_factors(count):
-            block = stride * factor
-            got = []
-            for step in range(1, factor):
-                pairs = []
-                for i in range(count):
-                    digit = (i // stride) % factor
-                    to = i + (((digit + step) % factor) - digit) * stride
-                    pairs.append((i, to))
-                got.append(lax.ppermute(value, axis, pairs))
-            for other in got:
-                value = value + other
-            stride = block
-    return value
+    return jnp.sum(lax.all_gather(value, AXES), axis=0)
 
 
 def per_device(mesh_shape, solution, residual, direction, density, labels):
@@ -541,7 +551,12 @@
             finish_step,
             [field, field, field, flat],
             ext, ends, around, total, image, inverse, residual, direction, hinv, hside,
-            scratch=[pltpu.VMEM((6, 3, 16, 24, 128), f32), pltpu.VMEM((16, 24, 128), f32)],
+            scratch=[
+                pltpu.VMEM((4, 3, 16, 24, 128), f32), pltpu.VMEM((16, 24, 128), f32),
+                pltpu.VMEM(field, f32), pltpu.VMEM(field, f32), pltpu.VMEM(field, f32),
+                pltpu.VMEM(flat, f32), pltpu.SemaphoreType.DMA((4,)),
+            ],
+            far_out=True,
         )
     )
 

time: 47.1 us -> 94.3 us (2.00); the launches traced: 46.9 us -> 92.9 us
  blocking collectives: 0 us -> 69 us
  starting transfers between devices: 22.6 us -> 9.54 us
  waiting for transfers between devices: 13 us -> 4.28 us
  Pallas kernels: 10.6 us -> 9.38 us
    all_gather x0 -> x1, blocking collectives: none -> 69 us  [total_over(): return jnp.sum(lax.all_gather(value, AXES), axis=0)]
    ppermute x5 -> x0, starting transfers between devices: 13 us -> none  [total_over(): got.append(lax.ppermute(value, axis, pairs))]
    ppermute x5 -> x0, waiting for transfers between devices: 8.47 us -> none  [total_over(): got.append(lax.ppermute(value, axis, pairs))]
    pallas_call x5, Pallas kernels: 10.6 us -> 9.38 us  [call(): pl.pallas_call(body, out_shape=[jax.ShapeDtypeStruct(shape, f32) for shap...]
  transfers between devices with their start and end apart: 12 -> 7, of which waited for: 7 -> 2; matrix products, arithmetic and copies ran while one was open for 0% -> 0% of each run, Pallas kernels for 1% -> 0%
where the time goes in v3:
time: 94.3 us; the launch traced here: 92.9 us
  blocking collectives  69 us (73%)
  starting transfers between devices  9.54 us (10%)
  Pallas kernels  9.38 us (10%)
  waiting for transfers between devices  4.28 us (5%)
    all_gather x1, blocking collectives, total_over(): return jnp.sum(lax.all_gather(value, AXES), axis=0)  69 us
    pallas_call x5, Pallas kernels, call(): pl.pallas_call(body, out_shape=[jax.ShapeDtypeStruct(shape, f32) for shap...  9.38 us
    ppermute x3, starting transfers between devices, per_device(): strips.append(lax.ppermute(array, plane, swap_pairs((nx, ny), (turn, s))))  6.06 us
    ppermute x3, waiting for transfers between devices, per_device(): strips.append(lax.ppermute(array, plane, swap_pairs((nx, ny), (turn, s))))  2.3 us
    ppermute x2, starting transfers between devices, per_device(): lax.ppermute(ends, 'gz', swap_pairs((nz,), (r,)))  2.3 us
    ppermute x2, waiting for transfers between devices, per_device(): lax.ppermute(ends, 'gz', swap_pairs((nz,), (r,)))  1.98 us
  transfers between devices with their start and end apart: 7, of which 2 were waited for; matrix products, arithmetic and copies ran while one was open for 0% of the time, Pallas kernels for 0%

profile of v3, /device:TPU:0, one launch (start us, length us, event | category | flops | bytes accessed | tf_op | source)
XLA Modules:
  0.0 92.9 jit_solution(14345603738777550828)
XLA Ops:
  0.6 0.0 copy-start.2
  0.6 0.0 copy-start
  0.7 1.2 %shard_map.84 = (f32[7,4,16,128]{3,2,1,0:T(8,128)S(1)}, f32[7,4,16,128]{3,2,1,0:T(8,128)S(1)}, f32[7,4,8,128]{3,2,1,0:T(8,128)S(1)}, f32[7,2,8,128]{3,2,1,0:T(8,128)S(1)}, f32[7,2,8,128]{3,2,1,0:T(8,128)S(1)}) custom-call(f32[3,8,16,128]{3,2,1,0:T(8,128)} %sol_any.1, f32[3,8,16,128]{3,2,1,0:T(8,128)} %dire.1, f32[8,16,128]{2,1,0:T(8,128)} %den_any.1, ...), custom_call_target="tpu_custom_call" | custom-call | flops 20000000 | bytes 20000 | tf_op jit(solution)/shard_map/pallas_call | solution.py:48
  1.9 0.5 collective-permute-start
  2.4 0.7 collective-permute-start.1
  3.0 2.6 %collective-permute-start.2 = (f32[7,4,8,128]{3,2,1,0:T(8,128)S(1)}, f32[7,4,8,128]{3,2,1,0:T(8,128)S(1)}, u32[]{:S(2)}, u32[]{:S(2)}) collective-permute-start(f32[7,4,8,128]{3,2,1,0:T(8,128)S(1)} %get-tuple-element.19), channel_id=1, source_target_pairs={{0,4},{4,0},{8,12},{12,8},{16,20},{20,16},{24,28},{28,24},{1,5},{5... | collective-permute-start | bytes 344072 | tf_op jit(solution)/shard_map/ppermute | solution.py:534
  5.6 2.7 %collective-permute-start.3 = (f32[7,2,8,128]{3,2,1,0:T(8,128)S(1)}, f32[7,2,8,128]{3,2,1,0:T(8,128)S(1)}, u32[]{:S(2)}, u32[]{:S(2)}) collective-permute-start(f32[7,2,8,128]{3,2,1,0:T(8,128)S(1)} %get-tuple-element.20), channel_id=1, source_target_pairs={{0,12},{4,8},{8,4},{12,0},{16,28},{20,24},{24,20},{28,16},{1,13},{... | collective-permute-start | bytes 172040 | tf_op jit(solution)/shard_map/ppermute | solution.py:534
  8.3 0.0 copy-start.1
  8.3 0.8 collective-permute-start.4
  9.1 2.3 %collective-permute-done.3.refs_1_ = f32[7,2,8,128]{3,2,1,0:T(8,128)S(1)} collective-permute-done((f32[7,2,8,128]{3,2,1,0:T(8,128)S(1)}, f32[7,2,8,128]{3,2,1,0:T(8,128)S(1)}, u32[]{:S(2)}, u32[]{:S(2)}) %collective-permute-start.3) | collective-permute-done | bytes 57376 | tf_op jit(solution)/shard_map/ppermute | solution.py:534
  11.4 0.0 collective-permute-done.4.refs_2_
  11.4 0.0 collective-permute-done.2.refs_0_
  11.4 0.0 collective-permute-done.got0
  11.4 0.0 collective-permute-done.1.got1
  11.4 0.5 shard_map.85
  11.9 1.6 %collective-permute-start.5 = (f32[7,24,128]{2,1,0:T(8,128)S(1)}, f32[7,24,128]{2,1,0:T(8,128)S(1)}, u32[]{:S(2)}, u32[]{:S(2)}) collective-permute-start(f32[7,24,128]{2,1,0:T(8,128)S(1)} %get-tuple-element.23.ends), channel_id=1, source_target_pairs={{0,1},{1,0},{2,3},{3,2},{4,5},{5,4},{6,7},{7,6},{8,9},{9,8},{10,11... | collective-permute-start | bytes 258056 | tf_op jit(solution)/shard_map/ppermute | solution.py:541
  13.5 0.7 collective-permute-start.6
  14.2 0.3 shard_map.87
  14.5 2.0 %collective-permute-done.5.got0 = f32[7,24,128]{2,1,0:T(8,128)S(1)} collective-permute-done((f32[7,24,128]{2,1,0:T(8,128)S(1)}, f32[7,24,128]{2,1,0:T(8,128)S(1)}, u32[]{:S(2)}, u32[]{:S(2)}) %collective-permute-start.5) | collective-permute-done | bytes 86048 | tf_op jit(solution)/shard_map/ppermute | solution.py:541
  16.4 0.0 collective-permute-done.6.got1
  16.4 0.0 copy-done.2
  16.4 0.0 copy-done
  16.5 2.4 %shard_map.86 = (f32[3,8,16,128]{3,2,1,0:T(8,128)S(1)}, f32[3,8,16,128]{3,2,1,0:T(8,128)S(1)}, f32[8,128]{1,0:T(8,128)S(1)}, f32[7,24,128]{2,1,0:T(8,128)S(1)}) custom-call(f32[7,16,24,128]{3,2,1,0:T(8,128)S(1)} %get-tuple-element.22.ext, f32[7,24,128]{2,1,0:T(8,128)S(1)} %collective-permute-done.5.got0, f32[7,24,128]{2,1,0:T(8,128)S(1)} %collective-permute-done.6.got1, ...), custom_call_target="tpu_custom_call" | custom-call | flops 20000000 | bytes 20000 | tf_op jit(solution)/shard_map/pallas_call | solution.py:48
  18.9 69.0 %all-gather = f32[256,128]{1,0:T(8,128)S(1)} all-gather(f32[8,128]{1,0:T(8,128)S(1)} %get-tuple-element.25), channel_id=2, replica_groups=mesh['gx'=4,'gy'=2,'gz'=4] {'gx','gy','gz'}, dimensions={0}, use_global_device_ids=true | all-gather | bytes 135168 | tf_op jit(solution)/shard_map/all_gather | solution.py:510
  87.9 0.0 copy-done.1
  87.9 5.0 %shard_map.88 = (f32[3,8,16,128]{3,2,1,0:T(8,128)}, f32[3,8,16,128]{3,2,1,0:T(8,128)}, f32[3,8,16,128]{3,2,1,0:T(8,128)}, f32[8,16,128]{2,1,0:T(8,128)}) custom-call(f32[7,16,24,128]{3,2,1,0:T(8,128)S(1)} %get-tuple-element.22.ext, f32[7,24,128]{2,1,0:T(8,128)S(1)} %get-tuple-element.23.ends, f32[7,24,128]{2,1,0:T(8,128)S(1)} %get-tuple-element.24.around, ...), custom_call_target="tpu_custom_call" | custom-call | flops 20000000 | bytes 20000 | tf_op jit(solution)/shard_map/pallas_call | solution.py:48
  (1 shorter events, 0.0 us)
Async XLA Ops:
  0.6 15.8 %copy-start.2 = (s32[8,16,128]{2,1,0:T(8,128)S(1)}, s32[8,16,128]{2,1,0:T(8,128)}, u32[]{:S(2)}) copy-start(s32[8,16,128]{2,1,0:T(8,128)} %lab.1) | copy-start | bytes 196612
  0.6 15.8 %copy-start = (f32[3,8,16,128]{3,2,1,0:T(8,128)S(1)}, f32[3,8,16,128]{3,2,1,0:T(8,128)}, u32[]{:S(2)}) copy-start(f32[3,8,16,128]{3,2,1,0:T(8,128)} %res.3) | copy-start | bytes 589828
  1.9 9.6 %collective-permute-start = (f32[7,4,16,128]{3,2,1,0:T(8,128)S(1)}, f32[7,4,16,128]{3,2,1,0:T(8,128)S(1)}, u32[]{:S(2)}, u32[]{:S(2)}) collective-permute-start(f32[7,4,16,128]{3,2,1,0:T(8,128)S(1)} %get-tuple-element.17.half0), channel_id=1, source_target_pairs={{0,8},{4,12},{8,0},{12,4},{16,24},{20,28},{24,16},{28,20},{1,9},{5... | collective-permute-start | bytes 688136 | tf_op jit(solution)/shard_map/ppermute | solution.py:530
  2.4 9.0 %collective-permute-start.1 = (f32[7,4,16,128]{3,2,1,0:T(8,128)S(1)}, f32[7,4,16,128]{3,2,1,0:T(8,128)S(1)}, u32[]{:S(2)}, u32[]{:S(2)}) collective-permute-start(f32[7,4,16,128]{3,2,1,0:T(8,128)S(1)} %get-tuple-element.18.half1), channel_id=1, source_target_pairs={{0,0},{4,4},{8,16},{12,20},{16,8},{20,12},{24,24},{28,28},{1,1},{5... | collective-permute-start | bytes 688136 | tf_op jit(solution)/shard_map/ppermute | solution.py:530
  3.0 8.4 %collective-permute-start.2 = (f32[7,4,8,128]{3,2,1,0:T(8,128)S(1)}, f32[7,4,8,128]{3,2,1,0:T(8,128)S(1)}, u32[]{:S(2)}, u32[]{:S(2)}) collective-permute-start(f32[7,4,8,128]{3,2,1,0:T(8,128)S(1)} %get-tuple-element.19), channel_id=1, source_target_pairs={{0,4},{4,0},{8,12},{12,8},{16,20},{20,16},{24,28},{28,24},{1,5},{5... | collective-permute-start | bytes 344072 | tf_op jit(solution)/shard_map/ppermute | solution.py:534
  5.6 5.8 %collective-permute-start.3 = (f32[7,2,8,128]{3,2,1,0:T(8,128)S(1)}, f32[7,2,8,128]{3,2,1,0:T(8,128)S(1)}, u32[]{:S(2)}, u32[]{:S(2)}) collective-permute-start(f32[7,2,8,128]{3,2,1,0:T(8,128)S(1)} %get-tuple-element.20), channel_id=1, source_target_pairs={{0,12},{4,8},{8,4},{12,0},{16,28},{20,24},{24,20},{28,16},{1,13},{... | collective-permute-start | bytes 172040 | tf_op jit(solution)/shard_map/ppermute | solution.py:534
  8.3 79.6 %copy-start.1 = (f32[3,8,16,128]{3,2,1,0:T(8,128)S(1)}, f32[3,8,16,128]{3,2,1,0:T(8,128)}, u32[]{:S(2)}) copy-start(f32[3,8,16,128]{3,2,1,0:T(8,128)} %dire.1) | copy-start | bytes 589828
  8.3 3.1 %collective-permute-start.4 = (f32[7,2,8,128]{3,2,1,0:T(8,128)S(1)}, f32[7,2,8,128]{3,2,1,0:T(8,128)S(1)}, u32[]{:S(2)}, u32[]{:S(2)}) collective-permute-start(f32[7,2,8,128]{3,2,1,0:T(8,128)S(1)} %get-tuple-element.21), channel_id=1, source_target_pairs={{0,0},{4,4},{8,20},{12,16},{16,12},{20,8},{24,24},{28,28},{1,1},{5... | collective-permute-start | bytes 172040 | tf_op jit(solution)/shard_map/ppermute | solution.py:534
  11.9 4.6 %collective-permute-start.5 = (f32[7,24,128]{2,1,0:T(8,128)S(1)}, f32[7,24,128]{2,1,0:T(8,128)S(1)}, u32[]{:S(2)}, u32[]{:S(2)}) collective-permute-start(f32[7,24,128]{2,1,0:T(8,128)S(1)} %get-tuple-element.23.ends), channel_id=1, source_target_pairs={{0,1},{1,0},{2,3},{3,2},{4,5},{5,4},{6,7},{7,6},{8,9},{9,8},{10,11... | collective-permute-start | bytes 258056 | tf_op jit(solution)/shard_map/ppermute | solution.py:541
  13.5 2.9 %collective-permute-start.6 = (f32[7,24,128]{2,1,0:T(8,128)S(1)}, f32[7,24,128]{2,1,0:T(8,128)S(1)}, u32[]{:S(2)}, u32[]{:S(2)}) collective-permute-start(f32[7,24,128]{2,1,0:T(8,128)S(1)} %get-tuple-element.23.ends), channel_id=1, source_target_pairs={{0,0},{1,2},{2,1},{3,3},{4,4},{5,6},{6,5},{7,7},{8,8},{9,10},{10,9... | collective-permute-start | bytes 258056 | tf_op jit(solution)/shard_map/ppermute | solution.py:541

commit v4 on v3

--- a/solution.py
+++ b/solution.py
@@ -144,15 +144,11 @@
                 if which is not None:
                     own = own * x_ok[which]
                 low, high = strip(which, f, t)
-                a, b = roll(own[0:8], 4, 0), roll(own[8:16], 4, 0)
                 if X % 2 == 0:
+                    low = roll(low, 4, 0)
+                else:
                     high = roll(high, 4, 0)
-                else:
-                    low = roll(low, 4, 0)
-                plane = jnp.concatenate(
-                    [jnp.where(sub < 4, low, a), jnp.where(sub < 4, a, b), jnp.where(sub < 4, b, high)],
-                    axis=0,
-                )
+                plane = jnp.concatenate([own, jnp.where(sub < 4, high, low)], axis=0)
                 ext[f, X] = plane
                 turned = roll(plane, 8 * X + 4, 1)
                 packed = turned if X == 0 else jnp.where(lane >= 8 * X, turned, packed)
@@ -172,7 +168,7 @@
     row, lane = rows_of(shape), lanes_of(shape)
     nx, ny, nz = counts
     base_x = lax.axis_index("gx") * 8 - HALO
-    base_y = lax.axis_index("gy") * 16 - HALO
+    base_y = lax.axis_index("gy") * 16
     base_z = lax.axis_index("gz") * 128
 
     def folded(place, limit):
@@ -181,7 +177,7 @@
 
         return [inside(place)] + [inside(place - k) + inside(place + k) for k in range(1, RAD + 1)]
 
-    along_y = folded(row + base_y, ny * 16)
+    along_y = folded(jnp.where(row < 16 + HALO, row, row - 24) + base_y, ny * 16)
 
     def partial(along_z):
         table = []
@@ -226,24 +222,25 @@
     keep = jnp.where(lows, (iz > 0).astype(f32), (iz < nz - 1).astype(f32))
     for f in range(7):
         around[f] = jnp.where(from_zero, got0[f], got1[f]) * keep
-    for g, f in enumerate(fields):
-        halo = around[f]
-        for n in range(10):
-            X = n + 3
+    parts = [jnp.zeros((16, 128), f32) for _ in range(4)]
+    for plane_at in range(10):
+        X = plane_at + 3
+        for g, f in enumerate(fields):
             value = ext[f, X]
-            near = roll(halo, 124 - 8 * X, 1)
+            near = roll(around[f], 124 - 8 * X, 1)
             if g == 3:
-                value = stiff_floor + (1.0 - stiff_floor) * value * value * value
-                value = jnp.where(ext[f, X] > 0, value, 0.0)
-                near_stiff = stiff_floor + (1.0 - stiff_floor) * near * near * near
-                near = jnp.where(near > 0, near_stiff, 0.0)
+                stiff = stiff_floor + (1.0 - stiff_floor) * value * value * value
+                value = jnp.where(value > 0, stiff, 0.0)
+                stiff = stiff_floor + (1.0 - stiff_floor) * near * near * near
+                near = jnp.where(near > 0, stiff, 0.0)
             up = roll(jnp.where(lane == 0, near, value), -1, 1)
             down = roll(jnp.where(lane == 127, near, value), 1, 1)
             for z, plane in enumerate((down, value, up)):
                 for y in range(3):
-                    shifts[g, y, z, n] = roll(plane, -(HALO - 1 + y), 0)[0:16]
-    parts = [jnp.zeros((16, 128), f32) for _ in range(4)]
-    for x in range(8):
+                    shifts[g, y, z, plane_at] = roll(plane, 1 - y, 0)[0:16]
+        x = plane_at - 2
+        if x < 0:
+            continue
         n = x + 1
         mid = [shifts[g, 1, 1, n] for g in range(4)]
         classes = {1: [None] * 3, 2: [None] * 3, 3: [None] * 3}
@@ -336,6 +333,7 @@
 pairs += [((a, 0, 1), 0, 0, 1, 1) for a in (-1, 0, 1)]
 pairs += [((a, 1, 1), 0, 0, 3, 3) for a in (-1, 0, 1)]
 pairs += [((a, -1, 1), 2, 2, 1, 1) for a in (-1, 0, 1)]
+distances = sorted({a * a + b * b for a in range(RAD + 1) for b in range(RAD + 1) if cone(a, b, 0) > 0})
 energy_scale = -penalty * (1.0 - stiff_floor) * 0.5
 
 
@@ -345,7 +343,7 @@
 
 def finish_step(
     ext, ends, around, total, image, inverse, res, dire, hinv, hside,
-    new_sol_any, new_res_any, new_dir_any, sens_any, us, scaled, new_sol, new_res, new_dir, sens, sems,
+    new_sol_any, new_res_any, new_dir_any, sens_any, us, lines, new_sol, new_res, new_dir, sens, sems,
 ):
     lane = lanes_of((24, 128))
     lows = lane % 8 < 4
@@ -375,19 +373,6 @@
         halos.append(halo_u)
         lefts.append(jnp.where(lows, halo_u, own_u))
         rights.append(jnp.where(lows, own_u, halo_u))
-    for X in range(16):
-        for c in range(3):
-            u = ext[3 + c, X] + alpha * ext[c, X]
-            if 4 <= X < 12:
-                new_sol[c, X - 4] = roll(u, -HALO, 0)[0:16]
-            near = roll(halos[c], 124 - 8 * X, 1)
-            up = roll(jnp.where(lane == 0, near, u), -1, 1)
-            us[0, c, X] = u
-            us[1, c, X] = up
-            us[2, c, X] = roll(u, -1, 0)
-            us[3, c, X] = roll(up, -1, 0)
-    copies[2].start()
-
     sides, side_low = [], None
     den_left = jnp.where(lows, around[6], ends[6])
     den_right = jnp.where(lows, ends[6], around[6])
@@ -417,8 +402,23 @@
         sides.append(energy_scale * (den * den) * energy * hside[s])
     ends_scaled = jnp.where(lows, sides[0], sides[1])
 
+    def iterate(X):
+        for c in range(3):
+            u = ext[3 + c, X] + alpha * ext[c, X]
+            if 4 <= X < 12:
+                new_sol[c, X - 4] = u[0:16]
+            near = roll(halos[c], 124 - 8 * X, 1)
+            up = roll(jnp.where(lane == 0, near, u), -1, 1)
+            us[0, c, X] = u
+            us[1, c, X] = up
+            us[2, c, X] = roll(u, -1, 0)
+            us[3, c, X] = roll(up, -1, 0)
+        if X == 11:
+            copies[2].start()
+
     acc = [[None] * 4 for _ in range(16)]
-    for X in range(16):
+
+    def pair_up(X):
         for o, field0, frame0, field1, frame1 in pairs:
             to = X + o[0]
             if not 0 <= to < 16 or not (1 <= X < 15 or 1 <= to < 15):
@@ -428,47 +428,48 @@
                 acc[X][frame0] = plus(acc[X][frame0], g)
             if 1 <= to < 15:
                 acc[to][frame1] = plus(acc[to][frame1], g)
-        done = X - 1
-        if done >= 1:
-            frames = acc[done]
-            up = frames[1] + roll(frames[3], 1, 0)
-            below = roll(side_low, 127 - (8 * done + 3), 1)
-            up = roll(jnp.where(lane == 127, below, up), 1, 1)
-            den = ext[6, done]
-            energy = frames[0] + roll(frames[2], 1, 0) + up
-            scaled[done] = energy_scale * (den * den) * energy * hinv[done]
-
-    rows = [[None] * (RAD + 1) for _ in range(8)]
-    for X in range(1, 15):
-        s = scaled[X]
+
+    def filter_lines(X):
+        frames = acc[X]
+        up = frames[1] + roll(frames[3], 1, 0)
+        below = roll(side_low, 127 - (8 * X + 3), 1)
+        up = roll(jnp.where(lane == 127, below, up), 1, 1)
+        den = ext[6, X]
+        energy = frames[0] + roll(frames[2], 1, 0) + up
+        s = energy_scale * (den * den) * energy * hinv[X]
         near = roll(ends_scaled, 124 - 8 * X, 1)
         fold = [s]
         for k in range(1, RAD + 1):
             above = roll(jnp.where(lane < k, near, s), -k, 1)
             under = roll(jnp.where(lane >= 128 - k, near, s), k, 1)
             fold.append(above + under)
-        made = {}
+        for i, d in enumerate(distances):
+            line = None
+            for k in range(RAD + 1):
+                w = max(0.0, RAD + 0.5 - math.sqrt(d + k * k))
+                if w > 0:
+                    line = plus(line, w * fold[k])
+            lines[X, i] = line
+
+    def filter_rows(x):
+        value = None
         for b in range(RAD + 1):
+            row = None
             for a in range(-RAD, RAD + 1):
-                x = X - a - HALO
-                if not 0 <= x < 8 or cone(a, b, 0) <= 0:
-                    continue
-                key = a * a + b * b
-                if key not in made:
-                    line = None
-                    for k in range(RAD + 1):
-                        w = cone(a, b, k)
-                        if w > 0:
-                            line = w * fold[k] if line is None else line + w * fold[k]
-                    made[key] = line
-                old = rows[x][b]
-                rows[x][b] = made[key] if old is None else old + made[key]
-        x = X - 2 * RAD - 1
-        if x >= 0:
-            value = rows[x][0]
-            for b in range(1, RAD + 1):
-                value = value + roll(rows[x][b], b, 0) + roll(rows[x][b], -b, 0)
-            sens[x] = roll(value, -HALO, 0)[0:16]
+                if cone(a, b, 0) > 0:
+                    row = plus(row, lines[x + HALO + a, distances.index(a * a + b * b)])
+            value = row if b == 0 else value + roll(row, b, 0) + roll(row, -b, 0)
+        sens[x] = value[0:16]
+
+    for X in range(16 + 1):
+        if X < 16:
+            iterate(X)
+        if X >= 1:
+            pair_up(X - 1)
+        if X >= 3:
+            filter_lines(X - 2)
+        if X - 2 - 2 * RAD - 1 >= 0:
+            filter_rows(X - 2 - 2 * RAD - 1)
     copies[3].start()
     for copy in copies:
         copy.wait()
@@ -507,7 +508,9 @@
 
 
 def total_over(value, mesh_shape):
-    return jnp.sum(lax.all_gather(value, AXES), axis=0)
+    count = math.prod(mesh_shape[a] for a in AXES)
+    copies = jnp.broadcast_to(value, (count,) + value.shape)
+    return jnp.sum(lax.all_to_all(copies, AXES, 0, 0), axis=0)
 
 
 def per_device(mesh_shape, solution, residual, direction, density, labels):
@@ -552,7 +555,7 @@
             [field, field, field, flat],
             ext, ends, around, total, image, inverse, residual, direction, hinv, hside,
             scratch=[
-                pltpu.VMEM((4, 3, 16, 24, 128), f32), pltpu.VMEM((16, 24, 128), f32),
+                pltpu.VMEM((4, 3, 16, 24, 128), f32), pltpu.VMEM((16, len(distances), 24, 128), f32),
                 pltpu.VMEM(field, f32), pltpu.VMEM(field, f32), pltpu.VMEM(field, f32),
                 pltpu.VMEM(flat, f32), pltpu.SemaphoreType.DMA((4,)),
             ],

time: 94.3 us -> 42.4 us (0.45); the launches traced: 92.9 us -> 42.2 us
  blocking collectives: 69 us -> 0 us
  starting transfers between devices: 9.54 us -> 19.2 us
  waiting for transfers between devices: 4.28 us -> 12.2 us
    all_gather x1 -> x0, blocking collectives: 69 us -> none  [total_over(): return jnp.sum(lax.all_gather(value, AXES), axis=0)]
    all_to_all x0 -> x1, starting transfers between devices: none -> 9.81 us  [total_over(): return jnp.sum(lax.all_to_all(copies, AXES, 0, 0), axis=0)]
    all_to_all x0 -> x1, waiting for transfers between devices: none -> 7.47 us  [total_over(): return jnp.sum(lax.all_to_all(copies, AXES, 0, 0), axis=0)]
  transfers between devices with their start and end apart: 7 -> 8, of which waited for: 2 -> 3; matrix products, arithmetic and copies ran while one was open for 0% -> 0% of each run, Pallas kernels for 0% -> 1%
where the time goes in v4:
time: 42.4 us; the launch traced here: 42.2 us
  starting transfers between devices  19.2 us (45%)
  waiting for transfers between devices  12.2 us (29%)
  Pallas kernels  9.34 us (22%)
  between operations  0.74 us (2%)
  local copies, waits for them, and re-layouts  0.68 us (2%)
    all_to_all x1, starting transfers between devices, total_over(): return jnp.sum(lax.all_to_all(copies, AXES, 0, 0), axis=0)  9.81 us
    pallas_call x5, Pallas kernels, call(): pl.pallas_call(body, out_shape=[jax.ShapeDtypeStruct(shape, f32) for shap...  9.34 us
    all_to_all x1, waiting for transfers between devices, total_over(): return jnp.sum(lax.all_to_all(copies, AXES, 0, 0), axis=0)  7.47 us
    ppermute x3, starting transfers between devices, per_device(): strips.append(lax.ppermute(array, plane, swap_pairs((nx, ny), (turn, s))))  5.93 us
    ppermute x3, waiting for transfers between devices, per_device(): strips.append(lax.ppermute(array, plane, swap_pairs((nx, ny), (turn, s))))  2.43 us
    ppermute x2, starting transfers between devices, per_device(): lax.ppermute(ends, 'gz', swap_pairs((nz,), (r,)))  2.3 us
    ppermute x2, waiting for transfers between devices, per_device(): lax.ppermute(ends, 'gz', swap_pairs((nz,), (r,)))  2.25 us
    ppermute x2, starting transfers between devices, per_device(): lax.ppermute(halves[r], plane, swap_pairs((nx, ny), (r, None)))  1.18 us
  transfers between devices with their start and end apart: 8, of which 3 were waited for; matrix products, arithmetic and copies ran while one was open for 0% of the time, Pallas kernels for 1%

profile of v4, /device:TPU:0, one launch (start us, length us, event | category | flops | bytes accessed | tf_op | source)
XLA Modules:
  0.0 42.2 jit_solution(13149559025701105361)
XLA Ops:
  0.6 0.0 copy-start.2
  0.6 0.0 copy-start
  0.7 1.2 %shard_map.84 = (f32[7,4,16,128]{3,2,1,0:T(8,128)S(1)}, f32[7,4,16,128]{3,2,1,0:T(8,128)S(1)}, f32[7,4,8,128]{3,2,1,0:T(8,128)S(1)}, f32[7,2,8,128]{3,2,1,0:T(8,128)S(1)}, f32[7,2,8,128]{3,2,1,0:T(8,128)S(1)}) custom-call(f32[3,8,16,128]{3,2,1,0:T(8,128)} %sol_any.1, f32[3,8,16,128]{3,2,1,0:T(8,128)} %dire.1, f32[8,16,128]{2,1,0:T(8,128)} %den_any.1, ...), custom_call_target="tpu_custom_call" | custom-call | flops 20000000 | bytes 20000 | tf_op jit(solution)/shard_map/pallas_call | solution.py:48
  1.9 0.5 %collective-permute-start = (f32[7,4,16,128]{3,2,1,0:T(8,128)S(1)}, f32[7,4,16,128]{3,2,1,0:T(8,128)S(1)}, u32[]{:S(2)}, u32[]{:S(2)}) collective-permute-start(f32[7,4,16,128]{3,2,1,0:T(8,128)S(1)} %get-tuple-element.17.half0), channel_id=1, source_target_pairs={{0,8},{4,12},{8,0},{12,4},{16,24},{20,28},{24,16},{28,20},{1,9},{5... | collective-permute-start | bytes 688136 | tf_op jit(solution)/shard_map/ppermute | solution.py:533
  2.4 0.7 %collective-permute-start.1 = (f32[7,4,16,128]{3,2,1,0:T(8,128)S(1)}, f32[7,4,16,128]{3,2,1,0:T(8,128)S(1)}, u32[]{:S(2)}, u32[]{:S(2)}) collective-permute-start(f32[7,4,16,128]{3,2,1,0:T(8,128)S(1)} %get-tuple-element.18.half1), channel_id=1, source_target_pairs={{0,0},{4,4},{8,16},{12,20},{16,8},{20,12},{24,24},{28,28},{1,1},{5... | collective-permute-start | bytes 688136 | tf_op jit(solution)/shard_map/ppermute | solution.py:533
  3.0 2.6 %collective-permute-start.2 = (f32[7,4,8,128]{3,2,1,0:T(8,128)S(1)}, f32[7,4,8,128]{3,2,1,0:T(8,128)S(1)}, u32[]{:S(2)}, u32[]{:S(2)}) collective-permute-start(f32[7,4,8,128]{3,2,1,0:T(8,128)S(1)} %get-tuple-element.19), channel_id=1, source_target_pairs={{0,4},{4,0},{8,12},{12,8},{16,20},{20,16},{24,28},{28,24},{1,5},{5... | collective-permute-start | bytes 344072 | tf_op jit(solution)/shard_map/ppermute | solution.py:537
  5.6 2.7 %collective-permute-start.3 = (f32[7,2,8,128]{3,2,1,0:T(8,128)S(1)}, f32[7,2,8,128]{3,2,1,0:T(8,128)S(1)}, u32[]{:S(2)}, u32[]{:S(2)}) collective-permute-start(f32[7,2,8,128]{3,2,1,0:T(8,128)S(1)} %get-tuple-element.20), channel_id=1, source_target_pairs={{0,12},{4,8},{8,4},{12,0},{16,28},{20,24},{24,20},{28,16},{1,13},{... | collective-permute-start | bytes 172040 | tf_op jit(solution)/shard_map/ppermute | solution.py:537
  8.3 0.7 %collective-permute-start.4 = (f32[7,2,8,128]{3,2,1,0:T(8,128)S(1)}, f32[7,2,8,128]{3,2,1,0:T(8,128)S(1)}, u32[]{:S(2)}, u32[]{:S(2)}) collective-permute-start(f32[7,2,8,128]{3,2,1,0:T(8,128)S(1)} %get-tuple-element.21), channel_id=1, source_target_pairs={{0,0},{4,4},{8,20},{12,16},{16,12},{20,8},{24,24},{28,28},{1,1},{5... | collective-permute-start | bytes 172040 | tf_op jit(solution)/shard_map/ppermute | solution.py:537
  9.0 2.4 %collective-permute-done.3.refs_1_ = f32[7,2,8,128]{3,2,1,0:T(8,128)S(1)} collective-permute-done((f32[7,2,8,128]{3,2,1,0:T(8,128)S(1)}, f32[7,2,8,128]{3,2,1,0:T(8,128)S(1)}, u32[]{:S(2)}, u32[]{:S(2)}) %collective-permute-start.3) | collective-permute-done | bytes 57376 | tf_op jit(solution)/shard_map/ppermute | solution.py:537
  11.4 0.0 collective-permute-done.4.refs_2_
  11.4 0.0 collective-permute-done.2.refs_0_
  11.4 0.0 collective-permute-done.got0
  11.4 0.0 collective-permute-done.1.got1
  11.4 0.5 %shard_map.85 = (f32[7,16,24,128]{3,2,1,0:T(8,128)S(1)}, f32[7,24,128]{2,1,0:T(8,128)S(1)}) custom-call(f32[7,4,16,128]{3,2,1,0:T(8,128)S(1)} %get-tuple-element.17.half0, f32[7,4,16,128]{3,2,1,0:T(8,128)S(1)} %get-tuple-element.18.half1, f32[7,4,16,128]{3,2,1,0:T(8,128)S(1)} %collective-permute-done.got0, ...), custom_call_target="tpu_custom_call" | custom-call | flops 20000000 | bytes 20000 | tf_op jit(solution)/shard_map/pallas_call | solution.py:48
  11.9 0.0 copy-start.1
  11.9 1.6 %collective-permute-start.5 = (f32[7,24,128]{2,1,0:T(8,128)S(1)}, f32[7,24,128]{2,1,0:T(8,128)S(1)}, u32[]{:S(2)}, u32[]{:S(2)}) collective-permute-start(f32[7,24,128]{2,1,0:T(8,128)S(1)} %get-tuple-element.23.ends), channel_id=1, source_target_pairs={{0,1},{1,0},{2,3},{3,2},{4,5},{5,4},{6,7},{7,6},{8,9},{9,8},{10,11... | collective-permute-start | bytes 258056 | tf_op jit(solution)/shard_map/ppermute | solution.py:544
  13.5 0.7 %collective-permute-start.6 = (f32[7,24,128]{2,1,0:T(8,128)S(1)}, f32[7,24,128]{2,1,0:T(8,128)S(1)}, u32[]{:S(2)}, u32[]{:S(2)}) collective-permute-start(f32[7,24,128]{2,1,0:T(8,128)S(1)} %get-tuple-element.23.ends), channel_id=1, source_target_pairs={{0,0},{1,2},{2,1},{3,3},{4,4},{5,6},{6,5},{7,7},{8,8},{9,10},{10,9... | collective-permute-start | bytes 258056 | tf_op jit(solution)/shard_map/ppermute | solution.py:544
  14.2 2.2 %collective-permute-done.5.got0 = f32[7,24,128]{2,1,0:T(8,128)S(1)} collective-permute-done((f32[7,24,128]{2,1,0:T(8,128)S(1)}, f32[7,24,128]{2,1,0:T(8,128)S(1)}, u32[]{:S(2)}, u32[]{:S(2)}) %collective-permute-start.5) | collective-permute-done | bytes 86048 | tf_op jit(solution)/shard_map/ppermute | solution.py:544
  16.5 0.0 collective-permute-done.6.got1
  16.5 0.0 copy-done.2
  16.5 0.0 copy-done
  16.5 2.3 %shard_map.86 = (f32[3,8,16,128]{3,2,1,0:T(8,128)S(1)}, f32[3,8,16,128]{3,2,1,0:T(8,128)S(1)}, f32[8,128]{1,0:T(8,128)S(1)}, f32[7,24,128]{2,1,0:T(8,128)S(1)}) custom-call(f32[7,16,24,128]{3,2,1,0:T(8,128)S(1)} %get-tuple-element.22.ext, f32[7,24,128]{2,1,0:T(8,128)S(1)} %collective-permute-done.5.got0, f32[7,24,128]{2,1,0:T(8,128)S(1)} %collective-permute-done.6.got1, ...), custom_call_target="tpu_custom_call" | custom-call | flops 20000000 | bytes 20000 | tf_op jit(solution)/shard_map/pallas_call | solution.py:48
  18.7 0.7 %broadcast_in_dim.3 = f32[32,8,128]{2,1,0:T(8,128)} broadcast(f32[8,128]{1,0:T(8,128)S(1)} %get-tuple-element.25), dimensions={1,2} | broadcast | bytes 135168 | tf_op jit(solution)/shard_map/broadcast_in_dim | solution.py:512
  19.4 9.8 %all-to-all-start = ((f32[32,8,128]{2,1,0:T(8,128)}), f32[32,8,128]{2,1,0:T(8,128)S(1)}, u32[]{:S(2)}, u32[]{:S(2)}) async-start(f32[32,8,128]{2,1,0:T(8,128)} %broadcast_in_dim.3), calls=%async_computation | async-start | bytes 262144 | tf_op jit(solution)/shard_map/all_to_all | solution.py:513
  29.2 0.3 shard_map.87
  29.5 7.5 %all-to-all-done = f32[32,8,128]{2,1,0:T(8,128)S(1)} async-done(((f32[32,8,128]{2,1,0:T(8,128)}), f32[32,8,128]{2,1,0:T(8,128)S(1)}, u32[]{:S(2)}, u32[]{:S(2)}) %all-to-all-start) | async-done | bytes 131104 | tf_op jit(solution)/shard_map/all_to_all | solution.py:513
  37.0 0.0 copy-done.1
  37.0 5.1 %shard_map.88 = (f32[3,8,16,128]{3,2,1,0:T(8,128)}, f32[3,8,16,128]{3,2,1,0:T(8,128)}, f32[3,8,16,128]{3,2,1,0:T(8,128)}, f32[8,16,128]{2,1,0:T(8,128)}) custom-call(f32[7,16,24,128]{3,2,1,0:T(8,128)S(1)} %get-tuple-element.22.ext, f32[7,24,128]{2,1,0:T(8,128)S(1)} %get-tuple-element.23.ends, f32[7,24,128]{2,1,0:T(8,128)S(1)} %get-tuple-element.24.around, ...), custom_call_target="tpu_custom_call" | custom-call | flops 20000000 | bytes 20000 | tf_op jit(solution)/shard_map/pallas_call | solution.py:48
  (1 shorter events, 0.0 us)
Async XLA Ops:
  0.6 15.8 %copy-start.2 = (s32[8,16,128]{2,1,0:T(8,128)S(1)}, s32[8,16,128]{2,1,0:T(8,128)}, u32[]{:S(2)}) copy-start(s32[8,16,128]{2,1,0:T(8,128)} %lab.1) | copy-start | bytes 196612
  0.6 15.8 %copy-start = (f32[3,8,16,128]{3,2,1,0:T(8,128)S(1)}, f32[3,8,16,128]{3,2,1,0:T(8,128)}, u32[]{:S(2)}) copy-start(f32[3,8,16,128]{3,2,1,0:T(8,128)} %res.3) | copy-start | bytes 589828
  1.9 9.6 %collective-permute-start = (f32[7,4,16,128]{3,2,1,0:T(8,128)S(1)}, f32[7,4,16,128]{3,2,1,0:T(8,128)S(1)}, u32[]{:S(2)}, u32[]{:S(2)}) collective-permute-start(f32[7,4,16,128]{3,2,1,0:T(8,128)S(1)} %get-tuple-element.17.half0), channel_id=1, source_target_pairs={{0,8},{4,12},{8,0},{12,4},{16,24},{20,28},{24,16},{28,20},{1,9},{5... | collective-permute-start | bytes 688136 | tf_op jit(solution)/shard_map/ppermute | solution.py:533
  2.4 9.0 %collective-permute-start.1 = (f32[7,4,16,128]{3,2,1,0:T(8,128)S(1)}, f32[7,4,16,128]{3,2,1,0:T(8,128)S(1)}, u32[]{:S(2)}, u32[]{:S(2)}) collective-permute-start(f32[7,4,16,128]{3,2,1,0:T(8,128)S(1)} %get-tuple-element.18.half1), channel_id=1, source_target_pairs={{0,0},{4,4},{8,16},{12,20},{16,8},{20,12},{24,24},{28,28},{1,1},{5... | collective-permute-start | bytes 688136 | tf_op jit(solution)/shard_map/ppermute | solution.py:533
  3.0 8.4 %collective-permute-start.2 = (f32[7,4,8,128]{3,2,1,0:T(8,128)S(1)}, f32[7,4,8,128]{3,2,1,0:T(8,128)S(1)}, u32[]{:S(2)}, u32[]{:S(2)}) collective-permute-start(f32[7,4,8,128]{3,2,1,0:T(8,128)S(1)} %get-tuple-element.19), channel_id=1, source_target_pairs={{0,4},{4,0},{8,12},{12,8},{16,20},{20,16},{24,28},{28,24},{1,5},{5... | collective-permute-start | bytes 344072 | tf_op jit(solution)/shard_map/ppermute | solution.py:537
  5.6 5.8 %collective-permute-start.3 = (f32[7,2,8,128]{3,2,1,0:T(8,128)S(1)}, f32[7,2,8,128]{3,2,1,0:T(8,128)S(1)}, u32[]{:S(2)}, u32[]{:S(2)}) collective-permute-start(f32[7,2,8,128]{3,2,1,0:T(8,128)S(1)} %get-tuple-element.20), channel_id=1, source_target_pairs={{0,12},{4,8},{8,4},{12,0},{16,28},{20,24},{24,20},{28,16},{1,13},{... | collective-permute-start | bytes 172040 | tf_op jit(solution)/shard_map/ppermute | solution.py:537
  8.3 3.1 %collective-permute-start.4 = (f32[7,2,8,128]{3,2,1,0:T(8,128)S(1)}, f32[7,2,8,128]{3,2,1,0:T(8,128)S(1)}, u32[]{:S(2)}, u32[]{:S(2)}) collective-permute-start(f32[7,2,8,128]{3,2,1,0:T(8,128)S(1)} %get-tuple-element.21), channel_id=1, source_target_pairs={{0,0},{4,4},{8,20},{12,16},{16,12},{20,8},{24,24},{28,28},{1,1},{5... | collective-permute-start | bytes 172040 | tf_op jit(solution)/shard_map/ppermute | solution.py:537
  11.9 25.1 %copy-start.1 = (f32[3,8,16,128]{3,2,1,0:T(8,128)S(1)}, f32[3,8,16,128]{3,2,1,0:T(8,128)}, u32[]{:S(2)}) copy-start(f32[3,8,16,128]{3,2,1,0:T(8,128)} %dire.1) | copy-start | bytes 589828
  11.9 4.6 %collective-permute-start.5 = (f32[7,24,128]{2,1,0:T(8,128)S(1)}, f32[7,24,128]{2,1,0:T(8,128)S(1)}, u32[]{:S(2)}, u32[]{:S(2)}) collective-permute-start(f32[7,24,128]{2,1,0:T(8,128)S(1)} %get-tuple-element.23.ends), channel_id=1, source_target_pairs={{0,1},{1,0},{2,3},{3,2},{4,5},{5,4},{6,7},{7,6},{8,9},{9,8},{10,11... | collective-permute-start | bytes 258056 | tf_op jit(solution)/shard_map/ppermute | solution.py:544
  13.5 2.9 %collective-permute-start.6 = (f32[7,24,128]{2,1,0:T(8,128)S(1)}, f32[7,24,128]{2,1,0:T(8,128)S(1)}, u32[]{:S(2)}, u32[]{:S(2)}) collective-permute-start(f32[7,24,128]{2,1,0:T(8,128)S(1)} %get-tuple-element.23.ends), channel_id=1, source_target_pairs={{0,0},{1,2},{2,1},{3,3},{4,4},{5,6},{6,5},{7,7},{8,8},{9,10},{10,9... | collective-permute-start | bytes 258056 | tf_op jit(solution)/shard_map/ppermute | solution.py:544
  19.4 17.6 %all-to-all-start = ((f32[32,8,128]{2,1,0:T(8,128)}), f32[32,8,128]{2,1,0:T(8,128)S(1)}, u32[]{:S(2)}, u32[]{:S(2)}) async-start(f32[32,8,128]{2,1,0:T(8,128)} %broadcast_in_dim.3), calls=%async_computation | async-start | bytes 262144 | tf_op jit(solution)/shard_map/all_to_all | solution.py:513

commit v5 on v4

--- a/solution.py
+++ b/solution.py
@@ -305,12 +305,12 @@
             parts[1] = parts[1] + mid[c] * total
             parts[2] = parts[2] + r * scaled
             parts[3] = parts[3] + total * scaled
-    sub = rows_of((8, 128))
-    out = jnp.zeros((8, 128), f32)
+    row = jnp.zeros((1, 128), f32)
     for k in range(4):
-        part = parts[k][0:8] + parts[k][8:16]
-        out = jnp.where(sub == k, jnp.sum(part, axis=0, keepdims=True), out)
-    sums[...] = out
+        part = jnp.sum(parts[k], axis=0, keepdims=True)
+        part = jnp.sum(part, axis=1, keepdims=True)
+        row = jnp.where(lanes_of((1, 128)) == k, part, row)
+    sums[...] = jnp.broadcast_to(row[None], sums.shape)
 
 
 def quadratic(d, o):
@@ -333,7 +333,6 @@
 pairs += [((a, 0, 1), 0, 0, 1, 1) for a in (-1, 0, 1)]
 pairs += [((a, 1, 1), 0, 0, 3, 3) for a in (-1, 0, 1)]
 pairs += [((a, -1, 1), 2, 2, 1, 1) for a in (-1, 0, 1)]
-distances = sorted({a * a + b * b for a in range(RAD + 1) for b in range(RAD + 1) if cone(a, b, 0) > 0})
 energy_scale = -penalty * (1.0 - stiff_floor) * 0.5
 
 
@@ -353,8 +352,8 @@
             ((new_res, new_res_any), (new_dir, new_dir_any), (new_sol, new_sol_any), (sens, sens_any))
         )
     ]
-    tot = jnp.sum(total[...], axis=1, keepdims=True)
-    rz, pq, s2, s3 = tot[0:1], tot[1:2], tot[2:3], tot[3:4]
+    tot = jnp.sum(total[...], axis=0)
+    rz, pq, s2, s3 = (tot[:, k : k + 1] for k in range(4))
     alpha = rz / pq
     beta = (rz + alpha * (alpha * s3 - 2.0 * s2)) / rz
 
@@ -443,21 +442,25 @@
             above = roll(jnp.where(lane < k, near, s), -k, 1)
             under = roll(jnp.where(lane >= 128 - k, near, s), k, 1)
             fold.append(above + under)
-        for i, d in enumerate(distances):
-            line = None
+        for k in range(RAD + 1):
+            lines[X, k] = fold[k]
+
+    def filter_rows(x):
+        groups = {}
+        for a in range(RAD + 1):
             for k in range(RAD + 1):
-                w = max(0.0, RAD + 0.5 - math.sqrt(d + k * k))
-                if w > 0:
-                    line = plus(line, w * fold[k])
-            lines[X, i] = line
-
-    def filter_rows(x):
+                if cone(a, 0, k) > 0:
+                    both = lines[x + HALO + a, k]
+                    if a > 0:
+                        both = both + lines[x + HALO - a, k]
+                    groups[a * a + k * k] = plus(groups.get(a * a + k * k), both)
         value = None
         for b in range(RAD + 1):
             row = None
-            for a in range(-RAD, RAD + 1):
-                if cone(a, b, 0) > 0:
-                    row = plus(row, lines[x + HALO + a, distances.index(a * a + b * b)])
+            for d, group in groups.items():
+                w = RAD + 0.5 - math.sqrt(d + b * b)
+                if w > 0:
+                    row = plus(row, w * group)
             value = row if b == 0 else value + roll(row, b, 0) + roll(row, -b, 0)
         sens[x] = value[0:16]
 
@@ -489,28 +492,12 @@
             rest //= count
         to = [p if t is None else partner(p, t, c) for p, t, c in zip(place, turns, counts)]
         if None in to:
-            to = place
+            continue
         index = 0
         for p, count in zip(to, counts):
             index = index * count + p
         pairs.append((flat, index))
     return pairs
-
-
-def prime_factors(count):
-    factors, p = [], 2
-    while count > 1:
-        while count % p == 0:
-            factors.append(p)
-            count //= p
-        p += 1
-    return factors
-
-
-def total_over(value, mesh_shape):
-    count = math.prod(mesh_shape[a] for a in AXES)
-    copies = jnp.broadcast_to(value, (count,) + value.shape)
-    return jnp.sum(lax.all_to_all(copies, AXES, 0, 0), axis=0)
 
 
 def per_device(mesh_shape, solution, residual, direction, density, labels):
@@ -544,18 +531,18 @@
     ends_got = [lax.ppermute(ends, "gz", swap_pairs((nz,), (r,))) for r in (0, 1)]
     image, inverse, sums, around = call(
         functools.partial(apply_operator, nz),
-        [field, field, (8, 128), (7, 24, 128)],
+        [field, field, (nx * ny * nz, 1, 128), (7, 24, 128)],
         ext, *ends_got, residual, labels,
         scratch=[pltpu.VMEM((4, 3, 3, 10, 16, 128), f32)],
     )
-    total = total_over(sums, mesh_shape)
+    total = lax.all_to_all(sums, AXES, 0, 0)
     return tuple(
         call(
             finish_step,
             [field, field, field, flat],
             ext, ends, around, total, image, inverse, residual, direction, hinv, hside,
             scratch=[
-                pltpu.VMEM((4, 3, 16, 24, 128), f32), pltpu.VMEM((16, len(distances), 24, 128), f32),
+                pltpu.VMEM((4, 3, 16, 24, 128), f32), pltpu.VMEM((16, RAD + 1, 24, 128), f32),
                 pltpu.VMEM(field, f32), pltpu.VMEM(field, f32), pltpu.VMEM(field, f32),
                 pltpu.VMEM(flat, f32), pltpu.SemaphoreType.DMA((4,)),
             ],

time: 42.4 us -> 40.4 us (0.953)
  starting transfers between devices: 19.2 us -> 18.3 us
  waiting for transfers between devices: 12.2 us -> 11.5 us
  local copies, waits for them, and re-layouts: 0.68 us -> 0.01 us
    all_to_all x1, starting transfers between devices: 9.81 us -> 5.92 us  [per_device(): total = lax.all_to_all(sums, AXES, 0, 0)]
    ppermute x2, starting transfers between devices: 2.3 us -> 5.13 us  [per_device(): lax.ppermute(ends, 'gz', swap_pairs((nz,), (r,)))]
    all_to_all x1, waiting for transfers between devices: 7.47 us -> 6.77 us  [per_device(): total = lax.all_to_all(sums, AXES, 0, 0)]
    broadcast_in_dim x1 -> x0, local copies, waits for them, and re-layouts: 0.67 us -> none  [total_over(): copies = jnp.broadcast_to(value, (count,) + value.shape)]
where the time goes in v5:
time: 40.4 us; the launch traced here: 40.2 us
  starting transfers between devices  18.3 us (45%)
  waiting for transfers between devices  11.5 us (28%)
  Pallas kernels  9.61 us (24%)
  between operations  0.72 us (2%)
    pallas_call x5, Pallas kernels, call(): pl.pallas_call(body, out_shape=[jax.ShapeDtypeStruct(shape, f32) for shap...  9.61 us
    all_to_all x1, waiting for transfers between devices, per_device(): total = lax.all_to_all(sums, AXES, 0, 0)  6.77 us
    ppermute x3, starting transfers between devices, per_device(): strips.append(lax.ppermute(array, plane, swap_pairs((nx, ny), (turn, s))))  6.06 us
    all_to_all x1, starting transfers between devices, per_device(): total = lax.all_to_all(sums, AXES, 0, 0)  5.92 us
    ppermute x2, starting transfers between devices, per_device(): lax.ppermute(ends, 'gz', swap_pairs((nz,), (r,)))  5.13 us
    ppermute x2, waiting for transfers between devices, per_device(): lax.ppermute(ends, 'gz', swap_pairs((nz,), (r,)))  2.46 us
    ppermute x3, waiting for transfers between devices, per_device(): strips.append(lax.ppermute(array, plane, swap_pairs((nx, ny), (turn, s))))  2.3 us
    ppermute x2, starting transfers between devices, per_device(): lax.ppermute(halves[r], plane, swap_pairs((nx, ny), (r, None)))  1.18 us
  transfers between devices with their start and end apart: 8, of which 3 were waited for; matrix products, arithmetic and copies ran while one was open for 0% of the time, Pallas kernels for 1%

profile of v5, /device:TPU:0, one launch (start us, length us, event | category | flops | bytes accessed | tf_op | source)
XLA Modules:
  0.0 40.2 jit_solution(17230446791054527389)
XLA Ops:
  0.6 0.0 copy-start.2
  0.6 0.0 copy-start
  0.7 1.2 %shard_map.84 = (f32[7,4,16,128]{3,2,1,0:T(8,128)S(1)}, f32[7,4,16,128]{3,2,1,0:T(8,128)S(1)}, f32[7,4,8,128]{3,2,1,0:T(8,128)S(1)}, f32[7,2,8,128]{3,2,1,0:T(8,128)S(1)}, f32[7,2,8,128]{3,2,1,0:T(8,128)S(1)}) custom-call(f32[3,8,16,128]{3,2,1,0:T(8,128)} %sol_any.1, f32[3,8,16,128]{3,2,1,0:T(8,128)} %dire.1, f32[8,16,128]{2,1,0:T(8,128)} %den_any.1, ...), custom_call_target="tpu_custom_call" | custom-call | flops 20000000 | bytes 20000 | tf_op jit(solution)/shard_map/pallas_call | solution.py:48
  1.9 0.5 %collective-permute-start = (f32[7,4,16,128]{3,2,1,0:T(8,128)S(1)}, f32[7,4,16,128]{3,2,1,0:T(8,128)S(1)}, u32[]{:S(2)}, u32[]{:S(2)}) collective-permute-start(f32[7,4,16,128]{3,2,1,0:T(8,128)S(1)} %get-tuple-element.17.half0), channel_id=1, source_target_pairs={{0,8},{4,12},{8,0},{12,4},{16,24},{20,28},{24,16},{28,20},{1,9},{5... | collective-permute-start | bytes 688136 | tf_op jit(solution)/shard_map/ppermute | solution.py:520
  2.4 0.7 %collective-permute-start.1 = (f32[7,4,16,128]{3,2,1,0:T(8,128)S(1)}, f32[7,4,16,128]{3,2,1,0:T(8,128)S(1)}, u32[]{:S(2)}, u32[]{:S(2)}) collective-permute-start(f32[7,4,16,128]{3,2,1,0:T(8,128)S(1)} %get-tuple-element.18.half1), channel_id=1, source_target_pairs={{8,16},{12,20},{16,8},{20,12},{9,17},{13,21},{17,9},{21,13},{10,18... | collective-permute-start | bytes 688136 | tf_op jit(solution)/shard_map/ppermute | solution.py:520
  3.0 2.6 %collective-permute-start.2 = (f32[7,4,8,128]{3,2,1,0:T(8,128)S(1)}, f32[7,4,8,128]{3,2,1,0:T(8,128)S(1)}, u32[]{:S(2)}, u32[]{:S(2)}) collective-permute-start(f32[7,4,8,128]{3,2,1,0:T(8,128)S(1)} %get-tuple-element.19), channel_id=1, source_target_pairs={{0,4},{4,0},{8,12},{12,8},{16,20},{20,16},{24,28},{28,24},{1,5},{5... | collective-permute-start | bytes 344072 | tf_op jit(solution)/shard_map/ppermute | solution.py:524
  5.6 2.7 %collective-permute-start.3 = (f32[7,2,8,128]{3,2,1,0:T(8,128)S(1)}, f32[7,2,8,128]{3,2,1,0:T(8,128)S(1)}, u32[]{:S(2)}, u32[]{:S(2)}) collective-permute-start(f32[7,2,8,128]{3,2,1,0:T(8,128)S(1)} %get-tuple-element.20), channel_id=1, source_target_pairs={{0,12},{4,8},{8,4},{12,0},{16,28},{20,24},{24,20},{28,16},{1,13},{... | collective-permute-start | bytes 172040 | tf_op jit(solution)/shard_map/ppermute | solution.py:524
  8.3 0.0 copy-start.1
  8.3 0.8 %collective-permute-start.4 = (f32[7,2,8,128]{3,2,1,0:T(8,128)S(1)}, f32[7,2,8,128]{3,2,1,0:T(8,128)S(1)}, u32[]{:S(2)}, u32[]{:S(2)}) collective-permute-start(f32[7,2,8,128]{3,2,1,0:T(8,128)S(1)} %get-tuple-element.21), channel_id=1, source_target_pairs={{8,20},{12,16},{16,12},{20,8},{9,21},{13,17},{17,13},{21,9},{10,22... | collective-permute-start | bytes 172040 | tf_op jit(solution)/shard_map/ppermute | solution.py:524
  9.1 2.3 %collective-permute-done.3.refs_1_ = f32[7,2,8,128]{3,2,1,0:T(8,128)S(1)} collective-permute-done((f32[7,2,8,128]{3,2,1,0:T(8,128)S(1)}, f32[7,2,8,128]{3,2,1,0:T(8,128)S(1)}, u32[]{:S(2)}, u32[]{:S(2)}) %collective-permute-start.3) | collective-permute-done | bytes 57376 | tf_op jit(solution)/shard_map/ppermute | solution.py:524
  11.4 0.0 collective-permute-done.4.refs_2_
  11.4 0.0 collective-permute-done.2.refs_0_
  11.4 0.0 collective-permute-done.got0
  11.4 0.0 collective-permute-done.1.got1
  11.4 0.5 %shard_map.85 = (f32[7,16,24,128]{3,2,1,0:T(8,128)S(1)}, f32[7,24,128]{2,1,0:T(8,128)S(1)}) custom-call(f32[7,4,16,128]{3,2,1,0:T(8,128)S(1)} %get-tuple-element.17.half0, f32[7,4,16,128]{3,2,1,0:T(8,128)S(1)} %get-tuple-element.18.half1, f32[7,4,16,128]{3,2,1,0:T(8,128)S(1)} %collective-permute-done.got0, ...), custom_call_target="tpu_custom_call" | custom-call | flops 20000000 | bytes 20000 | tf_op jit(solution)/shard_map/pallas_call | solution.py:48
  11.9 0.7 %collective-permute-start.6 = (f32[7,24,128]{2,1,0:T(8,128)S(1)}, f32[7,24,128]{2,1,0:T(8,128)S(1)}, u32[]{:S(2)}, u32[]{:S(2)}) collective-permute-start(f32[7,24,128]{2,1,0:T(8,128)S(1)} %get-tuple-element.23.ends), channel_id=1, source_target_pairs={{1,2},{2,1},{5,6},{6,5},{9,10},{10,9},{13,14},{14,13},{17,18},{18,... | collective-permute-start | bytes 258056 | tf_op jit(solution)/shard_map/ppermute | solution.py:531
  12.6 4.5 %collective-permute-start.5 = (f32[7,24,128]{2,1,0:T(8,128)S(1)}, f32[7,24,128]{2,1,0:T(8,128)S(1)}, u32[]{:S(2)}, u32[]{:S(2)}) collective-permute-start(f32[7,24,128]{2,1,0:T(8,128)S(1)} %get-tuple-element.23.ends), channel_id=1, source_target_pairs={{0,1},{1,0},{2,3},{3,2},{4,5},{5,4},{6,7},{7,6},{8,9},{9,8},{10,11... | collective-permute-start | bytes 258056 | tf_op jit(solution)/shard_map/ppermute | solution.py:531
  17.0 0.0 collective-permute-done.6.got1
  17.0 2.5 %collective-permute-done.5.got0 = f32[7,24,128]{2,1,0:T(8,128)S(1)} collective-permute-done((f32[7,24,128]{2,1,0:T(8,128)S(1)}, f32[7,24,128]{2,1,0:T(8,128)S(1)}, u32[]{:S(2)}, u32[]{:S(2)}) %collective-permute-start.5) | collective-permute-done | bytes 86048 | tf_op jit(solution)/shard_map/ppermute | solution.py:531
  19.5 0.0 copy-done.2
  19.5 0.0 copy-done
  19.5 2.8 %shard_map.86 = (f32[3,8,16,128]{3,2,1,0:T(8,128)S(1)}, f32[3,8,16,128]{3,2,1,0:T(8,128)S(1)}, f32[32,1,128]{2,1,0:T(1,128)}, f32[7,24,128]{2,1,0:T(8,128)S(1)}) custom-call(f32[7,16,24,128]{3,2,1,0:T(8,128)S(1)} %get-tuple-element.22.ext, f32[7,24,128]{2,1,0:T(8,128)S(1)} %collective-permute-done.5.got0, f32[7,24,128]{2,1,0:T(8,128)S(1)} %collective-permute-done.6.got1, ...), custom_call_target="tpu_custom_call" | custom-call | flops 20000000 | bytes 20000 | tf_op jit(solution)/shard_map/pallas_call | solution.py:48
  22.3 5.9 %all-to-all-start = ((f32[32,1,128]{2,1,0:T(1,128)}), f32[32,1,128]{2,1,0:T(1,128)S(1)}, u32[]{:S(2)}, u32[]{:S(2)}) async-start(f32[32,1,128]{2,1,0:T(1,128)} %get-tuple-element.25), calls=%async_computation | async-start | bytes 32768 | tf_op jit(solution)/shard_map/all_to_all | solution.py:538
  28.2 0.3 shard_map.87
  28.5 6.8 %all-to-all-done.total = f32[32,1,128]{2,1,0:T(1,128)S(1)} async-done(((f32[32,1,128]{2,1,0:T(1,128)}), f32[32,1,128]{2,1,0:T(1,128)S(1)}, u32[]{:S(2)}, u32[]{:S(2)}) %all-to-all-start) | async-done | bytes 16416 | tf_op jit(solution)/shard_map/all_to_all | solution.py:538
  35.3 0.0 copy-done.1
  35.3 4.9 %shard_map.88 = (f32[3,8,16,128]{3,2,1,0:T(8,128)}, f32[3,8,16,128]{3,2,1,0:T(8,128)}, f32[3,8,16,128]{3,2,1,0:T(8,128)}, f32[8,16,128]{2,1,0:T(8,128)}) custom-call(f32[7,16,24,128]{3,2,1,0:T(8,128)S(1)} %get-tuple-element.22.ext, f32[7,24,128]{2,1,0:T(8,128)S(1)} %get-tuple-element.23.ends, f32[7,24,128]{2,1,0:T(8,128)S(1)} %get-tuple-element.24.around, ...), custom_call_target="tpu_custom_call" | custom-call | flops 20000000 | bytes 20000 | tf_op jit(solution)/shard_map/pallas_call | solution.py:48
Async XLA Ops:
  0.6 18.9 %copy-start.2 = (s32[8,16,128]{2,1,0:T(8,128)S(1)}, s32[8,16,128]{2,1,0:T(8,128)}, u32[]{:S(2)}) copy-start(s32[8,16,128]{2,1,0:T(8,128)} %lab.1) | copy-start | bytes 196612
  0.6 18.9 %copy-start = (f32[3,8,16,128]{3,2,1,0:T(8,128)S(1)}, f32[3,8,16,128]{3,2,1,0:T(8,128)}, u32[]{:S(2)}) copy-start(f32[3,8,16,128]{3,2,1,0:T(8,128)} %res.3) | copy-start | bytes 589828
  1.9 9.6 %collective-permute-start = (f32[7,4,16,128]{3,2,1,0:T(8,128)S(1)}, f32[7,4,16,128]{3,2,1,0:T(8,128)S(1)}, u32[]{:S(2)}, u32[]{:S(2)}) collective-permute-start(f32[7,4,16,128]{3,2,1,0:T(8,128)S(1)} %get-tuple-element.17.half0), channel_id=1, source_target_pairs={{0,8},{4,12},{8,0},{12,4},{16,24},{20,28},{24,16},{28,20},{1,9},{5... | collective-permute-start | bytes 688136 | tf_op jit(solution)/shard_map/ppermute | solution.py:520
  2.4 9.0 %collective-permute-start.1 = (f32[7,4,16,128]{3,2,1,0:T(8,128)S(1)}, f32[7,4,16,128]{3,2,1,0:T(8,128)S(1)}, u32[]{:S(2)}, u32[]{:S(2)}) collective-permute-start(f32[7,4,16,128]{3,2,1,0:T(8,128)S(1)} %get-tuple-element.18.half1), channel_id=1, source_target_pairs={{8,16},{12,20},{16,8},{20,12},{9,17},{13,21},{17,9},{21,13},{10,18... | collective-permute-start | bytes 688136 | tf_op jit(solution)/shard_map/ppermute | solution.py:520
  3.0 8.4 %collective-permute-start.2 = (f32[7,4,8,128]{3,2,1,0:T(8,128)S(1)}, f32[7,4,8,128]{3,2,1,0:T(8,128)S(1)}, u32[]{:S(2)}, u32[]{:S(2)}) collective-permute-start(f32[7,4,8,128]{3,2,1,0:T(8,128)S(1)} %get-tuple-element.19), channel_id=1, source_target_pairs={{0,4},{4,0},{8,12},{12,8},{16,20},{20,16},{24,28},{28,24},{1,5},{5... | collective-permute-start | bytes 344072 | tf_op jit(solution)/shard_map/ppermute | solution.py:524
  5.6 5.8 %collective-permute-start.3 = (f32[7,2,8,128]{3,2,1,0:T(8,128)S(1)}, f32[7,2,8,128]{3,2,1,0:T(8,128)S(1)}, u32[]{:S(2)}, u32[]{:S(2)}) collective-permute-start(f32[7,2,8,128]{3,2,1,0:T(8,128)S(1)} %get-tuple-element.20), channel_id=1, source_target_pairs={{0,12},{4,8},{8,4},{12,0},{16,28},{20,24},{24,20},{28,16},{1,13},{... | collective-permute-start | bytes 172040 | tf_op jit(solution)/shard_map/ppermute | solution.py:524
  8.3 27.0 %copy-start.1 = (f32[3,8,16,128]{3,2,1,0:T(8,128)S(1)}, f32[3,8,16,128]{3,2,1,0:T(8,128)}, u32[]{:S(2)}) copy-start(f32[3,8,16,128]{3,2,1,0:T(8,128)} %dire.1) | copy-start | bytes 589828
  8.3 3.1 %collective-permute-start.4 = (f32[7,2,8,128]{3,2,1,0:T(8,128)S(1)}, f32[7,2,8,128]{3,2,1,0:T(8,128)S(1)}, u32[]{:S(2)}, u32[]{:S(2)}) collective-permute-start(f32[7,2,8,128]{3,2,1,0:T(8,128)S(1)} %get-tuple-element.21), channel_id=1, source_target_pairs={{8,20},{12,16},{16,12},{20,8},{9,21},{13,17},{17,13},{21,9},{10,22... | collective-permute-start | bytes 172040 | tf_op jit(solution)/shard_map/ppermute | solution.py:524
  11.9 5.1 %collective-permute-start.6 = (f32[7,24,128]{2,1,0:T(8,128)S(1)}, f32[7,24,128]{2,1,0:T(8,128)S(1)}, u32[]{:S(2)}, u32[]{:S(2)}) collective-permute-start(f32[7,24,128]{2,1,0:T(8,128)S(1)} %get-tuple-element.23.ends), channel_id=1, source_target_pairs={{1,2},{2,1},{5,6},{6,5},{9,10},{10,9},{13,14},{14,13},{17,18},{18,... | collective-permute-start | bytes 258056 | tf_op jit(solution)/shard_map/ppermute | solution.py:531
  12.6 6.9 %collective-permute-start.5 = (f32[7,24,128]{2,1,0:T(8,128)S(1)}, f32[7,24,128]{2,1,0:T(8,128)S(1)}, u32[]{:S(2)}, u32[]{:S(2)}) collective-permute-start(f32[7,24,128]{2,1,0:T(8,128)S(1)} %get-tuple-element.23.ends), channel_id=1, source_target_pairs={{0,1},{1,0},{2,3},{3,2},{4,5},{5,4},{6,7},{7,6},{8,9},{9,8},{10,11... | collective-permute-start | bytes 258056 | tf_op jit(solution)/shard_map/ppermute | solution.py:531
  22.3 13.0 %all-to-all-start = ((f32[32,1,128]{2,1,0:T(1,128)}), f32[32,1,128]{2,1,0:T(1,128)S(1)}, u32[]{:S(2)}, u32[]{:S(2)}) async-start(f32[32,1,128]{2,1,0:T(1,128)} %get-tuple-element.25), calls=%async_computation | async-start | bytes 32768 | tf_op jit(solution)/shard_map/all_to_all | solution.py:538

commit v6 on v5

--- a/solution.py
+++ b/solution.py
@@ -10,6 +10,7 @@
 
 RAD = 3
 HALO = RAD + 1
+ZTILES = 11
 stiff_floor = 0.001
 penalty = 3.0
 f32 = jnp.float32
@@ -109,11 +110,12 @@
 
 def extend(counts, half0, half1, got0, got1, *refs):
     nx, ny, nz = counts
-    sides, (ext, ends) = refs[:-2], refs[-2:]
+    sides, (ext, ends, send0, send1) = refs[:-4], refs[-4:]
     sub = rows_of((8, 128))
     lane = lanes_of((24, 128))
+    lows = lanes_of((8, 128)) % 8 < 4
     ix, iy = lax.axis_index("gx"), lax.axis_index("gy")
-    even_y = is_even("gy")
+    even_y, even_z = is_even("gy"), is_even("gz")
     x_ok = ((ix > 0).astype(f32), (ix < nx - 1).astype(f32))
     y_ok = ((iy > 0).astype(f32), (iy < ny - 1).astype(f32))
 
@@ -153,6 +155,16 @@
                 turned = roll(plane, 8 * X + 4, 1)
                 packed = turned if X == 0 else jnp.where(lane >= 8 * X, turned, packed)
             ends[f] = packed
+        for j in range(ZTILES):
+            tiles = []
+            for t in (j, j + ZTILES):
+                tiles.append(ends[t // 3, 8 * (t % 3) : 8 * (t % 3) + 8] if t < 21 else None)
+            up, down = tiles[0], tiles[0]
+            if tiles[1] is not None:
+                up = jnp.where(lows, tiles[0], roll(tiles[1], 4, 1))
+                down = jnp.where(lows, roll(tiles[1], -4, 1), tiles[0])
+            send0[j] = jnp.where(even_z, up, down)
+            send1[j] = jnp.where(even_z, down, up)
 
     @pl.when(ix % 2 == 0)
     def _():
@@ -217,11 +229,17 @@
     lane = lanes_of((24, 128))
     fields = (0, 1, 2, 6)
     iz = lax.axis_index("gz")
-    lows = lane % 8 < 4
-    from_zero = (lane // 4) % 2 == (iz + 1) % 2
+    even = is_even("gz")
+    lows = lanes_of((8, 128)) % 8 < 4
     keep = jnp.where(lows, (iz > 0).astype(f32), (iz < nz - 1).astype(f32))
-    for f in range(7):
-        around[f] = jnp.where(from_zero, got0[f], got1[f]) * keep
+    for j in range(ZTILES):
+        zero, one = got0[j], got1[j]
+        below, above = jnp.where(even, one, zero), jnp.where(even, zero, one)
+        for t in (j, j + ZTILES):
+            if t < 21:
+                if t != j:
+                    below, above = roll(below, -4, 1), roll(above, 4, 1)
+                around[t // 3, 8 * (t % 3) : 8 * (t % 3) + 8] = jnp.where(lows, below, above) * keep
     parts = [jnp.zeros((16, 128), f32) for _ in range(4)]
     for plane_at in range(10):
         X = plane_at + 3
@@ -305,11 +323,13 @@
             parts[1] = parts[1] + mid[c] * total
             parts[2] = parts[2] + r * scaled
             parts[3] = parts[3] + total * scaled
-    row = jnp.zeros((1, 128), f32)
+    place = lanes_of((1, 128)) // 32
+    row = None
     for k in range(4):
-        part = jnp.sum(parts[k], axis=0, keepdims=True)
-        part = jnp.sum(part, axis=1, keepdims=True)
-        row = jnp.where(lanes_of((1, 128)) == k, part, row)
+        part = parts[k][0:8] + parts[k][8:16]
+        part = part + roll(part, 64, 1)
+        part = jnp.sum(part + roll(part, 32, 1), axis=0, keepdims=True)
+        row = part if k == 0 else jnp.where(place == k, part, row)
     sums[...] = jnp.broadcast_to(row[None], sums.shape)
 
 
@@ -352,8 +372,9 @@
             ((new_res, new_res_any), (new_dir, new_dir_any), (new_sol, new_sol_any), (sens, sens_any))
         )
     ]
-    tot = jnp.sum(total[...], axis=0)
-    rz, pq, s2, s3 = (tot[:, k : k + 1] for k in range(4))
+    spread = jnp.broadcast_to(jnp.sum(total[...], axis=0), (8, 128))
+    tot = jnp.sum(jnp.where(lanes_of((8, 128)) // 32 == rows_of((8, 128)), spread, 0.0), axis=1, keepdims=True)
+    rz, pq, s2, s3 = (tot[k : k + 1] for k in range(4))
     alpha = rz / pq
     beta = (rz + alpha * (alpha * s3 - 2.0 * s2)) / rz
 
@@ -523,19 +544,21 @@
         for array, turn in zip(packed[2 + 3 * s : 5 + 3 * s], (None, 0, 1)):
             strips.append(lax.ppermute(array, plane, swap_pairs((nx, ny), (turn, s))))
     hinv, hside = call(functools.partial(inverse_sums, (nx, ny, nz)), [(16, 24, 128), (2, 24, 128)])
-    ext, ends = call(
+    zend = (ZTILES, 8, 128)
+    ext, ends, *sends = call(
         functools.partial(extend, (nx, ny, nz)),
-        [(7, 16, 24, 128), (7, 24, 128)],
+        [(7, 16, 24, 128), (7, 24, 128), zend, zend],
         *halves, *got, *strips,
     )
-    ends_got = [lax.ppermute(ends, "gz", swap_pairs((nz,), (r,))) for r in (0, 1)]
+    ends_got = [lax.ppermute(sends[r], "gz", swap_pairs((nz,), (r,))) for r in (0, 1)]
     image, inverse, sums, around = call(
         functools.partial(apply_operator, nz),
-        [field, field, (nx * ny * nz, 1, 128), (7, 24, 128)],
+        [field, field, (nx * ny, 1, 128), (7, 24, 128)],
         ext, *ends_got, residual, labels,
         scratch=[pltpu.VMEM((4, 3, 3, 10, 16, 128), f32)],
     )
-    total = lax.all_to_all(sums, AXES, 0, 0)
+    in_plane = jnp.sum(lax.all_to_all(sums, plane, 0, 0), axis=0, keepdims=True)
+    total = lax.all_to_all(jnp.broadcast_to(in_plane, (nz, 1, 128)), "gz", 0, 0)
     return tuple(
         call(
             finish_step,

time: 40.4 us -> 46.8 us (1.16)
  blocking collectives: 0 us -> 9.82 us
  waiting for transfers between devices: 11.5 us -> 9.32 us
  starting transfers between devices: 18.3 us -> 16.8 us
  local copies, waits for them, and re-layouts: 0.01 us -> 0.59 us
    all_to_all x0 -> x1, blocking collectives: none -> 9.82 us  [per_device(): in_plane = jnp.sum(lax.all_to_all(sums, plane, 0, 0), axis=0, keepdims=True)]
    ppermute x2, starting transfers between devices: 5.13 us -> 2.29 us  [per_device(): lax.ppermute(sends[r], 'gz', swap_pairs((nz,), (r,)))]
    all_to_all x1, waiting for transfers between devices: 6.77 us -> 5.21 us  [per_device(): total = lax.all_to_all(jnp.broadcast_to(in_plane, (nz, 1, 128)), 'gz', 0, 0)]
    all_to_all x1, starting transfers between devices: 5.92 us -> 7.3 us  [per_device(): total = lax.all_to_all(jnp.broadcast_to(in_plane, (nz, 1, 128)), 'gz', 0, 0)]
    ppermute x2, waiting for transfers between devices: 2.46 us -> 1.81 us  [per_device(): lax.ppermute(sends[r], 'gz', swap_pairs((nz,), (r,)))]
    broadcast_in_dim x0 -> x1, local copies, waits for them, and re-layouts: none -> 0.58 us  [per_device(): total = lax.all_to_all(jnp.broadcast_to(in_plane, (nz, 1, 128)), 'gz', 0, 0)]
where the time goes in v6:
time: 46.8 us; the launch traced here: 46.5 us
  starting transfers between devices  16.8 us (36%)
  blocking collectives  9.82 us (21%)
  waiting for transfers between devices  9.32 us (20%)
  Pallas kernels  9.21 us (20%)
  between operations  0.72 us (2%)
  local copies, waits for them, and re-layouts  0.59 us (1%)
    all_to_all x1, blocking collectives, per_device(): in_plane = jnp.sum(lax.all_to_all(sums, plane, 0, 0), axis=0, keepdims=True)  9.82 us
    pallas_call x5, Pallas kernels, call(): pl.pallas_call(body, out_shape=[jax.ShapeDtypeStruct(shape, f32) for shap...  9.21 us
    all_to_all x1, starting transfers between devices, per_device(): total = lax.all_to_all(jnp.broadcast_to(in_plane, (nz, 1, 128)), 'gz', 0, 0)  7.3 us
    ppermute x3, starting transfers between devices, per_device(): strips.append(lax.ppermute(array, plane, swap_pairs((nx, ny), (turn, s))))  6.06 us
    all_to_all x1, waiting for transfers between devices, per_device(): total = lax.all_to_all(jnp.broadcast_to(in_plane, (nz, 1, 128)), 'gz', 0, 0)  5.21 us
    ppermute x3, waiting for transfers between devices, per_device(): strips.append(lax.ppermute(array, plane, swap_pairs((nx, ny), (turn, s))))  2.3 us
    ppermute x2, starting transfers between devices, per_device(): lax.ppermute(sends[r], 'gz', swap_pairs((nz,), (r,)))  2.29 us
    ppermute x2, waiting for transfers between devices, per_device(): lax.ppermute(sends[r], 'gz', swap_pairs((nz,), (r,)))  1.81 us
  transfers between devices with their start and end apart: 8, of which 3 were waited for; matrix products, arithmetic and copies ran while one was open for 0% of the time, Pallas kernels for 1%

profile of v6, /device:TPU:0, one launch (start us, length us, event | category | flops | bytes accessed | tf_op | source)
XLA Modules:
  0.0 46.5 jit_solution(5408238358947324157)
XLA Ops:
  0.6 0.0 copy-start.2
  0.6 0.0 copy-start.1
  0.7 1.2 %shard_map.84 = (f32[7,4,16,128]{3,2,1,0:T(8,128)S(1)}, f32[7,4,16,128]{3,2,1,0:T(8,128)S(1)}, f32[7,4,8,128]{3,2,1,0:T(8,128)S(1)}, f32[7,2,8,128]{3,2,1,0:T(8,128)S(1)}, f32[7,2,8,128]{3,2,1,0:T(8,128)S(1)}) custom-call(f32[3,8,16,128]{3,2,1,0:T(8,128)} %sol_any.1, f32[3,8,16,128]{3,2,1,0:T(8,128)} %dire.1, f32[8,16,128]{2,1,0:T(8,128)} %den_any.1, ...), custom_call_target="tpu_custom_call" | custom-call | flops 20000000 | bytes 20000 | tf_op jit(solution)/shard_map/pallas_call | solution.py:49
  1.9 0.5 %collective-permute-start = (f32[7,4,16,128]{3,2,1,0:T(8,128)S(1)}, f32[7,4,16,128]{3,2,1,0:T(8,128)S(1)}, u32[]{:S(2)}, u32[]{:S(2)}) collective-permute-start(f32[7,4,16,128]{3,2,1,0:T(8,128)S(1)} %get-tuple-element.19.half0), channel_id=1, source_target_pairs={{0,8},{4,12},{8,0},{12,4},{16,24},{20,28},{24,16},{28,20},{1,9},{5... | collective-permute-start | bytes 688136 | tf_op jit(solution)/shard_map/ppermute | solution.py:541
  2.4 0.7 %collective-permute-start.1 = (f32[7,4,16,128]{3,2,1,0:T(8,128)S(1)}, f32[7,4,16,128]{3,2,1,0:T(8,128)S(1)}, u32[]{:S(2)}, u32[]{:S(2)}) collective-permute-start(f32[7,4,16,128]{3,2,1,0:T(8,128)S(1)} %get-tuple-element.20.half1), channel_id=1, source_target_pairs={{8,16},{12,20},{16,8},{20,12},{9,17},{13,21},{17,9},{21,13},{10,18... | collective-permute-start | bytes 688136 | tf_op jit(solution)/shard_map/ppermute | solution.py:541
  3.0 2.6 %collective-permute-start.2 = (f32[7,4,8,128]{3,2,1,0:T(8,128)S(1)}, f32[7,4,8,128]{3,2,1,0:T(8,128)S(1)}, u32[]{:S(2)}, u32[]{:S(2)}) collective-permute-start(f32[7,4,8,128]{3,2,1,0:T(8,128)S(1)} %get-tuple-element.21), channel_id=1, source_target_pairs={{0,4},{4,0},{8,12},{12,8},{16,20},{20,16},{24,28},{28,24},{1,5},{5... | collective-permute-start | bytes 344072 | tf_op jit(solution)/shard_map/ppermute | solution.py:545
  5.6 2.7 %collective-permute-start.3 = (f32[7,2,8,128]{3,2,1,0:T(8,128)S(1)}, f32[7,2,8,128]{3,2,1,0:T(8,128)S(1)}, u32[]{:S(2)}, u32[]{:S(2)}) collective-permute-start(f32[7,2,8,128]{3,2,1,0:T(8,128)S(1)} %get-tuple-element.22), channel_id=1, source_target_pairs={{0,12},{4,8},{8,4},{12,0},{16,28},{20,24},{24,20},{28,16},{1,13},{... | collective-permute-start | bytes 172040 | tf_op jit(solution)/shard_map/ppermute | solution.py:545
  8.3 0.0 copy-start
  8.3 0.8 %collective-permute-start.4 = (f32[7,2,8,128]{3,2,1,0:T(8,128)S(1)}, f32[7,2,8,128]{3,2,1,0:T(8,128)S(1)}, u32[]{:S(2)}, u32[]{:S(2)}) collective-permute-start(f32[7,2,8,128]{3,2,1,0:T(8,128)S(1)} %get-tuple-element.23), channel_id=1, source_target_pairs={{8,20},{12,16},{16,12},{20,8},{9,21},{13,17},{17,13},{21,9},{10,22... | collective-permute-start | bytes 172040 | tf_op jit(solution)/shard_map/ppermute | solution.py:545
  9.1 2.3 %collective-permute-done.3.refs_1_ = f32[7,2,8,128]{3,2,1,0:T(8,128)S(1)} collective-permute-done((f32[7,2,8,128]{3,2,1,0:T(8,128)S(1)}, f32[7,2,8,128]{3,2,1,0:T(8,128)S(1)}, u32[]{:S(2)}, u32[]{:S(2)}) %collective-permute-start.3) | collective-permute-done | bytes 57376 | tf_op jit(solution)/shard_map/ppermute | solution.py:545
  11.4 0.0 collective-permute-done.4.refs_2_
  11.4 0.0 collective-permute-done.2.refs_0_
  11.4 0.0 collective-permute-done.got0
  11.4 0.0 collective-permute-done.1.got1
  11.4 0.5 %shard_map.85 = (f32[7,16,24,128]{3,2,1,0:T(8,128)S(1)}, f32[7,24,128]{2,1,0:T(8,128)S(1)}, f32[11,8,128]{2,1,0:T(8,128)S(1)}, f32[11,8,128]{2,1,0:T(8,128)S(1)}) custom-call(f32[7,4,16,128]{3,2,1,0:T(8,128)S(1)} %get-tuple-element.19.half0, f32[7,4,16,128]{3,2,1,0:T(8,128)S(1)} %get-tuple-element.20.half1, f32[7,4,16,128]{3,2,1,0:T(8,128)S(1)} %collective-permute-done.got0, ...), custom_call_target="tpu_custom_call" | custom-call | flops 20000000 | bytes 20000 | tf_op jit(solution)/shard_map/pallas_call | solution.py:49
  12.0 1.6 %collective-permute-start.5 = (f32[11,8,128]{2,1,0:T(8,128)S(1)}, f32[11,8,128]{2,1,0:T(8,128)S(1)}, u32[]{:S(2)}, u32[]{:S(2)}) collective-permute-start(f32[11,8,128]{2,1,0:T(8,128)S(1)} %get-tuple-element.26), channel_id=1, source_target_pairs={{0,1},{1,0},{2,3},{3,2},{4,5},{5,4},{6,7},{7,6},{8,9},{9,8},{10,11... | collective-permute-start | bytes 135176 | tf_op jit(solution)/shard_map/ppermute | solution.py:553
  13.6 0.7 %collective-permute-start.6 = (f32[11,8,128]{2,1,0:T(8,128)S(1)}, f32[11,8,128]{2,1,0:T(8,128)S(1)}, u32[]{:S(2)}, u32[]{:S(2)}) collective-permute-start(f32[11,8,128]{2,1,0:T(8,128)S(1)} %get-tuple-element.27), channel_id=1, source_target_pairs={{1,2},{2,1},{5,6},{6,5},{9,10},{10,9},{13,14},{14,13},{17,18},{18,... | collective-permute-start | bytes 135176 | tf_op jit(solution)/shard_map/ppermute | solution.py:553
  14.3 1.8 %collective-permute-done.5.got0 = f32[11,8,128]{2,1,0:T(8,128)S(1)} collective-permute-done((f32[11,8,128]{2,1,0:T(8,128)S(1)}, f32[11,8,128]{2,1,0:T(8,128)S(1)}, u32[]{:S(2)}, u32[]{:S(2)}) %collective-permute-start.5) | collective-permute-done | bytes 45088 | tf_op jit(solution)/shard_map/ppermute | solution.py:553
  16.1 0.0 collective-permute-done.6.got1
  16.1 0.0 copy-done.2
  16.1 0.0 copy-done.1
  16.1 2.1 %shard_map.86 = (f32[3,8,16,128]{3,2,1,0:T(8,128)S(1)}, f32[3,8,16,128]{3,2,1,0:T(8,128)S(1)}, f32[8,1,128]{2,1,0:T(1,128)S(1)}, f32[7,24,128]{2,1,0:T(8,128)S(1)}) custom-call(f32[7,16,24,128]{3,2,1,0:T(8,128)S(1)} %get-tuple-element.24.ext, f32[11,8,128]{2,1,0:T(8,128)S(1)} %collective-permute-done.5.got0, f32[11,8,128]{2,1,0:T(8,128)S(1)} %collective-permute-done.6.got1, ...), custom_call_target="tpu_custom_call" | custom-call | flops 20000000 | bytes 20000 | tf_op jit(solution)/shard_map/pallas_call | solution.py:49
  18.2 9.8 %all_to_all.10 = f32[8,1,128]{2,1,0:T(1,128)S(1)} all-to-all(f32[8,1,128]{2,1,0:T(1,128)S(1)} %get-tuple-element.29), channel_id=1, replica_groups=mesh['gx'=4,'gy'=2,'gz'=4] {'gx','gy'}, dimensions={0} | all-to-all | bytes 8192 | tf_op jit(solution)/shard_map/all_to_all | solution.py:560
  28.1 0.6 %broadcast_in_dim.2 = f32[4,1,128]{2,1,0:T(1,128)} broadcast(f32[128]{0:T(128)S(1)} %reduce_sum.9), dimensions={2} | broadcast | bytes 2560 | tf_op jit(solution)/shard_map/broadcast_in_dim | solution.py:561
  28.6 7.3 %all-to-all-start.1 = ((f32[4,1,128]{2,1,0:T(1,128)}), f32[4,1,128]{2,1,0:T(1,128)S(1)}, u32[]{:S(2)}, u32[]{:S(2)}) async-start(f32[4,1,128]{2,1,0:T(1,128)} %broadcast_in_dim.2), calls=%async_computation.1 | async-start | bytes 4096 | tf_op jit(solution)/shard_map/all_to_all | solution.py:561
  35.9 0.3 shard_map.87
  36.2 5.2 %all-to-all-done.1.total = f32[4,1,128]{2,1,0:T(1,128)S(1)} async-done(((f32[4,1,128]{2,1,0:T(1,128)}), f32[4,1,128]{2,1,0:T(1,128)S(1)}, u32[]{:S(2)}, u32[]{:S(2)}) %all-to-all-start.1) | async-done | bytes 2080 | tf_op jit(solution)/shard_map/all_to_all | solution.py:561
  41.4 0.0 copy-done
  41.4 5.1 %shard_map.88 = (f32[3,8,16,128]{3,2,1,0:T(8,128)}, f32[3,8,16,128]{3,2,1,0:T(8,128)}, f32[3,8,16,128]{3,2,1,0:T(8,128)}, f32[8,16,128]{2,1,0:T(8,128)}) custom-call(f32[7,16,24,128]{3,2,1,0:T(8,128)S(1)} %get-tuple-element.24.ext, f32[7,24,128]{2,1,0:T(8,128)S(1)} %get-tuple-element.25.ends, f32[7,24,128]{2,1,0:T(8,128)S(1)} %get-tuple-element.28.around, ...), custom_call_target="tpu_custom_call" | custom-call | flops 20000000 | bytes 20000 | tf_op jit(solution)/shard_map/pallas_call | solution.py:49
  (1 shorter events, 0.0 us)
Async XLA Ops:
  0.6 15.5 %copy-start.2 = (s32[8,16,128]{2,1,0:T(8,128)S(1)}, s32[8,16,128]{2,1,0:T(8,128)}, u32[]{:S(2)}) copy-start(s32[8,16,128]{2,1,0:T(8,128)} %lab.1) | copy-start | bytes 196612
  0.6 15.4 %copy-start.1 = (f32[3,8,16,128]{3,2,1,0:T(8,128)S(1)}, f32[3,8,16,128]{3,2,1,0:T(8,128)}, u32[]{:S(2)}) copy-start(f32[3,8,16,128]{3,2,1,0:T(8,128)} %res.3) | copy-start | bytes 589828
  1.9 9.6 %collective-permute-start = (f32[7,4,16,128]{3,2,1,0:T(8,128)S(1)}, f32[7,4,16,128]{3,2,1,0:T(8,128)S(1)}, u32[]{:S(2)}, u32[]{:S(2)}) collective-permute-start(f32[7,4,16,128]{3,2,1,0:T(8,128)S(1)} %get-tuple-element.19.half0), channel_id=1, source_target_pairs={{0,8},{4,12},{8,0},{12,4},{16,24},{20,28},{24,16},{28,20},{1,9},{5... | collective-permute-start | bytes 688136 | tf_op jit(solution)/shard_map/ppermute | solution.py:541
  2.4 9.0 %collective-permute-start.1 = (f32[7,4,16,128]{3,2,1,0:T(8,128)S(1)}, f32[7,4,16,128]{3,2,1,0:T(8,128)S(1)}, u32[]{:S(2)}, u32[]{:S(2)}) collective-permute-start(f32[7,4,16,128]{3,2,1,0:T(8,128)S(1)} %get-tuple-element.20.half1), channel_id=1, source_target_pairs={{8,16},{12,20},{16,8},{20,12},{9,17},{13,21},{17,9},{21,13},{10,18... | collective-permute-start | bytes 688136 | tf_op jit(solution)/shard_map/ppermute | solution.py:541
  3.0 8.4 %collective-permute-start.2 = (f32[7,4,8,128]{3,2,1,0:T(8,128)S(1)}, f32[7,4,8,128]{3,2,1,0:T(8,128)S(1)}, u32[]{:S(2)}, u32[]{:S(2)}) collective-permute-start(f32[7,4,8,128]{3,2,1,0:T(8,128)S(1)} %get-tuple-element.21), channel_id=1, source_target_pairs={{0,4},{4,0},{8,12},{12,8},{16,20},{20,16},{24,28},{28,24},{1,5},{5... | collective-permute-start | bytes 344072 | tf_op jit(solution)/shard_map/ppermute | solution.py:545
  5.6 5.8 %collective-permute-start.3 = (f32[7,2,8,128]{3,2,1,0:T(8,128)S(1)}, f32[7,2,8,128]{3,2,1,0:T(8,128)S(1)}, u32[]{:S(2)}, u32[]{:S(2)}) collective-permute-start(f32[7,2,8,128]{3,2,1,0:T(8,128)S(1)} %get-tuple-element.22), channel_id=1, source_target_pairs={{0,12},{4,8},{8,4},{12,0},{16,28},{20,24},{24,20},{28,16},{1,13},{... | collective-permute-start | bytes 172040 | tf_op jit(solution)/shard_map/ppermute | solution.py:545
  8.3 33.1 %copy-start = (f32[3,8,16,128]{3,2,1,0:T(8,128)S(1)}, f32[3,8,16,128]{3,2,1,0:T(8,128)}, u32[]{:S(2)}) copy-start(f32[3,8,16,128]{3,2,1,0:T(8,128)} %dire.1) | copy-start | bytes 589828
  8.3 3.1 %collective-permute-start.4 = (f32[7,2,8,128]{3,2,1,0:T(8,128)S(1)}, f32[7,2,8,128]{3,2,1,0:T(8,128)S(1)}, u32[]{:S(2)}, u32[]{:S(2)}) collective-permute-start(f32[7,2,8,128]{3,2,1,0:T(8,128)S(1)} %get-tuple-element.23), channel_id=1, source_target_pairs={{8,20},{12,16},{16,12},{20,8},{9,21},{13,17},{17,13},{21,9},{10,22... | collective-permute-start | bytes 172040 | tf_op jit(solution)/shard_map/ppermute | solution.py:545
  12.0 4.1 %collective-permute-start.5 = (f32[11,8,128]{2,1,0:T(8,128)S(1)}, f32[11,8,128]{2,1,0:T(8,128)S(1)}, u32[]{:S(2)}, u32[]{:S(2)}) collective-permute-start(f32[11,8,128]{2,1,0:T(8,128)S(1)} %get-tuple-element.26), channel_id=1, source_target_pairs={{0,1},{1,0},{2,3},{3,2},{4,5},{5,4},{6,7},{7,6},{8,9},{9,8},{10,11... | collective-permute-start | bytes 135176 | tf_op jit(solution)/shard_map/ppermute | solution.py:553
  13.6 2.5 %collective-permute-start.6 = (f32[11,8,128]{2,1,0:T(8,128)S(1)}, f32[11,8,128]{2,1,0:T(8,128)S(1)}, u32[]{:S(2)}, u32[]{:S(2)}) collective-permute-start(f32[11,8,128]{2,1,0:T(8,128)S(1)} %get-tuple-element.27), channel_id=1, source_target_pairs={{1,2},{2,1},{5,6},{6,5},{9,10},{10,9},{13,14},{14,13},{17,18},{18,... | collective-permute-start | bytes 135176 | tf_op jit(solution)/shard_map/ppermute | solution.py:553
  28.6 12.8 %all-to-all-start.1 = ((f32[4,1,128]{2,1,0:T(1,128)}), f32[4,1,128]{2,1,0:T(1,128)S(1)}, u32[]{:S(2)}, u32[]{:S(2)}) async-start(f32[4,1,128]{2,1,0:T(1,128)} %broadcast_in_dim.2), calls=%async_computation.1 | async-start | bytes 4096 | tf_op jit(solution)/shard_map/all_to_all | solution.py:561

commit v7 on v6

--- a/solution.py
+++ b/solution.py
@@ -361,7 +361,7 @@
 
 
 def finish_step(
-    ext, ends, around, total, image, inverse, res, dire, hinv, hside,
+    ext, ends, around, ours, theirs, image, inverse, res, dire, hinv, hside,
     new_sol_any, new_res_any, new_dir_any, sens_any, us, lines, new_sol, new_res, new_dir, sens, sems,
 ):
     lane = lanes_of((24, 128))
@@ -372,7 +372,7 @@
             ((new_res, new_res_any), (new_dir, new_dir_any), (new_sol, new_sol_any), (sens, sens_any))
         )
     ]
-    spread = jnp.broadcast_to(jnp.sum(total[...], axis=0), (8, 128))
+    spread = jnp.broadcast_to(ours[...] + theirs[...], (8, 128))
     tot = jnp.sum(jnp.where(lanes_of((8, 128)) // 32 == rows_of((8, 128)), spread, 0.0), axis=1, keepdims=True)
     rz, pq, s2, s3 = (tot[k : k + 1] for k in range(4))
     alpha = rz / pq
@@ -526,6 +526,10 @@
     half, full, corner = (7, 4, 16, 128), (7, 4, 8, 128), (7, 2, 8, 128)
     rounds_y = 1 if ny == 2 else 2
     field, flat = (3, 8, 16, 128), (8, 16, 128)
+    steps = 2 if nx % 2 == 0 else 1
+    same = [
+        [i for i in range(nx * ny * nz) if i // (ny * nz) % steps == step] for step in range(steps)
+    ]
     packed = call(
         functools.partial(pack_faces, rounds_y),
         [half, half] + [full, corner, corner] * rounds_y,
@@ -553,17 +557,17 @@
     ends_got = [lax.ppermute(sends[r], "gz", swap_pairs((nz,), (r,))) for r in (0, 1)]
     image, inverse, sums, around = call(
         functools.partial(apply_operator, nz),
-        [field, field, (nx * ny, 1, 128), (7, 24, 128)],
+        [field, field, (len(same[0]), 1, 128), (7, 24, 128)],
         ext, *ends_got, residual, labels,
         scratch=[pltpu.VMEM((4, 3, 3, 10, 16, 128), f32)],
     )
-    in_plane = jnp.sum(lax.all_to_all(sums, plane, 0, 0), axis=0, keepdims=True)
-    total = lax.all_to_all(jnp.broadcast_to(in_plane, (nz, 1, 128)), "gz", 0, 0)
+    ours = jnp.sum(lax.all_to_all(sums, AXES, 0, 0, axis_index_groups=same), axis=0)
+    theirs = lax.ppermute(ours, "gx", swap_pairs((nx,), (0,))) if len(same) > 1 else jnp.zeros_like(ours)
     return tuple(
         call(
             finish_step,
             [field, field, field, flat],
-            ext, ends, around, total, image, inverse, residual, direction, hinv, hside,
+            ext, ends, around, ours, theirs, image, inverse, residual, direction, hinv, hside,
             scratch=[
                 pltpu.VMEM((4, 3, 16, 24, 128), f32), pltpu.VMEM((16, RAD + 1, 24, 128), f32),
                 pltpu.VMEM(field, f32), pltpu.VMEM(field, f32), pltpu.VMEM(field, f32),

time: 46.8 us -> 42.8 us (0.915)
  blocking collectives: 9.82 us -> 18 us
  starting transfers between devices: 16.8 us -> 9.59 us
  waiting for transfers between devices: 9.32 us -> 4.95 us
  local copies, waits for them, and re-layouts: 0.59 us -> 0.01 us
    all_to_all x1, blocking collectives: 9.82 us -> 18 us  [per_device(): lax.all_to_all(sums, AXES, 0, 0, axis_index_groups=same)]
    all_to_all x1 -> x0, starting transfers between devices: 7.3 us -> none  [per_device(): total = lax.all_to_all(jnp.broadcast_to(in_plane, (nz, 1, 128)), 'gz', 0, 0)]
    all_to_all x1 -> x0, waiting for transfers between devices: 5.21 us -> none  [per_device(): total = lax.all_to_all(jnp.broadcast_to(in_plane, (nz, 1, 128)), 'gz', 0, 0)]
    ppermute x0 -> x1, waiting for transfers between devices: none -> 0.83 us  [per_device(): lax.ppermute(ours, 'gx', swap_pairs((nx,), (0,)))]
    broadcast_in_dim x1 -> x0, local copies, waits for them, and re-layouts: 0.58 us -> none  [per_device(): total = lax.all_to_all(jnp.broadcast_to(in_plane, (nz, 1, 128)), 'gz', 0, 0)]
where the time goes in v7:
time: 42.8 us; the launch traced here: 42.6 us
  blocking collectives  18 us (42%)
  starting transfers between devices  9.59 us (22%)
  Pallas kernels  9.22 us (22%)
  waiting for transfers between devices  4.95 us (12%)
  between operations  0.73 us (2%)
    all_to_all x1, blocking collectives, per_device(): lax.all_to_all(sums, AXES, 0, 0, axis_index_groups=same)  18 us
    pallas_call x5, Pallas kernels, call(): pl.pallas_call(body, out_shape=[jax.ShapeDtypeStruct(shape, f32) for shap...  9.22 us
    ppermute x3, starting transfers between devices, per_device(): strips.append(lax.ppermute(array, plane, swap_pairs((nx, ny), (turn, s))))  6.06 us
    ppermute x3, waiting for transfers between devices, per_device(): strips.append(lax.ppermute(array, plane, swap_pairs((nx, ny), (turn, s))))  2.3 us
    ppermute x2, starting transfers between devices, per_device(): lax.ppermute(sends[r], 'gz', swap_pairs((nz,), (r,)))  2.29 us
    ppermute x2, waiting for transfers between devices, per_device(): lax.ppermute(sends[r], 'gz', swap_pairs((nz,), (r,)))  1.81 us
    ppermute x2, starting transfers between devices, per_device(): lax.ppermute(halves[r], plane, swap_pairs((nx, ny), (r, None)))  1.18 us
  transfers between devices with their start and end apart: 8, of which 3 were waited for; matrix products, arithmetic and copies ran while one was open for 0% of the time, Pallas kernels for 1%

profile of v7, /device:TPU:0, one launch (start us, length us, event | category | flops | bytes accessed | tf_op | source)
XLA Modules:
  0.0 42.6 jit_solution(161834611195890271)
XLA Ops:
  0.6 0.0 copy-start.2
  0.6 0.0 copy-start.1
  0.7 1.2 %shard_map.84 = (f32[7,4,16,128]{3,2,1,0:T(8,128)S(1)}, f32[7,4,16,128]{3,2,1,0:T(8,128)S(1)}, f32[7,4,8,128]{3,2,1,0:T(8,128)S(1)}, f32[7,2,8,128]{3,2,1,0:T(8,128)S(1)}, f32[7,2,8,128]{3,2,1,0:T(8,128)S(1)}) custom-call(f32[3,8,16,128]{3,2,1,0:T(8,128)} %sol_any.1, f32[3,8,16,128]{3,2,1,0:T(8,128)} %dire.1, f32[8,16,128]{2,1,0:T(8,128)} %den_any.1, ...), custom_call_target="tpu_custom_call" | custom-call | flops 20000000 | bytes 20000 | tf_op jit(solution)/shard_map/pallas_call | solution.py:49
  1.9 0.5 %collective-permute-start = (f32[7,4,16,128]{3,2,1,0:T(8,128)S(1)}, f32[7,4,16,128]{3,2,1,0:T(8,128)S(1)}, u32[]{:S(2)}, u32[]{:S(2)}) collective-permute-start(f32[7,4,16,128]{3,2,1,0:T(8,128)S(1)} %get-tuple-element.19.half0), channel_id=1, source_target_pairs={{0,8},{4,12},{8,0},{12,4},{16,24},{20,28},{24,16},{28,20},{1,9},{5... | collective-permute-start | bytes 688136 | tf_op jit(solution)/shard_map/ppermute | solution.py:545
  2.4 0.7 %collective-permute-start.1 = (f32[7,4,16,128]{3,2,1,0:T(8,128)S(1)}, f32[7,4,16,128]{3,2,1,0:T(8,128)S(1)}, u32[]{:S(2)}, u32[]{:S(2)}) collective-permute-start(f32[7,4,16,128]{3,2,1,0:T(8,128)S(1)} %get-tuple-element.20.half1), channel_id=1, source_target_pairs={{8,16},{12,20},{16,8},{20,12},{9,17},{13,21},{17,9},{21,13},{10,18... | collective-permute-start | bytes 688136 | tf_op jit(solution)/shard_map/ppermute | solution.py:545
  3.0 2.6 %collective-permute-start.2 = (f32[7,4,8,128]{3,2,1,0:T(8,128)S(1)}, f32[7,4,8,128]{3,2,1,0:T(8,128)S(1)}, u32[]{:S(2)}, u32[]{:S(2)}) collective-permute-start(f32[7,4,8,128]{3,2,1,0:T(8,128)S(1)} %get-tuple-element.21), channel_id=1, source_target_pairs={{0,4},{4,0},{8,12},{12,8},{16,20},{20,16},{24,28},{28,24},{1,5},{5... | collective-permute-start | bytes 344072 | tf_op jit(solution)/shard_map/ppermute | solution.py:549
  5.6 2.7 %collective-permute-start.3 = (f32[7,2,8,128]{3,2,1,0:T(8,128)S(1)}, f32[7,2,8,128]{3,2,1,0:T(8,128)S(1)}, u32[]{:S(2)}, u32[]{:S(2)}) collective-permute-start(f32[7,2,8,128]{3,2,1,0:T(8,128)S(1)} %get-tuple-element.22), channel_id=1, source_target_pairs={{0,12},{4,8},{8,4},{12,0},{16,28},{20,24},{24,20},{28,16},{1,13},{... | collective-permute-start | bytes 172040 | tf_op jit(solution)/shard_map/ppermute | solution.py:549
  8.3 0.0 copy-start
  8.3 0.8 %collective-permute-start.4 = (f32[7,2,8,128]{3,2,1,0:T(8,128)S(1)}, f32[7,2,8,128]{3,2,1,0:T(8,128)S(1)}, u32[]{:S(2)}, u32[]{:S(2)}) collective-permute-start(f32[7,2,8,128]{3,2,1,0:T(8,128)S(1)} %get-tuple-element.23), channel_id=1, source_target_pairs={{8,20},{12,16},{16,12},{20,8},{9,21},{13,17},{17,13},{21,9},{10,22... | collective-permute-start | bytes 172040 | tf_op jit(solution)/shard_map/ppermute | solution.py:549
  9.1 2.3 %collective-permute-done.3.refs_1_ = f32[7,2,8,128]{3,2,1,0:T(8,128)S(1)} collective-permute-done((f32[7,2,8,128]{3,2,1,0:T(8,128)S(1)}, f32[7,2,8,128]{3,2,1,0:T(8,128)S(1)}, u32[]{:S(2)}, u32[]{:S(2)}) %collective-permute-start.3) | collective-permute-done | bytes 57376 | tf_op jit(solution)/shard_map/ppermute | solution.py:549
  11.4 0.0 collective-permute-done.4.refs_2_
  11.4 0.0 collective-permute-done.2.refs_0_
  11.4 0.0 collective-permute-done.got0
  11.4 0.0 collective-permute-done.1.got1
  11.4 0.5 %shard_map.85 = (f32[7,16,24,128]{3,2,1,0:T(8,128)S(1)}, f32[7,24,128]{2,1,0:T(8,128)S(1)}, f32[11,8,128]{2,1,0:T(8,128)S(1)}, f32[11,8,128]{2,1,0:T(8,128)S(1)}) custom-call(f32[7,4,16,128]{3,2,1,0:T(8,128)S(1)} %get-tuple-element.19.half0, f32[7,4,16,128]{3,2,1,0:T(8,128)S(1)} %get-tuple-element.20.half1, f32[7,4,16,128]{3,2,1,0:T(8,128)S(1)} %collective-permute-done.got0, ...), custom_call_target="tpu_custom_call" | custom-call | flops 20000000 | bytes 20000 | tf_op jit(solution)/shard_map/pallas_call | solution.py:49
  12.0 1.6 %collective-permute-start.5 = (f32[11,8,128]{2,1,0:T(8,128)S(1)}, f32[11,8,128]{2,1,0:T(8,128)S(1)}, u32[]{:S(2)}, u32[]{:S(2)}) collective-permute-start(f32[11,8,128]{2,1,0:T(8,128)S(1)} %get-tuple-element.26), channel_id=1, source_target_pairs={{0,1},{1,0},{2,3},{3,2},{4,5},{5,4},{6,7},{7,6},{8,9},{9,8},{10,11... | collective-permute-start | bytes 135176 | tf_op jit(solution)/shard_map/ppermute | solution.py:557
  13.6 0.7 %collective-permute-start.6 = (f32[11,8,128]{2,1,0:T(8,128)S(1)}, f32[11,8,128]{2,1,0:T(8,128)S(1)}, u32[]{:S(2)}, u32[]{:S(2)}) collective-permute-start(f32[11,8,128]{2,1,0:T(8,128)S(1)} %get-tuple-element.27), channel_id=1, source_target_pairs={{1,2},{2,1},{5,6},{6,5},{9,10},{10,9},{13,14},{14,13},{17,18},{18,... | collective-permute-start | bytes 135176 | tf_op jit(solution)/shard_map/ppermute | solution.py:557
  14.3 1.8 %collective-permute-done.5.got0 = f32[11,8,128]{2,1,0:T(8,128)S(1)} collective-permute-done((f32[11,8,128]{2,1,0:T(8,128)S(1)}, f32[11,8,128]{2,1,0:T(8,128)S(1)}, u32[]{:S(2)}, u32[]{:S(2)}) %collective-permute-start.5) | collective-permute-done | bytes 45088 | tf_op jit(solution)/shard_map/ppermute | solution.py:557
  16.1 0.0 collective-permute-done.6.got1
  16.1 0.0 copy-done.2
  16.1 0.0 copy-done.1
  16.1 2.1 %shard_map.86 = (f32[3,8,16,128]{3,2,1,0:T(8,128)S(1)}, f32[3,8,16,128]{3,2,1,0:T(8,128)S(1)}, f32[16,1,128]{2,1,0:T(1,128)S(1)}, f32[7,24,128]{2,1,0:T(8,128)S(1)}) custom-call(f32[7,16,24,128]{3,2,1,0:T(8,128)S(1)} %get-tuple-element.24.ext, f32[11,8,128]{2,1,0:T(8,128)S(1)} %collective-permute-done.5.got0, f32[11,8,128]{2,1,0:T(8,128)S(1)} %collective-permute-done.6.got1, ...), custom_call_target="tpu_custom_call" | custom-call | flops 20000000 | bytes 20000 | tf_op jit(solution)/shard_map/pallas_call | solution.py:49
  18.2 18.0 %all_to_all.5 = f32[16,1,128]{2,1,0:T(1,128)S(1)} all-to-all(f32[16,1,128]{2,1,0:T(1,128)S(1)} %get-tuple-element.29), channel_id=1, replica_groups={{0,1,2,3,4,5,6,7,16,17,18,19,20,21,22,23},{8,9,10,11,12,13,14,15,24,25,..., dimensions={0} | all-to-all | bytes 16384 | tf_op jit(solution)/shard_map/all_to_all | solution.py:564
  36.3 0.1 collective-permute-start.7
  36.3 0.3 shard_map.87
  36.6 0.8 %collective-permute-done.7.theirs = f32[1,128]{1,0:T(1,128)S(1)} collective-permute-done((f32[1,128]{1,0:T(1,128)S(1)}, f32[1,128]{1,0:T(1,128)S(1)}, u32[]{:S(2)}, u32[]{:S(2)}) %collective-permute-start.7) | collective-permute-done | bytes 544 | tf_op jit(solution)/shard_map/ppermute | solution.py:565
  37.5 0.0 copy-done
  37.5 5.1 %shard_map.88 = (f32[3,8,16,128]{3,2,1,0:T(8,128)}, f32[3,8,16,128]{3,2,1,0:T(8,128)}, f32[3,8,16,128]{3,2,1,0:T(8,128)}, f32[8,16,128]{2,1,0:T(8,128)}) custom-call(f32[7,16,24,128]{3,2,1,0:T(8,128)S(1)} %get-tuple-element.24.ext, f32[7,24,128]{2,1,0:T(8,128)S(1)} %get-tuple-element.25.ends, f32[7,24,128]{2,1,0:T(8,128)S(1)} %get-tuple-element.28.around, ...), custom_call_target="tpu_custom_call" | custom-call | flops 20000000 | bytes 20000 | tf_op jit(solution)/shard_map/pallas_call | solution.py:49
  (1 shorter events, 0.0 us)
Async XLA Ops:
  0.6 15.5 %copy-start.2 = (s32[8,16,128]{2,1,0:T(8,128)S(1)}, s32[8,16,128]{2,1,0:T(8,128)}, u32[]{:S(2)}) copy-start(s32[8,16,128]{2,1,0:T(8,128)} %lab.1) | copy-start | bytes 196612
  0.6 15.4 %copy-start.1 = (f32[3,8,16,128]{3,2,1,0:T(8,128)S(1)}, f32[3,8,16,128]{3,2,1,0:T(8,128)}, u32[]{:S(2)}) copy-start(f32[3,8,16,128]{3,2,1,0:T(8,128)} %res.3) | copy-start | bytes 589828
  1.9 9.6 %collective-permute-start = (f32[7,4,16,128]{3,2,1,0:T(8,128)S(1)}, f32[7,4,16,128]{3,2,1,0:T(8,128)S(1)}, u32[]{:S(2)}, u32[]{:S(2)}) collective-permute-start(f32[7,4,16,128]{3,2,1,0:T(8,128)S(1)} %get-tuple-element.19.half0), channel_id=1, source_target_pairs={{0,8},{4,12},{8,0},{12,4},{16,24},{20,28},{24,16},{28,20},{1,9},{5... | collective-permute-start | bytes 688136 | tf_op jit(solution)/shard_map/ppermute | solution.py:545
  2.4 9.0 %collective-permute-start.1 = (f32[7,4,16,128]{3,2,1,0:T(8,128)S(1)}, f32[7,4,16,128]{3,2,1,0:T(8,128)S(1)}, u32[]{:S(2)}, u32[]{:S(2)}) collective-permute-start(f32[7,4,16,128]{3,2,1,0:T(8,128)S(1)} %get-tuple-element.20.half1), channel_id=1, source_target_pairs={{8,16},{12,20},{16,8},{20,12},{9,17},{13,21},{17,9},{21,13},{10,18... | collective-permute-start | bytes 688136 | tf_op jit(solution)/shard_map/ppermute | solution.py:545
  3.0 8.4 %collective-permute-start.2 = (f32[7,4,8,128]{3,2,1,0:T(8,128)S(1)}, f32[7,4,8,128]{3,2,1,0:T(8,128)S(1)}, u32[]{:S(2)}, u32[]{:S(2)}) collective-permute-start(f32[7,4,8,128]{3,2,1,0:T(8,128)S(1)} %get-tuple-element.21), channel_id=1, source_target_pairs={{0,4},{4,0},{8,12},{12,8},{16,20},{20,16},{24,28},{28,24},{1,5},{5... | collective-permute-start | bytes 344072 | tf_op jit(solution)/shard_map/ppermute | solution.py:549
  5.6 5.8 %collective-permute-start.3 = (f32[7,2,8,128]{3,2,1,0:T(8,128)S(1)}, f32[7,2,8,128]{3,2,1,0:T(8,128)S(1)}, u32[]{:S(2)}, u32[]{:S(2)}) collective-permute-start(f32[7,2,8,128]{3,2,1,0:T(8,128)S(1)} %get-tuple-element.22), channel_id=1, source_target_pairs={{0,12},{4,8},{8,4},{12,0},{16,28},{20,24},{24,20},{28,16},{1,13},{... | collective-permute-start | bytes 172040 | tf_op jit(solution)/shard_map/ppermute | solution.py:549
  8.3 29.1 %copy-start = (f32[3,8,16,128]{3,2,1,0:T(8,128)S(1)}, f32[3,8,16,128]{3,2,1,0:T(8,128)}, u32[]{:S(2)}) copy-start(f32[3,8,16,128]{3,2,1,0:T(8,128)} %dire.1) | copy-start | bytes 589828
  8.3 3.1 %collective-permute-start.4 = (f32[7,2,8,128]{3,2,1,0:T(8,128)S(1)}, f32[7,2,8,128]{3,2,1,0:T(8,128)S(1)}, u32[]{:S(2)}, u32[]{:S(2)}) collective-permute-start(f32[7,2,8,128]{3,2,1,0:T(8,128)S(1)} %get-tuple-element.23), channel_id=1, source_target_pairs={{8,20},{12,16},{16,12},{20,8},{9,21},{13,17},{17,13},{21,9},{10,22... | collective-permute-start | bytes 172040 | tf_op jit(solution)/shard_map/ppermute | solution.py:549
  12.0 4.1 %collective-permute-start.5 = (f32[11,8,128]{2,1,0:T(8,128)S(1)}, f32[11,8,128]{2,1,0:T(8,128)S(1)}, u32[]{:S(2)}, u32[]{:S(2)}) collective-permute-start(f32[11,8,128]{2,1,0:T(8,128)S(1)} %get-tuple-element.26), channel_id=1, source_target_pairs={{0,1},{1,0},{2,3},{3,2},{4,5},{5,4},{6,7},{7,6},{8,9},{9,8},{10,11... | collective-permute-start | bytes 135176 | tf_op jit(solution)/shard_map/ppermute | solution.py:557
  13.6 2.5 %collective-permute-start.6 = (f32[11,8,128]{2,1,0:T(8,128)S(1)}, f32[11,8,128]{2,1,0:T(8,128)S(1)}, u32[]{:S(2)}, u32[]{:S(2)}) collective-permute-start(f32[11,8,128]{2,1,0:T(8,128)S(1)} %get-tuple-element.27), channel_id=1, source_target_pairs={{1,2},{2,1},{5,6},{6,5},{9,10},{10,9},{13,14},{14,13},{17,18},{18,... | collective-permute-start | bytes 135176 | tf_op jit(solution)/shard_map/ppermute | solution.py:557
  36.3 1.2 %collective-permute-start.7 = (f32[1,128]{1,0:T(1,128)S(1)}, f32[1,128]{1,0:T(1,128)S(1)}, u32[]{:S(2)}, u32[]{:S(2)}) collective-permute-start(f32[1,128]{1,0:T(1,128)S(1)} %bitcast.1), channel_id=1, source_target_pairs={{0,8},{8,0},{16,24},{24,16},{1,9},{9,1},{17,25},{25,17},{2,10},{10... | collective-permute-start | bytes 1544 | tf_op jit(solution)/shard_map/ppermute | solution.py:565

commit v8 on v6

--- a/solution.py
+++ b/solution.py
@@ -240,7 +240,7 @@
                 if t != j:
                     below, above = roll(below, -4, 1), roll(above, 4, 1)
                 around[t // 3, 8 * (t % 3) : 8 * (t % 3) + 8] = jnp.where(lows, below, above) * keep
-    parts = [jnp.zeros((16, 128), f32) for _ in range(4)]
+    parts = [jnp.zeros((8, 128), f32) for _ in range(4)]
     for plane_at in range(10):
         X = plane_at + 3
         for g, f in enumerate(fields):
@@ -260,74 +260,74 @@
         if x < 0:
             continue
         n = x + 1
-        mid = [shifts[g, 1, 1, n] for g in range(4)]
-        classes = {1: [None] * 3, 2: [None] * 3, 3: [None] * 3}
-        faces = [None] * 3
-        edges = [None] * 3
-        corners = None
-
-        def add(old, new):
-            return new if old is None else old + new
-
-        for o in neighbour_offsets:
-            near = [shifts[g, 1 + o[1], 1 + o[2], n + o[0]] for g in range(4)]
-            norm = sum(abs(c) for c in o)
-            weight = mid[3] + near[3]
-            d = [mid[c] - near[c] for c in range(3)]
-            acc = classes[norm]
-            if norm == 1:
-                c0 = [c for c in range(3) if o[c] != 0][0]
-                faces[c0] = add(faces[c0], near[3])
-                for c in range(3):
-                    acc[c] = add(acc[c], weight * (d[c] + d[c] if c == c0 else d[c]))
-            else:
-                along = None
-                for c in range(3):
-                    if o[c] != 0:
-                        term = d[c]
-                        if along is None:
-                            along, sign = term, o[c]
+        for at in (slice(0, 8), slice(8, 16)):
+            mid = [shifts[g, 1, 1, n, at] for g in range(4)]
+            classes = {1: [None] * 3, 2: [None] * 3, 3: [None] * 3}
+            faces = [None] * 3
+            edges = [None] * 3
+            corners = None
+
+            def add(old, new):
+                return new if old is None else old + new
+
+            for o in neighbour_offsets:
+                near = [shifts[g, 1 + o[1], 1 + o[2], n + o[0], at] for g in range(4)]
+                norm = sum(abs(c) for c in o)
+                weight = mid[3] + near[3]
+                d = [mid[c] - near[c] for c in range(3)]
+                acc = classes[norm]
+                if norm == 1:
+                    c0 = [c for c in range(3) if o[c] != 0][0]
+                    faces[c0] = add(faces[c0], near[3])
+                    for c in range(3):
+                        acc[c] = add(acc[c], weight * (d[c] + d[c] if c == c0 else d[c]))
+                else:
+                    along = None
+                    for c in range(3):
+                        if o[c] != 0:
+                            term = d[c]
+                            if along is None:
+                                along, sign = term, o[c]
+                            else:
+                                along = along + term if o[c] == sign else along - term
+                    along = along * (1.0 / norm)
+                    for c in range(3):
+                        if o[c] == 0:
+                            pulled = d[c]
+                        elif o[c] == sign:
+                            pulled = d[c] + along
                         else:
-                            along = along + term if o[c] == sign else along - term
-                along = along * (1.0 / norm)
-                for c in range(3):
-                    if o[c] == 0:
-                        pulled = d[c]
-                    elif o[c] == sign:
-                        pulled = d[c] + along
+                            pulled = d[c] - along
+                        acc[c] = add(acc[c], weight * pulled)
+                    if norm == 2:
+                        c0 = [c for c in range(3) if o[c] == 0][0]
+                        edges[c0] = add(edges[c0], near[3])
                     else:
-                        pulled = d[c] - along
-                    acc[c] = add(acc[c], weight * pulled)
-                if norm == 2:
-                    c0 = [c for c in range(3) if o[c] == 0][0]
-                    edges[c0] = add(edges[c0], near[3])
-                else:
-                    corners = add(corners, near[3])
-        s0 = mid[3]
-        all_faces = faces[0] + faces[1] + faces[2]
-        all_edges = edges[0] + edges[1] + edges[2]
-        common = (all_faces + 6.0 * s0) + 0.75 * (all_edges + 12.0 * s0) + (4.0 / 9.0) * (corners + 8.0 * s0)
-        label = lab[x]
-        for c in range(3):
-            diag = 0.5 * (common + (faces[c] + 2.0 * s0) - 0.25 * (edges[c] + 4.0 * s0))
-            fixed = (label == 1) if c < 2 else (label >= 1)
-            total = 0.5 * classes[1][c] + 0.25 * classes[2][c] + (1.0 / 6.0) * classes[3][c]
-            total = jnp.where(fixed, 0.0, total)
-            inv = 1.0 / jnp.where(fixed, 1.0, diag)
-            r = res[c, x]
-            zeta = r * inv
-            scaled = total * inv
-            image[c, x] = total
-            inverse[c, x] = inv
-            parts[0] = parts[0] + r * zeta
-            parts[1] = parts[1] + mid[c] * total
-            parts[2] = parts[2] + r * scaled
-            parts[3] = parts[3] + total * scaled
+                        corners = add(corners, near[3])
+            s0 = mid[3]
+            all_faces = faces[0] + faces[1] + faces[2]
+            all_edges = edges[0] + edges[1] + edges[2]
+            common = (all_faces + 6.0 * s0) + 0.75 * (all_edges + 12.0 * s0) + (4.0 / 9.0) * (corners + 8.0 * s0)
+            label = lab[x, at]
+            for c in range(3):
+                diag = 0.5 * (common + (faces[c] + 2.0 * s0) - 0.25 * (edges[c] + 4.0 * s0))
+                fixed = (label == 1) if c < 2 else (label >= 1)
+                total = 0.5 * classes[1][c] + 0.25 * classes[2][c] + (1.0 / 6.0) * classes[3][c]
+                total = jnp.where(fixed, 0.0, total)
+                inv = 1.0 / jnp.where(fixed, 1.0, diag)
+                r = res[c, x, at]
+                zeta = r * inv
+                scaled = total * inv
+                image[c, x, at] = total
+                inverse[c, x, at] = inv
+                parts[0] = parts[0] + r * zeta
+                parts[1] = parts[1] + mid[c] * total
+                parts[2] = parts[2] + r * scaled
+                parts[3] = parts[3] + total * scaled
     place = lanes_of((1, 128)) // 32
     row = None
     for k in range(4):
-        part = parts[k][0:8] + parts[k][8:16]
-        part = part + roll(part, 64, 1)
+        part = parts[k] + roll(parts[k], 64, 1)
         part = jnp.sum(part + roll(part, 32, 1), axis=0, keepdims=True)
         row = part if k == 0 else jnp.where(place == k, part, row)
     sums[...] = jnp.broadcast_to(row[None], sums.shape)
@@ -436,21 +436,23 @@
         if X == 11:
             copies[2].start()
 
-    acc = [[None] * 4 for _ in range(16)]
+    acc = [[[None] * 3 for _ in range(4)] for _ in range(16)]
 
     def pair_up(X):
-        for o, field0, frame0, field1, frame1 in pairs:
-            to = X + o[0]
-            if not 0 <= to < 16 or not (1 <= X < 15 or 1 <= to < 15):
-                continue
-            g = quadratic([us[field0, c, X] - us[field1, c, to] for c in range(3)], o)
-            if 1 <= X < 15:
-                acc[X][frame0] = plus(acc[X][frame0], g)
-            if 1 <= to < 15:
-                acc[to][frame1] = plus(acc[to][frame1], g)
+        for r in range(3):
+            at = slice(8 * r, 8 * r + 8)
+            for o, field0, frame0, field1, frame1 in pairs:
+                to = X + o[0]
+                if not 0 <= to < 16 or not (1 <= X < 15 or 1 <= to < 15):
+                    continue
+                g = quadratic([us[field0, c, X, at] - us[field1, c, to, at] for c in range(3)], o)
+                if 1 <= X < 15:
+                    acc[X][frame0][r] = plus(acc[X][frame0][r], g)
+                if 1 <= to < 15:
+                    acc[to][frame1][r] = plus(acc[to][frame1][r], g)
 
     def filter_lines(X):
-        frames = acc[X]
+        frames = [jnp.concatenate(tiles, axis=0) for tiles in acc[X]]
         up = frames[1] + roll(frames[3], 1, 0)
         below = roll(side_low, 127 - (8 * X + 3), 1)
         up = roll(jnp.where(lane == 127, below, up), 1, 1)
@@ -553,12 +555,11 @@
     ends_got = [lax.ppermute(sends[r], "gz", swap_pairs((nz,), (r,))) for r in (0, 1)]
     image, inverse, sums, around = call(
         functools.partial(apply_operator, nz),
-        [field, field, (nx * ny, 1, 128), (7, 24, 128)],
+        [field, field, (nx * ny * nz, 1, 128), (7, 24, 128)],
         ext, *ends_got, residual, labels,
         scratch=[pltpu.VMEM((4, 3, 3, 10, 16, 128), f32)],
     )
-    in_plane = jnp.sum(lax.all_to_all(sums, plane, 0, 0), axis=0, keepdims=True)
-    total = lax.all_to_all(jnp.broadcast_to(in_plane, (nz, 1, 128)), "gz", 0, 0)
+    total = lax.all_to_all(sums, AXES, 0, 0)
     return tuple(
         call(
             finish_step,

time: 46.8 us -> 40.8 us (0.87)
  blocking collectives: 9.82 us -> 0 us
  starting transfers between devices: 16.8 us -> 19.5 us
  waiting for transfers between devices: 9.32 us -> 10.9 us
  local copies, waits for them, and re-layouts: 0.59 us -> 0.01 us
    all_to_all x1 -> x0, blocking collectives: 9.82 us -> none  [per_device(): in_plane = jnp.sum(lax.all_to_all(sums, plane, 0, 0), axis=0, keepdims=True)]
    all_to_all x1, starting transfers between devices: 7.3 us -> 9.94 us  [per_device(): total = lax.all_to_all(sums, AXES, 0, 0)]
    all_to_all x1, waiting for transfers between devices: 5.21 us -> 6.77 us  [per_device(): total = lax.all_to_all(sums, AXES, 0, 0)]
    broadcast_in_dim x1 -> x0, local copies, waits for them, and re-layouts: 0.58 us -> none  [per_device(): total = lax.all_to_all(jnp.broadcast_to(in_plane, (nz, 1, 128)), 'gz', 0, 0)]
where the time goes in v8:
time: 40.8 us; the launch traced here: 40.6 us
  starting transfers between devices  19.5 us (48%)
  waiting for transfers between devices  10.9 us (27%)
  Pallas kernels  9.53 us (23%)
  between operations  0.72 us (2%)
    all_to_all x1, starting transfers between devices, per_device(): total = lax.all_to_all(sums, AXES, 0, 0)  9.94 us
    pallas_call x5, Pallas kernels, call(): pl.pallas_call(body, out_shape=[jax.ShapeDtypeStruct(shape, f32) for shap...  9.53 us
    all_to_all x1, waiting for transfers between devices, per_device(): total = lax.all_to_all(sums, AXES, 0, 0)  6.77 us
    ppermute x3, starting transfers between devices, per_device(): strips.append(lax.ppermute(array, plane, swap_pairs((nx, ny), (turn, s))))  6.06 us
    ppermute x3, waiting for transfers between devices, per_device(): strips.append(lax.ppermute(array, plane, swap_pairs((nx, ny), (turn, s))))  2.3 us
    ppermute x2, starting transfers between devices, per_device(): lax.ppermute(sends[r], 'gz', swap_pairs((nz,), (r,)))  2.29 us
    ppermute x2, waiting for transfers between devices, per_device(): lax.ppermute(sends[r], 'gz', swap_pairs((nz,), (r,)))  1.81 us
    ppermute x2, starting transfers between devices, per_device(): lax.ppermute(halves[r], plane, swap_pairs((nx, ny), (r, None)))  1.18 us
  transfers between devices with their start and end apart: 8, of which 3 were waited for; matrix products, arithmetic and copies ran while one was open for 0% of the time, Pallas kernels for 1%

profile of v8, /device:TPU:0, one launch (start us, length us, event | category | flops | bytes accessed | tf_op | source)
XLA Modules:
  0.0 40.6 jit_solution(15381493691487229775)
XLA Ops:
  0.6 0.0 copy-start.2
  0.6 0.0 copy-start.1
  0.7 1.2 %shard_map.84 = (f32[7,4,16,128]{3,2,1,0:T(8,128)S(1)}, f32[7,4,16,128]{3,2,1,0:T(8,128)S(1)}, f32[7,4,8,128]{3,2,1,0:T(8,128)S(1)}, f32[7,2,8,128]{3,2,1,0:T(8,128)S(1)}, f32[7,2,8,128]{3,2,1,0:T(8,128)S(1)}) custom-call(f32[3,8,16,128]{3,2,1,0:T(8,128)} %sol_any.1, f32[3,8,16,128]{3,2,1,0:T(8,128)} %dire.1, f32[8,16,128]{2,1,0:T(8,128)} %den_any.1, ...), custom_call_target="tpu_custom_call" | custom-call | flops 20000000 | bytes 20000 | tf_op jit(solution)/shard_map/pallas_call | solution.py:49
  1.9 0.5 %collective-permute-start = (f32[7,4,16,128]{3,2,1,0:T(8,128)S(1)}, f32[7,4,16,128]{3,2,1,0:T(8,128)S(1)}, u32[]{:S(2)}, u32[]{:S(2)}) collective-permute-start(f32[7,4,16,128]{3,2,1,0:T(8,128)S(1)} %get-tuple-element.19.half0), channel_id=1, source_target_pairs={{0,8},{4,12},{8,0},{12,4},{16,24},{20,28},{24,16},{28,20},{1,9},{5... | collective-permute-start | bytes 688136 | tf_op jit(solution)/shard_map/ppermute | solution.py:543
  2.4 0.7 %collective-permute-start.1 = (f32[7,4,16,128]{3,2,1,0:T(8,128)S(1)}, f32[7,4,16,128]{3,2,1,0:T(8,128)S(1)}, u32[]{:S(2)}, u32[]{:S(2)}) collective-permute-start(f32[7,4,16,128]{3,2,1,0:T(8,128)S(1)} %get-tuple-element.20.half1), channel_id=1, source_target_pairs={{8,16},{12,20},{16,8},{20,12},{9,17},{13,21},{17,9},{21,13},{10,18... | collective-permute-start | bytes 688136 | tf_op jit(solution)/shard_map/ppermute | solution.py:543
  3.0 2.6 %collective-permute-start.2 = (f32[7,4,8,128]{3,2,1,0:T(8,128)S(1)}, f32[7,4,8,128]{3,2,1,0:T(8,128)S(1)}, u32[]{:S(2)}, u32[]{:S(2)}) collective-permute-start(f32[7,4,8,128]{3,2,1,0:T(8,128)S(1)} %get-tuple-element.21), channel_id=1, source_target_pairs={{0,4},{4,0},{8,12},{12,8},{16,20},{20,16},{24,28},{28,24},{1,5},{5... | collective-permute-start | bytes 344072 | tf_op jit(solution)/shard_map/ppermute | solution.py:547
  5.6 2.7 %collective-permute-start.3 = (f32[7,2,8,128]{3,2,1,0:T(8,128)S(1)}, f32[7,2,8,128]{3,2,1,0:T(8,128)S(1)}, u32[]{:S(2)}, u32[]{:S(2)}) collective-permute-start(f32[7,2,8,128]{3,2,1,0:T(8,128)S(1)} %get-tuple-element.22), channel_id=1, source_target_pairs={{0,12},{4,8},{8,4},{12,0},{16,28},{20,24},{24,20},{28,16},{1,13},{... | collective-permute-start | bytes 172040 | tf_op jit(solution)/shard_map/ppermute | solution.py:547
  8.3 0.0 copy-start
  8.3 0.8 %collective-permute-start.4 = (f32[7,2,8,128]{3,2,1,0:T(8,128)S(1)}, f32[7,2,8,128]{3,2,1,0:T(8,128)S(1)}, u32[]{:S(2)}, u32[]{:S(2)}) collective-permute-start(f32[7,2,8,128]{3,2,1,0:T(8,128)S(1)} %get-tuple-element.23), channel_id=1, source_target_pairs={{8,20},{12,16},{16,12},{20,8},{9,21},{13,17},{17,13},{21,9},{10,22... | collective-permute-start | bytes 172040 | tf_op jit(solution)/shard_map/ppermute | solution.py:547
  9.1 2.3 %collective-permute-done.3.refs_1_ = f32[7,2,8,128]{3,2,1,0:T(8,128)S(1)} collective-permute-done((f32[7,2,8,128]{3,2,1,0:T(8,128)S(1)}, f32[7,2,8,128]{3,2,1,0:T(8,128)S(1)}, u32[]{:S(2)}, u32[]{:S(2)}) %collective-permute-start.3) | collective-permute-done | bytes 57376 | tf_op jit(solution)/shard_map/ppermute | solution.py:547
  11.4 0.0 collective-permute-done.4.refs_2_
  11.4 0.0 collective-permute-done.2.refs_0_
  11.4 0.0 collective-permute-done.got0
  11.4 0.0 collective-permute-done.1.got1
  11.4 0.5 %shard_map.85 = (f32[7,16,24,128]{3,2,1,0:T(8,128)S(1)}, f32[7,24,128]{2,1,0:T(8,128)S(1)}, f32[11,8,128]{2,1,0:T(8,128)S(1)}, f32[11,8,128]{2,1,0:T(8,128)S(1)}) custom-call(f32[7,4,16,128]{3,2,1,0:T(8,128)S(1)} %get-tuple-element.19.half0, f32[7,4,16,128]{3,2,1,0:T(8,128)S(1)} %get-tuple-element.20.half1, f32[7,4,16,128]{3,2,1,0:T(8,128)S(1)} %collective-permute-done.got0, ...), custom_call_target="tpu_custom_call" | custom-call | flops 20000000 | bytes 20000 | tf_op jit(solution)/shard_map/pallas_call | solution.py:49
  12.0 1.6 %collective-permute-start.5 = (f32[11,8,128]{2,1,0:T(8,128)S(1)}, f32[11,8,128]{2,1,0:T(8,128)S(1)}, u32[]{:S(2)}, u32[]{:S(2)}) collective-permute-start(f32[11,8,128]{2,1,0:T(8,128)S(1)} %get-tuple-element.26), channel_id=1, source_target_pairs={{0,1},{1,0},{2,3},{3,2},{4,5},{5,4},{6,7},{7,6},{8,9},{9,8},{10,11... | collective-permute-start | bytes 135176 | tf_op jit(solution)/shard_map/ppermute | solution.py:555
  13.6 0.7 %collective-permute-start.6 = (f32[11,8,128]{2,1,0:T(8,128)S(1)}, f32[11,8,128]{2,1,0:T(8,128)S(1)}, u32[]{:S(2)}, u32[]{:S(2)}) collective-permute-start(f32[11,8,128]{2,1,0:T(8,128)S(1)} %get-tuple-element.27), channel_id=1, source_target_pairs={{1,2},{2,1},{5,6},{6,5},{9,10},{10,9},{13,14},{14,13},{17,18},{18,... | collective-permute-start | bytes 135176 | tf_op jit(solution)/shard_map/ppermute | solution.py:555
  14.3 1.8 %collective-permute-done.5.got0 = f32[11,8,128]{2,1,0:T(8,128)S(1)} collective-permute-done((f32[11,8,128]{2,1,0:T(8,128)S(1)}, f32[11,8,128]{2,1,0:T(8,128)S(1)}, u32[]{:S(2)}, u32[]{:S(2)}) %collective-permute-start.5) | collective-permute-done | bytes 45088 | tf_op jit(solution)/shard_map/ppermute | solution.py:555
  16.1 0.0 collective-permute-done.6.got1
  16.1 0.0 copy-done.2
  16.1 0.0 copy-done.1
  16.1 2.7 %shard_map.86 = (f32[3,8,16,128]{3,2,1,0:T(8,128)S(1)}, f32[3,8,16,128]{3,2,1,0:T(8,128)S(1)}, f32[32,1,128]{2,1,0:T(1,128)}, f32[7,24,128]{2,1,0:T(8,128)S(1)}) custom-call(f32[7,16,24,128]{3,2,1,0:T(8,128)S(1)} %get-tuple-element.24.ext, f32[11,8,128]{2,1,0:T(8,128)S(1)} %collective-permute-done.5.got0, f32[11,8,128]{2,1,0:T(8,128)S(1)} %collective-permute-done.6.got1, ...), custom_call_target="tpu_custom_call" | custom-call | flops 20000000 | bytes 20000 | tf_op jit(solution)/shard_map/pallas_call | solution.py:49
  18.8 9.9 %all-to-all-start = ((f32[32,1,128]{2,1,0:T(1,128)}), f32[32,1,128]{2,1,0:T(1,128)S(1)}, u32[]{:S(2)}, u32[]{:S(2)}) async-start(f32[32,1,128]{2,1,0:T(1,128)} %get-tuple-element.29), calls=%async_computation | async-start | bytes 32768 | tf_op jit(solution)/shard_map/all_to_all | solution.py:562
  28.7 0.3 shard_map.87
  29.0 6.8 %all-to-all-done.total = f32[32,1,128]{2,1,0:T(1,128)S(1)} async-done(((f32[32,1,128]{2,1,0:T(1,128)}), f32[32,1,128]{2,1,0:T(1,128)S(1)}, u32[]{:S(2)}, u32[]{:S(2)}) %all-to-all-start) | async-done | bytes 16416 | tf_op jit(solution)/shard_map/all_to_all | solution.py:562
  35.8 0.0 copy-done
  35.8 4.8 %shard_map.88 = (f32[3,8,16,128]{3,2,1,0:T(8,128)}, f32[3,8,16,128]{3,2,1,0:T(8,128)}, f32[3,8,16,128]{3,2,1,0:T(8,128)}, f32[8,16,128]{2,1,0:T(8,128)}) custom-call(f32[7,16,24,128]{3,2,1,0:T(8,128)S(1)} %get-tuple-element.24.ext, f32[7,24,128]{2,1,0:T(8,128)S(1)} %get-tuple-element.25.ends, f32[7,24,128]{2,1,0:T(8,128)S(1)} %get-tuple-element.28.around, ...), custom_call_target="tpu_custom_call" | custom-call | flops 20000000 | bytes 20000 | tf_op jit(solution)/shard_map/pallas_call | solution.py:49
Async XLA Ops:
  0.6 15.5 %copy-start.2 = (s32[8,16,128]{2,1,0:T(8,128)S(1)}, s32[8,16,128]{2,1,0:T(8,128)}, u32[]{:S(2)}) copy-start(s32[8,16,128]{2,1,0:T(8,128)} %lab.1) | copy-start | bytes 196612
  0.6 15.4 %copy-start.1 = (f32[3,8,16,128]{3,2,1,0:T(8,128)S(1)}, f32[3,8,16,128]{3,2,1,0:T(8,128)}, u32[]{:S(2)}) copy-start(f32[3,8,16,128]{3,2,1,0:T(8,128)} %res.3) | copy-start | bytes 589828
  1.9 9.6 %collective-permute-start = (f32[7,4,16,128]{3,2,1,0:T(8,128)S(1)}, f32[7,4,16,128]{3,2,1,0:T(8,128)S(1)}, u32[]{:S(2)}, u32[]{:S(2)}) collective-permute-start(f32[7,4,16,128]{3,2,1,0:T(8,128)S(1)} %get-tuple-element.19.half0), channel_id=1, source_target_pairs={{0,8},{4,12},{8,0},{12,4},{16,24},{20,28},{24,16},{28,20},{1,9},{5... | collective-permute-start | bytes 688136 | tf_op jit(solution)/shard_map/ppermute | solution.py:543
  2.4 9.0 %collective-permute-start.1 = (f32[7,4,16,128]{3,2,1,0:T(8,128)S(1)}, f32[7,4,16,128]{3,2,1,0:T(8,128)S(1)}, u32[]{:S(2)}, u32[]{:S(2)}) collective-permute-start(f32[7,4,16,128]{3,2,1,0:T(8,128)S(1)} %get-tuple-element.20.half1), channel_id=1, source_target_pairs={{8,16},{12,20},{16,8},{20,12},{9,17},{13,21},{17,9},{21,13},{10,18... | collective-permute-start | bytes 688136 | tf_op jit(solution)/shard_map/ppermute | solution.py:543
  3.0 8.4 %collective-permute-start.2 = (f32[7,4,8,128]{3,2,1,0:T(8,128)S(1)}, f32[7,4,8,128]{3,2,1,0:T(8,128)S(1)}, u32[]{:S(2)}, u32[]{:S(2)}) collective-permute-start(f32[7,4,8,128]{3,2,1,0:T(8,128)S(1)} %get-tuple-element.21), channel_id=1, source_target_pairs={{0,4},{4,0},{8,12},{12,8},{16,20},{20,16},{24,28},{28,24},{1,5},{5... | collective-permute-start | bytes 344072 | tf_op jit(solution)/shard_map/ppermute | solution.py:547
  5.6 5.8 %collective-permute-start.3 = (f32[7,2,8,128]{3,2,1,0:T(8,128)S(1)}, f32[7,2,8,128]{3,2,1,0:T(8,128)S(1)}, u32[]{:S(2)}, u32[]{:S(2)}) collective-permute-start(f32[7,2,8,128]{3,2,1,0:T(8,128)S(1)} %get-tuple-element.22), channel_id=1, source_target_pairs={{0,12},{4,8},{8,4},{12,0},{16,28},{20,24},{24,20},{28,16},{1,13},{... | collective-permute-start | bytes 172040 | tf_op jit(solution)/shard_map/ppermute | solution.py:547
  8.3 27.5 %copy-start = (f32[3,8,16,128]{3,2,1,0:T(8,128)S(1)}, f32[3,8,16,128]{3,2,1,0:T(8,128)}, u32[]{:S(2)}) copy-start(f32[3,8,16,128]{3,2,1,0:T(8,128)} %dire.1) | copy-start | bytes 589828
  8.3 3.1 %collective-permute-start.4 = (f32[7,2,8,128]{3,2,1,0:T(8,128)S(1)}, f32[7,2,8,128]{3,2,1,0:T(8,128)S(1)}, u32[]{:S(2)}, u32[]{:S(2)}) collective-permute-start(f32[7,2,8,128]{3,2,1,0:T(8,128)S(1)} %get-tuple-element.23), channel_id=1, source_target_pairs={{8,20},{12,16},{16,12},{20,8},{9,21},{13,17},{17,13},{21,9},{10,22... | collective-permute-start | bytes 172040 | tf_op jit(solution)/shard_map/ppermute | solution.py:547
  12.0 4.1 %collective-permute-start.5 = (f32[11,8,128]{2,1,0:T(8,128)S(1)}, f32[11,8,128]{2,1,0:T(8,128)S(1)}, u32[]{:S(2)}, u32[]{:S(2)}) collective-permute-start(f32[11,8,128]{2,1,0:T(8,128)S(1)} %get-tuple-element.26), channel_id=1, source_target_pairs={{0,1},{1,0},{2,3},{3,2},{4,5},{5,4},{6,7},{7,6},{8,9},{9,8},{10,11... | collective-permute-start | bytes 135176 | tf_op jit(solution)/shard_map/ppermute | solution.py:555
  13.6 2.5 %collective-permute-start.6 = (f32[11,8,128]{2,1,0:T(8,128)S(1)}, f32[11,8,128]{2,1,0:T(8,128)S(1)}, u32[]{:S(2)}, u32[]{:S(2)}) collective-permute-start(f32[11,8,128]{2,1,0:T(8,128)S(1)} %get-tuple-element.27), channel_id=1, source_target_pairs={{1,2},{2,1},{5,6},{6,5},{9,10},{10,9},{13,14},{14,13},{17,18},{18,... | collective-permute-start | bytes 135176 | tf_op jit(solution)/shard_map/ppermute | solution.py:555
  18.8 17.0 %all-to-all-start = ((f32[32,1,128]{2,1,0:T(1,128)}), f32[32,1,128]{2,1,0:T(1,128)S(1)}, u32[]{:S(2)}, u32[]{:S(2)}) async-start(f32[32,1,128]{2,1,0:T(1,128)} %get-tuple-element.29), calls=%async_computation | async-start | bytes 32768 | tf_op jit(solution)/shard_map/all_to_all | solution.py:562

commit v9 on v6

--- a/solution.py
+++ b/solution.py
@@ -436,21 +436,23 @@
         if X == 11:
             copies[2].start()
 
-    acc = [[None] * 4 for _ in range(16)]
+    acc = [[[None] * 3 for _ in range(4)] for _ in range(16)]
 
     def pair_up(X):
-        for o, field0, frame0, field1, frame1 in pairs:
-            to = X + o[0]
-            if not 0 <= to < 16 or not (1 <= X < 15 or 1 <= to < 15):
-                continue
-            g = quadratic([us[field0, c, X] - us[field1, c, to] for c in range(3)], o)
-            if 1 <= X < 15:
-                acc[X][frame0] = plus(acc[X][frame0], g)
-            if 1 <= to < 15:
-                acc[to][frame1] = plus(acc[to][frame1], g)
+        for r in range(3):
+            at = slice(8 * r, 8 * r + 8)
+            for o, field0, frame0, field1, frame1 in pairs:
+                to = X + o[0]
+                if not 0 <= to < 16 or not (1 <= X < 15 or 1 <= to < 15):
+                    continue
+                g = quadratic([us[field0, c, X, at] - us[field1, c, to, at] for c in range(3)], o)
+                if 1 <= X < 15:
+                    acc[X][frame0][r] = plus(acc[X][frame0][r], g)
+                if 1 <= to < 15:
+                    acc[to][frame1][r] = plus(acc[to][frame1][r], g)
 
     def filter_lines(X):
-        frames = acc[X]
+        frames = [jnp.concatenate(tiles, axis=0) for tiles in acc[X]]
         up = frames[1] + roll(frames[3], 1, 0)
         below = roll(side_low, 127 - (8 * X + 3), 1)
         up = roll(jnp.where(lane == 127, below, up), 1, 1)
@@ -553,12 +555,11 @@
     ends_got = [lax.ppermute(sends[r], "gz", swap_pairs((nz,), (r,))) for r in (0, 1)]
     image, inverse, sums, around = call(
         functools.partial(apply_operator, nz),
-        [field, field, (nx * ny, 1, 128), (7, 24, 128)],
+        [field, field, (nx * ny * nz, 1, 128), (7, 24, 128)],
         ext, *ends_got, residual, labels,
         scratch=[pltpu.VMEM((4, 3, 3, 10, 16, 128), f32)],
     )
-    in_plane = jnp.sum(lax.all_to_all(sums, plane, 0, 0), axis=0, keepdims=True)
-    total = lax.all_to_all(jnp.broadcast_to(in_plane, (nz, 1, 128)), "gz", 0, 0)
+    total = lax.all_to_all(sums, AXES, 0, 0)
     return tuple(
         call(
             finish_step,

time: 46.8 us -> 40.9 us (0.87)
  blocking collectives: 9.82 us -> 0 us
  starting transfers between devices: 16.8 us -> 19.5 us
  waiting for transfers between devices: 9.32 us -> 10.9 us
  local copies, waits for them, and re-layouts: 0.59 us -> 0.01 us
    all_to_all x1 -> x0, blocking collectives: 9.82 us -> none  [per_device(): in_plane = jnp.sum(lax.all_to_all(sums, plane, 0, 0), axis=0, keepdims=True)]
    all_to_all x1, starting transfers between devices: 7.3 us -> 9.94 us  [per_device(): total = lax.all_to_all(sums, AXES, 0, 0)]
    all_to_all x1, waiting for transfers between devices: 5.21 us -> 6.77 us  [per_device(): total = lax.all_to_all(sums, AXES, 0, 0)]
    broadcast_in_dim x1 -> x0, local copies, waits for them, and re-layouts: 0.58 us -> none  [per_device(): total = lax.all_to_all(jnp.broadcast_to(in_plane, (nz, 1, 128)), 'gz', 0, 0)]
where the time goes in v9:
time: 40.9 us; the launch traced here: 40.6 us
  starting transfers between devices  19.5 us (48%)
  waiting for transfers between devices  10.9 us (27%)
  Pallas kernels  9.55 us (23%)
  between operations  0.72 us (2%)
    all_to_all x1, starting transfers between devices, per_device(): total = lax.all_to_all(sums, AXES, 0, 0)  9.94 us
    pallas_call x5, Pallas kernels, call(): pl.pallas_call(body, out_shape=[jax.ShapeDtypeStruct(shape, f32) for shap...  9.55 us
    all_to_all x1, waiting for transfers between devices, per_device(): total = lax.all_to_all(sums, AXES, 0, 0)  6.77 us
    ppermute x3, starting transfers between devices, per_device(): strips.append(lax.ppermute(array, plane, swap_pairs((nx, ny), (turn, s))))  6.06 us
    ppermute x3, waiting for transfers between devices, per_device(): strips.append(lax.ppermute(array, plane, swap_pairs((nx, ny), (turn, s))))  2.3 us
    ppermute x2, starting transfers between devices, per_device(): lax.ppermute(sends[r], 'gz', swap_pairs((nz,), (r,)))  2.29 us
    ppermute x2, waiting for transfers between devices, per_device(): lax.ppermute(sends[r], 'gz', swap_pairs((nz,), (r,)))  1.81 us
    ppermute x2, starting transfers between devices, per_device(): lax.ppermute(halves[r], plane, swap_pairs((nx, ny), (r, None)))  1.18 us
  transfers between devices with their start and end apart: 8, of which 3 were waited for; matrix products, arithmetic and copies ran while one was open for 0% of the time, Pallas kernels for 1%

profile of v9, /device:TPU:0, one launch (start us, length us, event | category | flops | bytes accessed | tf_op | source)
XLA Modules:
  0.0 40.6 jit_solution(7496611210137325772)
XLA Ops:
  0.6 0.0 copy-start.2
  0.6 0.0 copy-start.1
  0.7 1.2 %shard_map.84 = (f32[7,4,16,128]{3,2,1,0:T(8,128)S(1)}, f32[7,4,16,128]{3,2,1,0:T(8,128)S(1)}, f32[7,4,8,128]{3,2,1,0:T(8,128)S(1)}, f32[7,2,8,128]{3,2,1,0:T(8,128)S(1)}, f32[7,2,8,128]{3,2,1,0:T(8,128)S(1)}) custom-call(f32[3,8,16,128]{3,2,1,0:T(8,128)} %sol_any.1, f32[3,8,16,128]{3,2,1,0:T(8,128)} %dire.1, f32[8,16,128]{2,1,0:T(8,128)} %den_any.1, ...), custom_call_target="tpu_custom_call" | custom-call | flops 20000000 | bytes 20000 | tf_op jit(solution)/shard_map/pallas_call | solution.py:49
  1.9 0.5 %collective-permute-start = (f32[7,4,16,128]{3,2,1,0:T(8,128)S(1)}, f32[7,4,16,128]{3,2,1,0:T(8,128)S(1)}, u32[]{:S(2)}, u32[]{:S(2)}) collective-permute-start(f32[7,4,16,128]{3,2,1,0:T(8,128)S(1)} %get-tuple-element.19.half0), channel_id=1, source_target_pairs={{0,8},{4,12},{8,0},{12,4},{16,24},{20,28},{24,16},{28,20},{1,9},{5... | collective-permute-start | bytes 688136 | tf_op jit(solution)/shard_map/ppermute | solution.py:543
  2.4 0.7 %collective-permute-start.1 = (f32[7,4,16,128]{3,2,1,0:T(8,128)S(1)}, f32[7,4,16,128]{3,2,1,0:T(8,128)S(1)}, u32[]{:S(2)}, u32[]{:S(2)}) collective-permute-start(f32[7,4,16,128]{3,2,1,0:T(8,128)S(1)} %get-tuple-element.20.half1), channel_id=1, source_target_pairs={{8,16},{12,20},{16,8},{20,12},{9,17},{13,21},{17,9},{21,13},{10,18... | collective-permute-start | bytes 688136 | tf_op jit(solution)/shard_map/ppermute | solution.py:543
  3.0 2.6 %collective-permute-start.2 = (f32[7,4,8,128]{3,2,1,0:T(8,128)S(1)}, f32[7,4,8,128]{3,2,1,0:T(8,128)S(1)}, u32[]{:S(2)}, u32[]{:S(2)}) collective-permute-start(f32[7,4,8,128]{3,2,1,0:T(8,128)S(1)} %get-tuple-element.21), channel_id=1, source_target_pairs={{0,4},{4,0},{8,12},{12,8},{16,20},{20,16},{24,28},{28,24},{1,5},{5... | collective-permute-start | bytes 344072 | tf_op jit(solution)/shard_map/ppermute | solution.py:547
  5.6 2.7 %collective-permute-start.3 = (f32[7,2,8,128]{3,2,1,0:T(8,128)S(1)}, f32[7,2,8,128]{3,2,1,0:T(8,128)S(1)}, u32[]{:S(2)}, u32[]{:S(2)}) collective-permute-start(f32[7,2,8,128]{3,2,1,0:T(8,128)S(1)} %get-tuple-element.22), channel_id=1, source_target_pairs={{0,12},{4,8},{8,4},{12,0},{16,28},{20,24},{24,20},{28,16},{1,13},{... | collective-permute-start | bytes 172040 | tf_op jit(solution)/shard_map/ppermute | solution.py:547
  8.3 0.0 copy-start
  8.3 0.8 %collective-permute-start.4 = (f32[7,2,8,128]{3,2,1,0:T(8,128)S(1)}, f32[7,2,8,128]{3,2,1,0:T(8,128)S(1)}, u32[]{:S(2)}, u32[]{:S(2)}) collective-permute-start(f32[7,2,8,128]{3,2,1,0:T(8,128)S(1)} %get-tuple-element.23), channel_id=1, source_target_pairs={{8,20},{12,16},{16,12},{20,8},{9,21},{13,17},{17,13},{21,9},{10,22... | collective-permute-start | bytes 172040 | tf_op jit(solution)/shard_map/ppermute | solution.py:547
  9.1 2.3 %collective-permute-done.3.refs_1_ = f32[7,2,8,128]{3,2,1,0:T(8,128)S(1)} collective-permute-done((f32[7,2,8,128]{3,2,1,0:T(8,128)S(1)}, f32[7,2,8,128]{3,2,1,0:T(8,128)S(1)}, u32[]{:S(2)}, u32[]{:S(2)}) %collective-permute-start.3) | collective-permute-done | bytes 57376 | tf_op jit(solution)/shard_map/ppermute | solution.py:547
  11.4 0.0 collective-permute-done.4.refs_2_
  11.4 0.0 collective-permute-done.2.refs_0_
  11.4 0.0 collective-permute-done.got0
  11.4 0.0 collective-permute-done.1.got1
  11.4 0.5 %shard_map.85 = (f32[7,16,24,128]{3,2,1,0:T(8,128)S(1)}, f32[7,24,128]{2,1,0:T(8,128)S(1)}, f32[11,8,128]{2,1,0:T(8,128)S(1)}, f32[11,8,128]{2,1,0:T(8,128)S(1)}) custom-call(f32[7,4,16,128]{3,2,1,0:T(8,128)S(1)} %get-tuple-element.19.half0, f32[7,4,16,128]{3,2,1,0:T(8,128)S(1)} %get-tuple-element.20.half1, f32[7,4,16,128]{3,2,1,0:T(8,128)S(1)} %collective-permute-done.got0, ...), custom_call_target="tpu_custom_call" | custom-call | flops 20000000 | bytes 20000 | tf_op jit(solution)/shard_map/pallas_call | solution.py:49
  12.0 1.6 %collective-permute-start.5 = (f32[11,8,128]{2,1,0:T(8,128)S(1)}, f32[11,8,128]{2,1,0:T(8,128)S(1)}, u32[]{:S(2)}, u32[]{:S(2)}) collective-permute-start(f32[11,8,128]{2,1,0:T(8,128)S(1)} %get-tuple-element.26), channel_id=1, source_target_pairs={{0,1},{1,0},{2,3},{3,2},{4,5},{5,4},{6,7},{7,6},{8,9},{9,8},{10,11... | collective-permute-start | bytes 135176 | tf_op jit(solution)/shard_map/ppermute | solution.py:555
  13.6 0.7 %collective-permute-start.6 = (f32[11,8,128]{2,1,0:T(8,128)S(1)}, f32[11,8,128]{2,1,0:T(8,128)S(1)}, u32[]{:S(2)}, u32[]{:S(2)}) collective-permute-start(f32[11,8,128]{2,1,0:T(8,128)S(1)} %get-tuple-element.27), channel_id=1, source_target_pairs={{1,2},{2,1},{5,6},{6,5},{9,10},{10,9},{13,14},{14,13},{17,18},{18,... | collective-permute-start | bytes 135176 | tf_op jit(solution)/shard_map/ppermute | solution.py:555
  14.3 1.8 %collective-permute-done.5.got0 = f32[11,8,128]{2,1,0:T(8,128)S(1)} collective-permute-done((f32[11,8,128]{2,1,0:T(8,128)S(1)}, f32[11,8,128]{2,1,0:T(8,128)S(1)}, u32[]{:S(2)}, u32[]{:S(2)}) %collective-permute-start.5) | collective-permute-done | bytes 45088 | tf_op jit(solution)/shard_map/ppermute | solution.py:555
  16.1 0.0 collective-permute-done.6.got1
  16.1 0.0 copy-done.2
  16.1 0.0 copy-done.1
  16.1 2.7 %shard_map.86 = (f32[3,8,16,128]{3,2,1,0:T(8,128)S(1)}, f32[3,8,16,128]{3,2,1,0:T(8,128)S(1)}, f32[32,1,128]{2,1,0:T(1,128)}, f32[7,24,128]{2,1,0:T(8,128)S(1)}) custom-call(f32[7,16,24,128]{3,2,1,0:T(8,128)S(1)} %get-tuple-element.24.ext, f32[11,8,128]{2,1,0:T(8,128)S(1)} %collective-permute-done.5.got0, f32[11,8,128]{2,1,0:T(8,128)S(1)} %collective-permute-done.6.got1, ...), custom_call_target="tpu_custom_call" | custom-call | flops 20000000 | bytes 20000 | tf_op jit(solution)/shard_map/pallas_call | solution.py:49
  18.8 9.9 %all-to-all-start = ((f32[32,1,128]{2,1,0:T(1,128)}), f32[32,1,128]{2,1,0:T(1,128)S(1)}, u32[]{:S(2)}, u32[]{:S(2)}) async-start(f32[32,1,128]{2,1,0:T(1,128)} %get-tuple-element.29), calls=%async_computation | async-start | bytes 32768 | tf_op jit(solution)/shard_map/all_to_all | solution.py:562
  28.8 0.3 shard_map.87
  29.0 6.8 %all-to-all-done.total = f32[32,1,128]{2,1,0:T(1,128)S(1)} async-done(((f32[32,1,128]{2,1,0:T(1,128)}), f32[32,1,128]{2,1,0:T(1,128)S(1)}, u32[]{:S(2)}, u32[]{:S(2)}) %all-to-all-start) | async-done | bytes 16416 | tf_op jit(solution)/shard_map/all_to_all | solution.py:562
  35.8 0.0 copy-done
  35.8 4.8 %shard_map.88 = (f32[3,8,16,128]{3,2,1,0:T(8,128)}, f32[3,8,16,128]{3,2,1,0:T(8,128)}, f32[3,8,16,128]{3,2,1,0:T(8,128)}, f32[8,16,128]{2,1,0:T(8,128)}) custom-call(f32[7,16,24,128]{3,2,1,0:T(8,128)S(1)} %get-tuple-element.24.ext, f32[7,24,128]{2,1,0:T(8,128)S(1)} %get-tuple-element.25.ends, f32[7,24,128]{2,1,0:T(8,128)S(1)} %get-tuple-element.28.around, ...), custom_call_target="tpu_custom_call" | custom-call | flops 20000000 | bytes 20000 | tf_op jit(solution)/shard_map/pallas_call | solution.py:49
Async XLA Ops:
  0.6 15.5 %copy-start.2 = (s32[8,16,128]{2,1,0:T(8,128)S(1)}, s32[8,16,128]{2,1,0:T(8,128)}, u32[]{:S(2)}) copy-start(s32[8,16,128]{2,1,0:T(8,128)} %lab.1) | copy-start | bytes 196612
  0.6 15.4 %copy-start.1 = (f32[3,8,16,128]{3,2,1,0:T(8,128)S(1)}, f32[3,8,16,128]{3,2,1,0:T(8,128)}, u32[]{:S(2)}) copy-start(f32[3,8,16,128]{3,2,1,0:T(8,128)} %res.3) | copy-start | bytes 589828
  1.9 9.6 %collective-permute-start = (f32[7,4,16,128]{3,2,1,0:T(8,128)S(1)}, f32[7,4,16,128]{3,2,1,0:T(8,128)S(1)}, u32[]{:S(2)}, u32[]{:S(2)}) collective-permute-start(f32[7,4,16,128]{3,2,1,0:T(8,128)S(1)} %get-tuple-element.19.half0), channel_id=1, source_target_pairs={{0,8},{4,12},{8,0},{12,4},{16,24},{20,28},{24,16},{28,20},{1,9},{5... | collective-permute-start | bytes 688136 | tf_op jit(solution)/shard_map/ppermute | solution.py:543
  2.4 9.0 %collective-permute-start.1 = (f32[7,4,16,128]{3,2,1,0:T(8,128)S(1)}, f32[7,4,16,128]{3,2,1,0:T(8,128)S(1)}, u32[]{:S(2)}, u32[]{:S(2)}) collective-permute-start(f32[7,4,16,128]{3,2,1,0:T(8,128)S(1)} %get-tuple-element.20.half1), channel_id=1, source_target_pairs={{8,16},{12,20},{16,8},{20,12},{9,17},{13,21},{17,9},{21,13},{10,18... | collective-permute-start | bytes 688136 | tf_op jit(solution)/shard_map/ppermute | solution.py:543
  3.0 8.4 %collective-permute-start.2 = (f32[7,4,8,128]{3,2,1,0:T(8,128)S(1)}, f32[7,4,8,128]{3,2,1,0:T(8,128)S(1)}, u32[]{:S(2)}, u32[]{:S(2)}) collective-permute-start(f32[7,4,8,128]{3,2,1,0:T(8,128)S(1)} %get-tuple-element.21), channel_id=1, source_target_pairs={{0,4},{4,0},{8,12},{12,8},{16,20},{20,16},{24,28},{28,24},{1,5},{5... | collective-permute-start | bytes 344072 | tf_op jit(solution)/shard_map/ppermute | solution.py:547
  5.6 5.8 %collective-permute-start.3 = (f32[7,2,8,128]{3,2,1,0:T(8,128)S(1)}, f32[7,2,8,128]{3,2,1,0:T(8,128)S(1)}, u32[]{:S(2)}, u32[]{:S(2)}) collective-permute-start(f32[7,2,8,128]{3,2,1,0:T(8,128)S(1)} %get-tuple-element.22), channel_id=1, source_target_pairs={{0,12},{4,8},{8,4},{12,0},{16,28},{20,24},{24,20},{28,16},{1,13},{... | collective-permute-start | bytes 172040 | tf_op jit(solution)/shard_map/ppermute | solution.py:547
  8.3 27.5 %copy-start = (f32[3,8,16,128]{3,2,1,0:T(8,128)S(1)}, f32[3,8,16,128]{3,2,1,0:T(8,128)}, u32[]{:S(2)}) copy-start(f32[3,8,16,128]{3,2,1,0:T(8,128)} %dire.1) | copy-start | bytes 589828
  8.3 3.1 %collective-permute-start.4 = (f32[7,2,8,128]{3,2,1,0:T(8,128)S(1)}, f32[7,2,8,128]{3,2,1,0:T(8,128)S(1)}, u32[]{:S(2)}, u32[]{:S(2)}) collective-permute-start(f32[7,2,8,128]{3,2,1,0:T(8,128)S(1)} %get-tuple-element.23), channel_id=1, source_target_pairs={{8,20},{12,16},{16,12},{20,8},{9,21},{13,17},{17,13},{21,9},{10,22... | collective-permute-start | bytes 172040 | tf_op jit(solution)/shard_map/ppermute | solution.py:547
  12.0 4.1 %collective-permute-start.5 = (f32[11,8,128]{2,1,0:T(8,128)S(1)}, f32[11,8,128]{2,1,0:T(8,128)S(1)}, u32[]{:S(2)}, u32[]{:S(2)}) collective-permute-start(f32[11,8,128]{2,1,0:T(8,128)S(1)} %get-tuple-element.26), channel_id=1, source_target_pairs={{0,1},{1,0},{2,3},{3,2},{4,5},{5,4},{6,7},{7,6},{8,9},{9,8},{10,11... | collective-permute-start | bytes 135176 | tf_op jit(solution)/shard_map/ppermute | solution.py:555
  13.6 2.5 %collective-permute-start.6 = (f32[11,8,128]{2,1,0:T(8,128)S(1)}, f32[11,8,128]{2,1,0:T(8,128)S(1)}, u32[]{:S(2)}, u32[]{:S(2)}) collective-permute-start(f32[11,8,128]{2,1,0:T(8,128)S(1)} %get-tuple-element.27), channel_id=1, source_target_pairs={{1,2},{2,1},{5,6},{6,5},{9,10},{10,9},{13,14},{14,13},{17,18},{18,... | collective-permute-start | bytes 135176 | tf_op jit(solution)/shard_map/ppermute | solution.py:555
  18.8 17.0 %all-to-all-start = ((f32[32,1,128]{2,1,0:T(1,128)}), f32[32,1,128]{2,1,0:T(1,128)S(1)}, u32[]{:S(2)}, u32[]{:S(2)}) async-start(f32[32,1,128]{2,1,0:T(1,128)} %get-tuple-element.29), calls=%async_computation | async-start | bytes 32768 | tf_op jit(solution)/shard_map/all_to_all | solution.py:562

commit v10 on v9

--- a/solution.py
+++ b/solution.py
@@ -110,7 +110,7 @@
 
 def extend(counts, half0, half1, got0, got1, *refs):
     nx, ny, nz = counts
-    sides, (ext, ends, send0, send1) = refs[:-4], refs[-4:]
+    sides, (ext, ends, send1, send0) = refs[:-4], refs[-4:]
     sub = rows_of((8, 128))
     lane = lanes_of((24, 128))
     lows = lanes_of((8, 128)) % 8 < 4
@@ -225,7 +225,7 @@
         side[s] = finish(total, along_x, along_z)
 
 
-def apply_operator(nz, ext, got0, got1, res, lab, image, inverse, sums, around, shifts):
+def apply_operator(nz, ext, got1, got0, res, lab, image, inverse, sums, around, shifts):
     lane = lanes_of((24, 128))
     fields = (0, 1, 2, 6)
     iz = lax.axis_index("gz")
@@ -552,7 +552,9 @@
         [(7, 16, 24, 128), (7, 24, 128), zend, zend],
         *halves, *got, *strips,
     )
-    ends_got = [lax.ppermute(sends[r], "gz", swap_pairs((nz,), (r,))) for r in (0, 1)]
+    later = lax.ppermute(sends[0], "gz", swap_pairs((nz,), (1,)))
+    first = lax.ppermute(sends[1], "gz", swap_pairs((nz,), (0,)))
+    ends_got = [later, first]
     image, inverse, sums, around = call(
         functools.partial(apply_operator, nz),
         [field, field, (nx * ny * nz, 1, 128), (7, 24, 128)],

time: 40.9 us -> 39.9 us (0.976)
  starting transfers between devices: 19.5 us -> 18.3 us
    all_to_all x1, starting transfers between devices: 9.94 us -> 5.92 us  [per_device(): total = lax.all_to_all(sums, AXES, 0, 0)]
    ppermute x2, starting transfers between devices: 2.29 us -> 5.13 us  [the longest x1 4.46 us: per_device(): first = lax.ppermute(sends[1], 'gz', swap_pairs((nz,), (0,)))]
where the time goes in v10:
time: 39.9 us; the launch traced here: 39.7 us
  starting transfers between devices  18.3 us (46%)
  waiting for transfers between devices  11.1 us (28%)
  Pallas kernels  9.55 us (24%)
  between operations  0.72 us (2%)
    pallas_call x5, Pallas kernels, call(): pl.pallas_call(body, out_shape=[jax.ShapeDtypeStruct(shape, f32) for shap...  9.55 us
    all_to_all x1, waiting for transfers between devices, per_device(): total = lax.all_to_all(sums, AXES, 0, 0)  6.77 us
    ppermute x3, starting transfers between devices, per_device(): strips.append(lax.ppermute(array, plane, swap_pairs((nx, ny), (turn, s))))  6.06 us
    all_to_all x1, starting transfers between devices, per_device(): total = lax.all_to_all(sums, AXES, 0, 0)  5.92 us
    ppermute x1, starting transfers between devices, per_device(): first = lax.ppermute(sends[1], 'gz', swap_pairs((nz,), (0,)))  4.46 us
    ppermute x3, waiting for transfers between devices, per_device(): strips.append(lax.ppermute(array, plane, swap_pairs((nx, ny), (turn, s))))  2.3 us
    ppermute x1, waiting for transfers between devices, per_device(): first = lax.ppermute(sends[1], 'gz', swap_pairs((nz,), (0,)))  2.02 us
    ppermute x2, starting transfers between devices, per_device(): lax.ppermute(halves[r], plane, swap_pairs((nx, ny), (r, None)))  1.18 us
  transfers between devices with their start and end apart: 8, of which 3 were waited for; matrix products, arithmetic and copies ran while one was open for 0% of the time, Pallas kernels for 1%

profile of v10, /device:TPU:0, one launch (start us, length us, event | category | flops | bytes accessed | tf_op | source)
XLA Modules:
  0.0 39.7 jit_solution(15943287776660232251)
XLA Ops:
  0.6 0.0 copy-start.2
  0.6 0.0 copy-start.1
  0.7 1.2 %shard_map.84 = (f32[7,4,16,128]{3,2,1,0:T(8,128)S(1)}, f32[7,4,16,128]{3,2,1,0:T(8,128)S(1)}, f32[7,4,8,128]{3,2,1,0:T(8,128)S(1)}, f32[7,2,8,128]{3,2,1,0:T(8,128)S(1)}, f32[7,2,8,128]{3,2,1,0:T(8,128)S(1)}) custom-call(f32[3,8,16,128]{3,2,1,0:T(8,128)} %sol_any.1, f32[3,8,16,128]{3,2,1,0:T(8,128)} %dire.1, f32[8,16,128]{2,1,0:T(8,128)} %den_any.1, ...), custom_call_target="tpu_custom_call" | custom-call | flops 20000000 | bytes 20000 | tf_op jit(solution)/shard_map/pallas_call | solution.py:49
  1.9 0.5 %collective-permute-start = (f32[7,4,16,128]{3,2,1,0:T(8,128)S(1)}, f32[7,4,16,128]{3,2,1,0:T(8,128)S(1)}, u32[]{:S(2)}, u32[]{:S(2)}) collective-permute-start(f32[7,4,16,128]{3,2,1,0:T(8,128)S(1)} %get-tuple-element.19.half0), channel_id=1, source_target_pairs={{0,8},{4,12},{8,0},{12,4},{16,24},{20,28},{24,16},{28,20},{1,9},{5... | collective-permute-start | bytes 688136 | tf_op jit(solution)/shard_map/ppermute | solution.py:543
  2.4 0.7 %collective-permute-start.1 = (f32[7,4,16,128]{3,2,1,0:T(8,128)S(1)}, f32[7,4,16,128]{3,2,1,0:T(8,128)S(1)}, u32[]{:S(2)}, u32[]{:S(2)}) collective-permute-start(f32[7,4,16,128]{3,2,1,0:T(8,128)S(1)} %get-tuple-element.20.half1), channel_id=1, source_target_pairs={{8,16},{12,20},{16,8},{20,12},{9,17},{13,21},{17,9},{21,13},{10,18... | collective-permute-start | bytes 688136 | tf_op jit(solution)/shard_map/ppermute | solution.py:543
  3.0 2.6 %collective-permute-start.2 = (f32[7,4,8,128]{3,2,1,0:T(8,128)S(1)}, f32[7,4,8,128]{3,2,1,0:T(8,128)S(1)}, u32[]{:S(2)}, u32[]{:S(2)}) collective-permute-start(f32[7,4,8,128]{3,2,1,0:T(8,128)S(1)} %get-tuple-element.21), channel_id=1, source_target_pairs={{0,4},{4,0},{8,12},{12,8},{16,20},{20,16},{24,28},{28,24},{1,5},{5... | collective-permute-start | bytes 344072 | tf_op jit(solution)/shard_map/ppermute | solution.py:547
  5.6 2.7 %collective-permute-start.3 = (f32[7,2,8,128]{3,2,1,0:T(8,128)S(1)}, f32[7,2,8,128]{3,2,1,0:T(8,128)S(1)}, u32[]{:S(2)}, u32[]{:S(2)}) collective-permute-start(f32[7,2,8,128]{3,2,1,0:T(8,128)S(1)} %get-tuple-element.22), channel_id=1, source_target_pairs={{0,12},{4,8},{8,4},{12,0},{16,28},{20,24},{24,20},{28,16},{1,13},{... | collective-permute-start | bytes 172040 | tf_op jit(solution)/shard_map/ppermute | solution.py:547
  8.3 0.0 copy-start
  8.3 0.8 %collective-permute-start.4 = (f32[7,2,8,128]{3,2,1,0:T(8,128)S(1)}, f32[7,2,8,128]{3,2,1,0:T(8,128)S(1)}, u32[]{:S(2)}, u32[]{:S(2)}) collective-permute-start(f32[7,2,8,128]{3,2,1,0:T(8,128)S(1)} %get-tuple-element.23), channel_id=1, source_target_pairs={{8,20},{12,16},{16,12},{20,8},{9,21},{13,17},{17,13},{21,9},{10,22... | collective-permute-start | bytes 172040 | tf_op jit(solution)/shard_map/ppermute | solution.py:547
  9.1 2.3 %collective-permute-done.3.refs_1_ = f32[7,2,8,128]{3,2,1,0:T(8,128)S(1)} collective-permute-done((f32[7,2,8,128]{3,2,1,0:T(8,128)S(1)}, f32[7,2,8,128]{3,2,1,0:T(8,128)S(1)}, u32[]{:S(2)}, u32[]{:S(2)}) %collective-permute-start.3) | collective-permute-done | bytes 57376 | tf_op jit(solution)/shard_map/ppermute | solution.py:547
  11.4 0.0 collective-permute-done.4.refs_2_
  11.4 0.0 collective-permute-done.2.refs_0_
  11.4 0.0 collective-permute-done.got0
  11.4 0.0 collective-permute-done.1.got1
  11.4 0.5 %shard_map.85 = (f32[7,16,24,128]{3,2,1,0:T(8,128)S(1)}, f32[7,24,128]{2,1,0:T(8,128)S(1)}, f32[11,8,128]{2,1,0:T(8,128)S(1)}, f32[11,8,128]{2,1,0:T(8,128)S(1)}) custom-call(f32[7,4,16,128]{3,2,1,0:T(8,128)S(1)} %get-tuple-element.19.half0, f32[7,4,16,128]{3,2,1,0:T(8,128)S(1)} %get-tuple-element.20.half1, f32[7,4,16,128]{3,2,1,0:T(8,128)S(1)} %collective-permute-done.got0, ...), custom_call_target="tpu_custom_call" | custom-call | flops 20000000 | bytes 20000 | tf_op jit(solution)/shard_map/pallas_call | solution.py:49
  12.0 0.7 %collective-permute-start.5 = (f32[11,8,128]{2,1,0:T(8,128)S(1)}, f32[11,8,128]{2,1,0:T(8,128)S(1)}, u32[]{:S(2)}, u32[]{:S(2)}) collective-permute-start(f32[11,8,128]{2,1,0:T(8,128)S(1)} %get-tuple-element.26), channel_id=1, source_target_pairs={{1,2},{2,1},{5,6},{6,5},{9,10},{10,9},{13,14},{14,13},{17,18},{18,... | collective-permute-start | bytes 135176 | tf_op jit(solution)/shard_map/ppermute | solution.py:555
  12.6 4.5 %collective-permute-start.6 = (f32[11,8,128]{2,1,0:T(8,128)S(1)}, f32[11,8,128]{2,1,0:T(8,128)S(1)}, u32[]{:S(2)}, u32[]{:S(2)}) collective-permute-start(f32[11,8,128]{2,1,0:T(8,128)S(1)} %get-tuple-element.27), channel_id=1, source_target_pairs={{0,1},{1,0},{2,3},{3,2},{4,5},{5,4},{6,7},{7,6},{8,9},{9,8},{10,11... | collective-permute-start | bytes 135176 | tf_op jit(solution)/shard_map/ppermute | solution.py:556
  17.1 0.0 collective-permute-done.5.got1
  17.1 2.0 %collective-permute-done.6.got0 = f32[11,8,128]{2,1,0:T(8,128)S(1)} collective-permute-done((f32[11,8,128]{2,1,0:T(8,128)S(1)}, f32[11,8,128]{2,1,0:T(8,128)S(1)}, u32[]{:S(2)}, u32[]{:S(2)}) %collective-permute-start.6) | collective-permute-done | bytes 45088 | tf_op jit(solution)/shard_map/ppermute | solution.py:556
  19.1 0.0 copy-done.2
  19.1 0.0 copy-done.1
  19.1 2.7 %shard_map.86 = (f32[3,8,16,128]{3,2,1,0:T(8,128)S(1)}, f32[3,8,16,128]{3,2,1,0:T(8,128)S(1)}, f32[32,1,128]{2,1,0:T(1,128)}, f32[7,24,128]{2,1,0:T(8,128)S(1)}) custom-call(f32[7,16,24,128]{3,2,1,0:T(8,128)S(1)} %get-tuple-element.24.ext, f32[11,8,128]{2,1,0:T(8,128)S(1)} %collective-permute-done.5.got1, f32[11,8,128]{2,1,0:T(8,128)S(1)} %collective-permute-done.6.got0, ...), custom_call_target="tpu_custom_call" | custom-call | flops 20000000 | bytes 20000 | tf_op jit(solution)/shard_map/pallas_call | solution.py:49
  21.9 5.9 %all-to-all-start = ((f32[32,1,128]{2,1,0:T(1,128)}), f32[32,1,128]{2,1,0:T(1,128)S(1)}, u32[]{:S(2)}, u32[]{:S(2)}) async-start(f32[32,1,128]{2,1,0:T(1,128)} %get-tuple-element.29), calls=%async_computation | async-start | bytes 32768 | tf_op jit(solution)/shard_map/all_to_all | solution.py:564
  27.8 0.3 shard_map.87
  28.1 6.8 %all-to-all-done.total = f32[32,1,128]{2,1,0:T(1,128)S(1)} async-done(((f32[32,1,128]{2,1,0:T(1,128)}), f32[32,1,128]{2,1,0:T(1,128)S(1)}, u32[]{:S(2)}, u32[]{:S(2)}) %all-to-all-start) | async-done | bytes 16416 | tf_op jit(solution)/shard_map/all_to_all | solution.py:564
  34.8 0.0 copy-done
  34.8 4.8 %shard_map.88 = (f32[3,8,16,128]{3,2,1,0:T(8,128)}, f32[3,8,16,128]{3,2,1,0:T(8,128)}, f32[3,8,16,128]{3,2,1,0:T(8,128)}, f32[8,16,128]{2,1,0:T(8,128)}) custom-call(f32[7,16,24,128]{3,2,1,0:T(8,128)S(1)} %get-tuple-element.24.ext, f32[7,24,128]{2,1,0:T(8,128)S(1)} %get-tuple-element.25.ends, f32[7,24,128]{2,1,0:T(8,128)S(1)} %get-tuple-element.28.around, ...), custom_call_target="tpu_custom_call" | custom-call | flops 20000000 | bytes 20000 | tf_op jit(solution)/shard_map/pallas_call | solution.py:49
Async XLA Ops:
  0.6 18.5 %copy-start.2 = (s32[8,16,128]{2,1,0:T(8,128)S(1)}, s32[8,16,128]{2,1,0:T(8,128)}, u32[]{:S(2)}) copy-start(s32[8,16,128]{2,1,0:T(8,128)} %lab.1) | copy-start | bytes 196612
  0.6 18.5 %copy-start.1 = (f32[3,8,16,128]{3,2,1,0:T(8,128)S(1)}, f32[3,8,16,128]{3,2,1,0:T(8,128)}, u32[]{:S(2)}) copy-start(f32[3,8,16,128]{3,2,1,0:T(8,128)} %res.3) | copy-start | bytes 589828
  1.9 9.6 %collective-permute-start = (f32[7,4,16,128]{3,2,1,0:T(8,128)S(1)}, f32[7,4,16,128]{3,2,1,0:T(8,128)S(1)}, u32[]{:S(2)}, u32[]{:S(2)}) collective-permute-start(f32[7,4,16,128]{3,2,1,0:T(8,128)S(1)} %get-tuple-element.19.half0), channel_id=1, source_target_pairs={{0,8},{4,12},{8,0},{12,4},{16,24},{20,28},{24,16},{28,20},{1,9},{5... | collective-permute-start | bytes 688136 | tf_op jit(solution)/shard_map/ppermute | solution.py:543
  2.4 9.0 %collective-permute-start.1 = (f32[7,4,16,128]{3,2,1,0:T(8,128)S(1)}, f32[7,4,16,128]{3,2,1,0:T(8,128)S(1)}, u32[]{:S(2)}, u32[]{:S(2)}) collective-permute-start(f32[7,4,16,128]{3,2,1,0:T(8,128)S(1)} %get-tuple-element.20.half1), channel_id=1, source_target_pairs={{8,16},{12,20},{16,8},{20,12},{9,17},{13,21},{17,9},{21,13},{10,18... | collective-permute-start | bytes 688136 | tf_op jit(solution)/shard_map/ppermute | solution.py:543
  3.0 8.4 %collective-permute-start.2 = (f32[7,4,8,128]{3,2,1,0:T(8,128)S(1)}, f32[7,4,8,128]{3,2,1,0:T(8,128)S(1)}, u32[]{:S(2)}, u32[]{:S(2)}) collective-permute-start(f32[7,4,8,128]{3,2,1,0:T(8,128)S(1)} %get-tuple-element.21), channel_id=1, source_target_pairs={{0,4},{4,0},{8,12},{12,8},{16,20},{20,16},{24,28},{28,24},{1,5},{5... | collective-permute-start | bytes 344072 | tf_op jit(solution)/shard_map/ppermute | solution.py:547
  5.6 5.8 %collective-permute-start.3 = (f32[7,2,8,128]{3,2,1,0:T(8,128)S(1)}, f32[7,2,8,128]{3,2,1,0:T(8,128)S(1)}, u32[]{:S(2)}, u32[]{:S(2)}) collective-permute-start(f32[7,2,8,128]{3,2,1,0:T(8,128)S(1)} %get-tuple-element.22), channel_id=1, source_target_pairs={{0,12},{4,8},{8,4},{12,0},{16,28},{20,24},{24,20},{28,16},{1,13},{... | collective-permute-start | bytes 172040 | tf_op jit(solution)/shard_map/ppermute | solution.py:547
  8.3 26.5 %copy-start = (f32[3,8,16,128]{3,2,1,0:T(8,128)S(1)}, f32[3,8,16,128]{3,2,1,0:T(8,128)}, u32[]{:S(2)}) copy-start(f32[3,8,16,128]{3,2,1,0:T(8,128)} %dire.1) | copy-start | bytes 589828
  8.3 3.1 %collective-permute-start.4 = (f32[7,2,8,128]{3,2,1,0:T(8,128)S(1)}, f32[7,2,8,128]{3,2,1,0:T(8,128)S(1)}, u32[]{:S(2)}, u32[]{:S(2)}) collective-permute-start(f32[7,2,8,128]{3,2,1,0:T(8,128)S(1)} %get-tuple-element.23), channel_id=1, source_target_pairs={{8,20},{12,16},{16,12},{20,8},{9,21},{13,17},{17,13},{21,9},{10,22... | collective-permute-start | bytes 172040 | tf_op jit(solution)/shard_map/ppermute | solution.py:547
  12.0 5.1 %collective-permute-start.5 = (f32[11,8,128]{2,1,0:T(8,128)S(1)}, f32[11,8,128]{2,1,0:T(8,128)S(1)}, u32[]{:S(2)}, u32[]{:S(2)}) collective-permute-start(f32[11,8,128]{2,1,0:T(8,128)S(1)} %get-tuple-element.26), channel_id=1, source_target_pairs={{1,2},{2,1},{5,6},{6,5},{9,10},{10,9},{13,14},{14,13},{17,18},{18,... | collective-permute-start | bytes 135176 | tf_op jit(solution)/shard_map/ppermute | solution.py:555
  12.6 6.5 %collective-permute-start.6 = (f32[11,8,128]{2,1,0:T(8,128)S(1)}, f32[11,8,128]{2,1,0:T(8,128)S(1)}, u32[]{:S(2)}, u32[]{:S(2)}) collective-permute-start(f32[11,8,128]{2,1,0:T(8,128)S(1)} %get-tuple-element.27), channel_id=1, source_target_pairs={{0,1},{1,0},{2,3},{3,2},{4,5},{5,4},{6,7},{7,6},{8,9},{9,8},{10,11... | collective-permute-start | bytes 135176 | tf_op jit(solution)/shard_map/ppermute | solution.py:556
  21.9 13.0 %all-to-all-start = ((f32[32,1,128]{2,1,0:T(1,128)}), f32[32,1,128]{2,1,0:T(1,128)S(1)}, u32[]{:S(2)}, u32[]{:S(2)}) async-start(f32[32,1,128]{2,1,0:T(1,128)} %get-tuple-element.29), calls=%async_computation | async-start | bytes 32768 | tf_op jit(solution)/shard_map/all_to_all | solution.py:564

commit v11 on v10

--- a/solution.py
+++ b/solution.py
@@ -108,7 +108,7 @@
                 corner1[f, t] = jnp.where(even_x, low, high)
 
 
-def extend(counts, half0, half1, got0, got1, *refs):
+def extend(counts, half0, half1, got1, got0, *refs):
     nx, ny, nz = counts
     sides, (ext, ends, send1, send0) = refs[:-4], refs[-4:]
     sub = rows_of((8, 128))
@@ -123,7 +123,7 @@
         def strip(which, f, t):
             tiles = []
             for s in range(len(sides) // 3):
-                rows, corner0, corner1 = sides[3 * s : 3 * s + 3]
+                rows, corner1, corner0 = sides[3 * s : 3 * s + 3]
                 ref = rows if which is None else (corner0, corner1)[order[which]]
                 tiles.append(ref[f, t])
             keep = 1.0 if which is None else x_ok[which]
@@ -540,10 +540,11 @@
     )
     halves = packed[:2]
     plane = ("gx", "gy")
-    got = [lax.ppermute(halves[r], plane, swap_pairs((nx, ny), (r, None))) for r in (0, 1)]
+    got = [lax.ppermute(halves[r], plane, swap_pairs((nx, ny), (r, None))) for r in (1, 0)]
     strips = []
     for s in range(rounds_y):
-        for array, turn in zip(packed[2 + 3 * s : 5 + 3 * s], (None, 0, 1)):
+        rows, corner0, corner1 = packed[2 + 3 * s : 5 + 3 * s]
+        for array, turn in ((rows, None), (corner1, 1), (corner0, 0)):
             strips.append(lax.ppermute(array, plane, swap_pairs((nx, ny), (turn, s))))
     hinv, hside = call(functools.partial(inverse_sums, (nx, ny, nz)), [(16, 24, 128), (2, 24, 128)])
     zend = (ZTILES, 8, 128)

time: 39.9 us -> 40.7 us (1.020)
  starting transfers between devices: 18.3 us -> 19.3 us
    ppermute x2, starting transfers between devices: 1.18 us -> 5.03 us  [per_device(): lax.ppermute(halves[r], plane, swap_pairs((nx, ny), (r, None)))]
    all_to_all x1, starting transfers between devices: 5.92 us -> 4.46 us  [per_device(): total = lax.all_to_all(sums, AXES, 0, 0)]
    ppermute x3, starting transfers between devices: 6.06 us -> 4.64 us  [per_device(): strips.append(lax.ppermute(array, plane, swap_pairs((nx, ny), (turn, s))))]
where the time goes in v11:
time: 40.7 us; the launch traced here: 40.5 us
  starting transfers between devices  19.3 us (47%)
  waiting for transfers between devices  10.9 us (27%)
  Pallas kernels  9.55 us (23%)
  between operations  0.72 us (2%)
    pallas_call x5, Pallas kernels, call(): pl.pallas_call(body, out_shape=[jax.ShapeDtypeStruct(shape, f32) for shap...  9.55 us
    all_to_all x1, waiting for transfers between devices, per_device(): total = lax.all_to_all(sums, AXES, 0, 0)  6.77 us
    ppermute x2, starting transfers between devices, per_device(): lax.ppermute(halves[r], plane, swap_pairs((nx, ny), (r, None)))  5.03 us
    ppermute x3, starting transfers between devices, per_device(): strips.append(lax.ppermute(array, plane, swap_pairs((nx, ny), (turn, s))))  4.64 us
    ppermute x1, starting transfers between devices, per_device(): first = lax.ppermute(sends[1], 'gz', swap_pairs((nz,), (0,)))  4.46 us
    all_to_all x1, starting transfers between devices, per_device(): total = lax.all_to_all(sums, AXES, 0, 0)  4.46 us
    ppermute x1, waiting for transfers between devices, per_device(): first = lax.ppermute(sends[1], 'gz', swap_pairs((nz,), (0,)))  2.26 us
    ppermute x3, waiting for transfers between devices, per_device(): strips.append(lax.ppermute(array, plane, swap_pairs((nx, ny), (turn, s))))  1.9 us
  transfers between devices with their start and end apart: 8, of which 3 were waited for; matrix products, arithmetic and copies ran while one was open for 0% of the time, Pallas kernels for 1%

profile of v11, /device:TPU:0, one launch (start us, length us, event | category | flops | bytes accessed | tf_op | source)
XLA Modules:
  0.0 40.5 jit_solution(11581605154085984632)
XLA Ops:
  0.6 0.0 copy-start.2
  0.6 0.0 copy-start.1
  0.7 1.2 %shard_map.84 = (f32[7,4,16,128]{3,2,1,0:T(8,128)S(1)}, f32[7,4,16,128]{3,2,1,0:T(8,128)S(1)}, f32[7,4,8,128]{3,2,1,0:T(8,128)S(1)}, f32[7,2,8,128]{3,2,1,0:T(8,128)S(1)}, f32[7,2,8,128]{3,2,1,0:T(8,128)S(1)}) custom-call(f32[3,8,16,128]{3,2,1,0:T(8,128)} %sol_any.1, f32[3,8,16,128]{3,2,1,0:T(8,128)} %dire.1, f32[8,16,128]{2,1,0:T(8,128)} %den_any.1, ...), custom_call_target="tpu_custom_call" | custom-call | flops 20000000 | bytes 20000 | tf_op jit(solution)/shard_map/pallas_call | solution.py:49
  1.9 0.7 %collective-permute-start = (f32[7,4,16,128]{3,2,1,0:T(8,128)S(1)}, f32[7,4,16,128]{3,2,1,0:T(8,128)S(1)}, u32[]{:S(2)}, u32[]{:S(2)}) collective-permute-start(f32[7,4,16,128]{3,2,1,0:T(8,128)S(1)} %get-tuple-element.20.half1), channel_id=1, source_target_pairs={{8,16},{12,20},{16,8},{20,12},{9,17},{13,21},{17,9},{21,13},{10,18... | collective-permute-start | bytes 688136 | tf_op jit(solution)/shard_map/ppermute | solution.py:543
  2.5 4.4 %collective-permute-start.1 = (f32[7,4,16,128]{3,2,1,0:T(8,128)S(1)}, f32[7,4,16,128]{3,2,1,0:T(8,128)S(1)}, u32[]{:S(2)}, u32[]{:S(2)}) collective-permute-start(f32[7,4,16,128]{3,2,1,0:T(8,128)S(1)} %get-tuple-element.19.half0), channel_id=1, source_target_pairs={{0,8},{4,12},{8,0},{12,4},{16,24},{20,28},{24,16},{28,20},{1,9},{5... | collective-permute-start | bytes 688136 | tf_op jit(solution)/shard_map/ppermute | solution.py:543
  6.9 1.5 %collective-permute-start.2 = (f32[7,4,8,128]{3,2,1,0:T(8,128)S(1)}, f32[7,4,8,128]{3,2,1,0:T(8,128)S(1)}, u32[]{:S(2)}, u32[]{:S(2)}) collective-permute-start(f32[7,4,8,128]{3,2,1,0:T(8,128)S(1)} %get-tuple-element.21), channel_id=1, source_target_pairs={{0,4},{4,0},{8,12},{12,8},{16,20},{20,16},{24,28},{28,24},{1,5},{5... | collective-permute-start | bytes 344072 | tf_op jit(solution)/shard_map/ppermute | solution.py:548
  8.4 0.7 %collective-permute-start.3 = (f32[7,2,8,128]{3,2,1,0:T(8,128)S(1)}, f32[7,2,8,128]{3,2,1,0:T(8,128)S(1)}, u32[]{:S(2)}, u32[]{:S(2)}) collective-permute-start(f32[7,2,8,128]{3,2,1,0:T(8,128)S(1)} %get-tuple-element.22), channel_id=1, source_target_pairs={{8,20},{12,16},{16,12},{20,8},{9,21},{13,17},{17,13},{21,9},{10,22... | collective-permute-start | bytes 172040 | tf_op jit(solution)/shard_map/ppermute | solution.py:548
  9.1 0.0 copy-start
  9.1 2.5 %collective-permute-start.4 = (f32[7,2,8,128]{3,2,1,0:T(8,128)S(1)}, f32[7,2,8,128]{3,2,1,0:T(8,128)S(1)}, u32[]{:S(2)}, u32[]{:S(2)}) collective-permute-start(f32[7,2,8,128]{3,2,1,0:T(8,128)S(1)} %get-tuple-element.23), channel_id=1, source_target_pairs={{0,12},{4,8},{8,4},{12,0},{16,28},{20,24},{24,20},{28,16},{1,13},{... | collective-permute-start | bytes 172040 | tf_op jit(solution)/shard_map/ppermute | solution.py:548
  11.5 0.0 collective-permute-done.3.refs_1_
  11.6 1.9 %collective-permute-done.4.refs_2_ = f32[7,2,8,128]{3,2,1,0:T(8,128)S(1)} collective-permute-done((f32[7,2,8,128]{3,2,1,0:T(8,128)S(1)}, f32[7,2,8,128]{3,2,1,0:T(8,128)S(1)}, u32[]{:S(2)}, u32[]{:S(2)}) %collective-permute-start.4) | collective-permute-done | bytes 57376 | tf_op jit(solution)/shard_map/ppermute | solution.py:548
  13.4 0.0 collective-permute-done.2.refs_0_
  13.4 0.0 collective-permute-done.got1
  13.4 0.0 collective-permute-done.1.got0
  13.5 0.5 %shard_map.85 = (f32[7,16,24,128]{3,2,1,0:T(8,128)S(1)}, f32[7,24,128]{2,1,0:T(8,128)S(1)}, f32[11,8,128]{2,1,0:T(8,128)S(1)}, f32[11,8,128]{2,1,0:T(8,128)S(1)}) custom-call(f32[7,4,16,128]{3,2,1,0:T(8,128)S(1)} %get-tuple-element.19.half0, f32[7,4,16,128]{3,2,1,0:T(8,128)S(1)} %get-tuple-element.20.half1, f32[7,4,16,128]{3,2,1,0:T(8,128)S(1)} %collective-permute-done.got1, ...), custom_call_target="tpu_custom_call" | custom-call | flops 20000000 | bytes 20000 | tf_op jit(solution)/shard_map/pallas_call | solution.py:49
  14.0 0.7 %collective-permute-start.5 = (f32[11,8,128]{2,1,0:T(8,128)S(1)}, f32[11,8,128]{2,1,0:T(8,128)S(1)}, u32[]{:S(2)}, u32[]{:S(2)}) collective-permute-start(f32[11,8,128]{2,1,0:T(8,128)S(1)} %get-tuple-element.26), channel_id=1, source_target_pairs={{1,2},{2,1},{5,6},{6,5},{9,10},{10,9},{13,14},{14,13},{17,18},{18,... | collective-permute-start | bytes 135176 | tf_op jit(solution)/shard_map/ppermute | solution.py:556
  14.7 4.5 %collective-permute-start.6 = (f32[11,8,128]{2,1,0:T(8,128)S(1)}, f32[11,8,128]{2,1,0:T(8,128)S(1)}, u32[]{:S(2)}, u32[]{:S(2)}) collective-permute-start(f32[11,8,128]{2,1,0:T(8,128)S(1)} %get-tuple-element.27), channel_id=1, source_target_pairs={{0,1},{1,0},{2,3},{3,2},{4,5},{5,4},{6,7},{7,6},{8,9},{9,8},{10,11... | collective-permute-start | bytes 135176 | tf_op jit(solution)/shard_map/ppermute | solution.py:557
  19.1 0.0 collective-permute-done.5.got1
  19.1 2.3 %collective-permute-done.6.got0 = f32[11,8,128]{2,1,0:T(8,128)S(1)} collective-permute-done((f32[11,8,128]{2,1,0:T(8,128)S(1)}, f32[11,8,128]{2,1,0:T(8,128)S(1)}, u32[]{:S(2)}, u32[]{:S(2)}) %collective-permute-start.6) | collective-permute-done | bytes 45088 | tf_op jit(solution)/shard_map/ppermute | solution.py:557
  21.4 0.0 copy-done.2
  21.4 0.0 copy-done.1
  21.4 2.7 %shard_map.86 = (f32[3,8,16,128]{3,2,1,0:T(8,128)S(1)}, f32[3,8,16,128]{3,2,1,0:T(8,128)S(1)}, f32[32,1,128]{2,1,0:T(1,128)}, f32[7,24,128]{2,1,0:T(8,128)S(1)}) custom-call(f32[7,16,24,128]{3,2,1,0:T(8,128)S(1)} %get-tuple-element.24.ext, f32[11,8,128]{2,1,0:T(8,128)S(1)} %collective-permute-done.5.got1, f32[11,8,128]{2,1,0:T(8,128)S(1)} %collective-permute-done.6.got0, ...), custom_call_target="tpu_custom_call" | custom-call | flops 20000000 | bytes 20000 | tf_op jit(solution)/shard_map/pallas_call | solution.py:49
  24.1 4.5 %all-to-all-start = ((f32[32,1,128]{2,1,0:T(1,128)}), f32[32,1,128]{2,1,0:T(1,128)S(1)}, u32[]{:S(2)}, u32[]{:S(2)}) async-start(f32[32,1,128]{2,1,0:T(1,128)} %get-tuple-element.29), calls=%async_computation | async-start | bytes 32768 | tf_op jit(solution)/shard_map/all_to_all | solution.py:565
  28.6 0.3 shard_map.87
  28.9 6.8 %all-to-all-done.total = f32[32,1,128]{2,1,0:T(1,128)S(1)} async-done(((f32[32,1,128]{2,1,0:T(1,128)}), f32[32,1,128]{2,1,0:T(1,128)S(1)}, u32[]{:S(2)}, u32[]{:S(2)}) %all-to-all-start) | async-done | bytes 16416 | tf_op jit(solution)/shard_map/all_to_all | solution.py:565
  35.6 0.0 copy-done
  35.6 4.8 %shard_map.88 = (f32[3,8,16,128]{3,2,1,0:T(8,128)}, f32[3,8,16,128]{3,2,1,0:T(8,128)}, f32[3,8,16,128]{3,2,1,0:T(8,128)}, f32[8,16,128]{2,1,0:T(8,128)}) custom-call(f32[7,16,24,128]{3,2,1,0:T(8,128)S(1)} %get-tuple-element.24.ext, f32[7,24,128]{2,1,0:T(8,128)S(1)} %get-tuple-element.25.ends, f32[7,24,128]{2,1,0:T(8,128)S(1)} %get-tuple-element.28.around, ...), custom_call_target="tpu_custom_call" | custom-call | flops 20000000 | bytes 20000 | tf_op jit(solution)/shard_map/pallas_call | solution.py:49
Async XLA Ops:
  0.6 20.8 %copy-start.2 = (s32[8,16,128]{2,1,0:T(8,128)S(1)}, s32[8,16,128]{2,1,0:T(8,128)}, u32[]{:S(2)}) copy-start(s32[8,16,128]{2,1,0:T(8,128)} %lab.1) | copy-start | bytes 196612
  0.6 20.8 %copy-start.1 = (f32[3,8,16,128]{3,2,1,0:T(8,128)S(1)}, f32[3,8,16,128]{3,2,1,0:T(8,128)}, u32[]{:S(2)}) copy-start(f32[3,8,16,128]{3,2,1,0:T(8,128)} %res.3) | copy-start | bytes 589828
  1.9 11.6 %collective-permute-start = (f32[7,4,16,128]{3,2,1,0:T(8,128)S(1)}, f32[7,4,16,128]{3,2,1,0:T(8,128)S(1)}, u32[]{:S(2)}, u32[]{:S(2)}) collective-permute-start(f32[7,4,16,128]{3,2,1,0:T(8,128)S(1)} %get-tuple-element.20.half1), channel_id=1, source_target_pairs={{8,16},{12,20},{16,8},{20,12},{9,17},{13,21},{17,9},{21,13},{10,18... | collective-permute-start | bytes 688136 | tf_op jit(solution)/shard_map/ppermute | solution.py:543
  2.5 10.9 %collective-permute-start.1 = (f32[7,4,16,128]{3,2,1,0:T(8,128)S(1)}, f32[7,4,16,128]{3,2,1,0:T(8,128)S(1)}, u32[]{:S(2)}, u32[]{:S(2)}) collective-permute-start(f32[7,4,16,128]{3,2,1,0:T(8,128)S(1)} %get-tuple-element.19.half0), channel_id=1, source_target_pairs={{0,8},{4,12},{8,0},{12,4},{16,24},{20,28},{24,16},{28,20},{1,9},{5... | collective-permute-start | bytes 688136 | tf_op jit(solution)/shard_map/ppermute | solution.py:543
  6.9 6.6 %collective-permute-start.2 = (f32[7,4,8,128]{3,2,1,0:T(8,128)S(1)}, f32[7,4,8,128]{3,2,1,0:T(8,128)S(1)}, u32[]{:S(2)}, u32[]{:S(2)}) collective-permute-start(f32[7,4,8,128]{3,2,1,0:T(8,128)S(1)} %get-tuple-element.21), channel_id=1, source_target_pairs={{0,4},{4,0},{8,12},{12,8},{16,20},{20,16},{24,28},{28,24},{1,5},{5... | collective-permute-start | bytes 344072 | tf_op jit(solution)/shard_map/ppermute | solution.py:548
  8.4 3.1 %collective-permute-start.3 = (f32[7,2,8,128]{3,2,1,0:T(8,128)S(1)}, f32[7,2,8,128]{3,2,1,0:T(8,128)S(1)}, u32[]{:S(2)}, u32[]{:S(2)}) collective-permute-start(f32[7,2,8,128]{3,2,1,0:T(8,128)S(1)} %get-tuple-element.22), channel_id=1, source_target_pairs={{8,20},{12,16},{16,12},{20,8},{9,21},{13,17},{17,13},{21,9},{10,22... | collective-permute-start | bytes 172040 | tf_op jit(solution)/shard_map/ppermute | solution.py:548
  9.1 26.6 %copy-start = (f32[3,8,16,128]{3,2,1,0:T(8,128)S(1)}, f32[3,8,16,128]{3,2,1,0:T(8,128)}, u32[]{:S(2)}) copy-start(f32[3,8,16,128]{3,2,1,0:T(8,128)} %dire.1) | copy-start | bytes 589828
  9.1 4.4 %collective-permute-start.4 = (f32[7,2,8,128]{3,2,1,0:T(8,128)S(1)}, f32[7,2,8,128]{3,2,1,0:T(8,128)S(1)}, u32[]{:S(2)}, u32[]{:S(2)}) collective-permute-start(f32[7,2,8,128]{3,2,1,0:T(8,128)S(1)} %get-tuple-element.23), channel_id=1, source_target_pairs={{0,12},{4,8},{8,4},{12,0},{16,28},{20,24},{24,20},{28,16},{1,13},{... | collective-permute-start | bytes 172040 | tf_op jit(solution)/shard_map/ppermute | solution.py:548
  14.0 5.1 %collective-permute-start.5 = (f32[11,8,128]{2,1,0:T(8,128)S(1)}, f32[11,8,128]{2,1,0:T(8,128)S(1)}, u32[]{:S(2)}, u32[]{:S(2)}) collective-permute-start(f32[11,8,128]{2,1,0:T(8,128)S(1)} %get-tuple-element.26), channel_id=1, source_target_pairs={{1,2},{2,1},{5,6},{6,5},{9,10},{10,9},{13,14},{14,13},{17,18},{18,... | collective-permute-start | bytes 135176 | tf_op jit(solution)/shard_map/ppermute | solution.py:556
  14.7 6.7 %collective-permute-start.6 = (f32[11,8,128]{2,1,0:T(8,128)S(1)}, f32[11,8,128]{2,1,0:T(8,128)S(1)}, u32[]{:S(2)}, u32[]{:S(2)}) collective-permute-start(f32[11,8,128]{2,1,0:T(8,128)S(1)} %get-tuple-element.27), channel_id=1, source_target_pairs={{0,1},{1,0},{2,3},{3,2},{4,5},{5,4},{6,7},{7,6},{8,9},{9,8},{10,11... | collective-permute-start | bytes 135176 | tf_op jit(solution)/shard_map/ppermute | solution.py:557
  24.1 11.5 %all-to-all-start = ((f32[32,1,128]{2,1,0:T(1,128)}), f32[32,1,128]{2,1,0:T(1,128)S(1)}, u32[]{:S(2)}, u32[]{:S(2)}) async-start(f32[32,1,128]{2,1,0:T(1,128)} %get-tuple-element.29), calls=%async_computation | async-start | bytes 32768 | tf_op jit(solution)/shard_map/all_to_all | solution.py:565

commit v12 on v10

--- a/solution.py
+++ b/solution.py
@@ -42,13 +42,16 @@
     return value if amount == 0 else pltpu.roll(value, amount, axis)
 
 
-def call(body, outs, *args, scratch=(), cost=20000, far=(), far_out=False):
+def call(body, outs, *args, scratch=(), cost=20000, far=(), far_out=False, near_out=()):
     args = [
         pltpu.with_memory_space_constraint(a, pltpu.HBM) if i in far else a for i, a in enumerate(args)
     ]
     return pl.pallas_call(
         body,
-        out_shape=[jax.ShapeDtypeStruct(shape, f32) for shape in outs],
+        out_shape=[
+            pltpu.VMEM(shape, f32) if i in near_out else jax.ShapeDtypeStruct(shape, f32)
+            for i, shape in enumerate(outs)
+        ],
         in_specs=[
             pl.BlockSpec(memory_space=pl.ANY if i in far else pltpu.VMEM) for i in range(len(args))
         ],
@@ -560,6 +563,7 @@
         [field, field, (nx * ny * nz, 1, 128), (7, 24, 128)],
         ext, *ends_got, residual, labels,
         scratch=[pltpu.VMEM((4, 3, 3, 10, 16, 128), f32)],
+        near_out=(2,),
     )
     total = lax.all_to_all(sums, AXES, 0, 0)
     return tuple(

time: 39.9 us -> 39.9 us (level)
  no operation moved by 1% of the time
where the time goes in v12:
time: 39.9 us; the launch traced here: 39.7 us
  starting transfers between devices  18.3 us (46%)
  waiting for transfers between devices  11.1 us (28%)
  Pallas kernels  9.55 us (24%)
  between operations  0.72 us (2%)
    pallas_call x5, Pallas kernels, call(): pl.pallas_call(body, out_shape=[pltpu.VMEM(shape, f32) if i in near_out e...  9.55 us
    all_to_all x1, waiting for transfers between devices, per_device(): total = lax.all_to_all(sums, AXES, 0, 0)  6.77 us
    ppermute x3, starting transfers between devices, per_device(): strips.append(lax.ppermute(array, plane, swap_pairs((nx, ny), (turn, s))))  6.06 us
    all_to_all x1, starting transfers between devices, per_device(): total = lax.all_to_all(sums, AXES, 0, 0)  5.92 us
    ppermute x1, starting transfers between devices, per_device(): first = lax.ppermute(sends[1], 'gz', swap_pairs((nz,), (0,)))  4.46 us
    ppermute x3, waiting for transfers between devices, per_device(): strips.append(lax.ppermute(array, plane, swap_pairs((nx, ny), (turn, s))))  2.3 us
    ppermute x1, waiting for transfers between devices, per_device(): first = lax.ppermute(sends[1], 'gz', swap_pairs((nz,), (0,)))  2.02 us
    ppermute x2, starting transfers between devices, per_device(): lax.ppermute(halves[r], plane, swap_pairs((nx, ny), (r, None)))  1.18 us
  transfers between devices with their start and end apart: 8, of which 3 were waited for; matrix products, arithmetic and copies ran while one was open for 0% of the time, Pallas kernels for 1%

profile of v12, /device:TPU:0, one launch (start us, length us, event | category | flops | bytes accessed | tf_op | source)
XLA Modules:
  0.0 39.7 jit_solution(15943287776660232251)
XLA Ops:
  0.6 0.0 copy-start.2
  0.6 0.0 copy-start.1
  0.7 1.2 %shard_map.84 = (f32[7,4,16,128]{3,2,1,0:T(8,128)S(1)}, f32[7,4,16,128]{3,2,1,0:T(8,128)S(1)}, f32[7,4,8,128]{3,2,1,0:T(8,128)S(1)}, f32[7,2,8,128]{3,2,1,0:T(8,128)S(1)}, f32[7,2,8,128]{3,2,1,0:T(8,128)S(1)}) custom-call(f32[3,8,16,128]{3,2,1,0:T(8,128)} %sol_any.1, f32[3,8,16,128]{3,2,1,0:T(8,128)} %dire.1, f32[8,16,128]{2,1,0:T(8,128)} %den_any.1, ...), custom_call_target="tpu_custom_call" | custom-call | flops 20000000 | bytes 20000 | tf_op jit(solution)/shard_map/pallas_call | solution.py:49
  1.9 0.5 %collective-permute-start = (f32[7,4,16,128]{3,2,1,0:T(8,128)S(1)}, f32[7,4,16,128]{3,2,1,0:T(8,128)S(1)}, u32[]{:S(2)}, u32[]{:S(2)}) collective-permute-start(f32[7,4,16,128]{3,2,1,0:T(8,128)S(1)} %get-tuple-element.19.half0), channel_id=1, source_target_pairs={{0,8},{4,12},{8,0},{12,4},{16,24},{20,28},{24,16},{28,20},{1,9},{5... | collective-permute-start | bytes 688136 | tf_op jit(solution)/shard_map/ppermute | solution.py:546
  2.4 0.7 %collective-permute-start.1 = (f32[7,4,16,128]{3,2,1,0:T(8,128)S(1)}, f32[7,4,16,128]{3,2,1,0:T(8,128)S(1)}, u32[]{:S(2)}, u32[]{:S(2)}) collective-permute-start(f32[7,4,16,128]{3,2,1,0:T(8,128)S(1)} %get-tuple-element.20.half1), channel_id=1, source_target_pairs={{8,16},{12,20},{16,8},{20,12},{9,17},{13,21},{17,9},{21,13},{10,18... | collective-permute-start | bytes 688136 | tf_op jit(solution)/shard_map/ppermute | solution.py:546
  3.0 2.6 %collective-permute-start.2 = (f32[7,4,8,128]{3,2,1,0:T(8,128)S(1)}, f32[7,4,8,128]{3,2,1,0:T(8,128)S(1)}, u32[]{:S(2)}, u32[]{:S(2)}) collective-permute-start(f32[7,4,8,128]{3,2,1,0:T(8,128)S(1)} %get-tuple-element.21), channel_id=1, source_target_pairs={{0,4},{4,0},{8,12},{12,8},{16,20},{20,16},{24,28},{28,24},{1,5},{5... | collective-permute-start | bytes 344072 | tf_op jit(solution)/shard_map/ppermute | solution.py:550
  5.6 2.7 %collective-permute-start.3 = (f32[7,2,8,128]{3,2,1,0:T(8,128)S(1)}, f32[7,2,8,128]{3,2,1,0:T(8,128)S(1)}, u32[]{:S(2)}, u32[]{:S(2)}) collective-permute-start(f32[7,2,8,128]{3,2,1,0:T(8,128)S(1)} %get-tuple-element.22), channel_id=1, source_target_pairs={{0,12},{4,8},{8,4},{12,0},{16,28},{20,24},{24,20},{28,16},{1,13},{... | collective-permute-start | bytes 172040 | tf_op jit(solution)/shard_map/ppermute | solution.py:550
  8.3 0.0 copy-start
  8.3 0.8 %collective-permute-start.4 = (f32[7,2,8,128]{3,2,1,0:T(8,128)S(1)}, f32[7,2,8,128]{3,2,1,0:T(8,128)S(1)}, u32[]{:S(2)}, u32[]{:S(2)}) collective-permute-start(f32[7,2,8,128]{3,2,1,0:T(8,128)S(1)} %get-tuple-element.23), channel_id=1, source_target_pairs={{8,20},{12,16},{16,12},{20,8},{9,21},{13,17},{17,13},{21,9},{10,22... | collective-permute-start | bytes 172040 | tf_op jit(solution)/shard_map/ppermute | solution.py:550
  9.1 2.3 %collective-permute-done.3.refs_1_ = f32[7,2,8,128]{3,2,1,0:T(8,128)S(1)} collective-permute-done((f32[7,2,8,128]{3,2,1,0:T(8,128)S(1)}, f32[7,2,8,128]{3,2,1,0:T(8,128)S(1)}, u32[]{:S(2)}, u32[]{:S(2)}) %collective-permute-start.3) | collective-permute-done | bytes 57376 | tf_op jit(solution)/shard_map/ppermute | solution.py:550
  11.4 0.0 collective-permute-done.4.refs_2_
  11.4 0.0 collective-permute-done.2.refs_0_
  11.4 0.0 collective-permute-done.got0
  11.4 0.0 collective-permute-done.1.got1
  11.4 0.5 %shard_map.85 = (f32[7,16,24,128]{3,2,1,0:T(8,128)S(1)}, f32[7,24,128]{2,1,0:T(8,128)S(1)}, f32[11,8,128]{2,1,0:T(8,128)S(1)}, f32[11,8,128]{2,1,0:T(8,128)S(1)}) custom-call(f32[7,4,16,128]{3,2,1,0:T(8,128)S(1)} %get-tuple-element.19.half0, f32[7,4,16,128]{3,2,1,0:T(8,128)S(1)} %get-tuple-element.20.half1, f32[7,4,16,128]{3,2,1,0:T(8,128)S(1)} %collective-permute-done.got0, ...), custom_call_target="tpu_custom_call" | custom-call | flops 20000000 | bytes 20000 | tf_op jit(solution)/shard_map/pallas_call | solution.py:49
  12.0 0.7 %collective-permute-start.5 = (f32[11,8,128]{2,1,0:T(8,128)S(1)}, f32[11,8,128]{2,1,0:T(8,128)S(1)}, u32[]{:S(2)}, u32[]{:S(2)}) collective-permute-start(f32[11,8,128]{2,1,0:T(8,128)S(1)} %get-tuple-element.26), channel_id=1, source_target_pairs={{1,2},{2,1},{5,6},{6,5},{9,10},{10,9},{13,14},{14,13},{17,18},{18,... | collective-permute-start | bytes 135176 | tf_op jit(solution)/shard_map/ppermute | solution.py:558
  12.6 4.5 %collective-permute-start.6 = (f32[11,8,128]{2,1,0:T(8,128)S(1)}, f32[11,8,128]{2,1,0:T(8,128)S(1)}, u32[]{:S(2)}, u32[]{:S(2)}) collective-permute-start(f32[11,8,128]{2,1,0:T(8,128)S(1)} %get-tuple-element.27), channel_id=1, source_target_pairs={{0,1},{1,0},{2,3},{3,2},{4,5},{5,4},{6,7},{7,6},{8,9},{9,8},{10,11... | collective-permute-start | bytes 135176 | tf_op jit(solution)/shard_map/ppermute | solution.py:559
  17.1 0.0 collective-permute-done.5.got1
  17.1 2.0 %collective-permute-done.6.got0 = f32[11,8,128]{2,1,0:T(8,128)S(1)} collective-permute-done((f32[11,8,128]{2,1,0:T(8,128)S(1)}, f32[11,8,128]{2,1,0:T(8,128)S(1)}, u32[]{:S(2)}, u32[]{:S(2)}) %collective-permute-start.6) | collective-permute-done | bytes 45088 | tf_op jit(solution)/shard_map/ppermute | solution.py:559
  19.1 0.0 copy-done.2
  19.1 0.0 copy-done.1
  19.1 2.7 %shard_map.86 = (f32[3,8,16,128]{3,2,1,0:T(8,128)S(1)}, f32[3,8,16,128]{3,2,1,0:T(8,128)S(1)}, f32[32,1,128]{2,1,0:T(1,128)}, f32[7,24,128]{2,1,0:T(8,128)S(1)}) custom-call(f32[7,16,24,128]{3,2,1,0:T(8,128)S(1)} %get-tuple-element.24.ext, f32[11,8,128]{2,1,0:T(8,128)S(1)} %collective-permute-done.5.got1, f32[11,8,128]{2,1,0:T(8,128)S(1)} %collective-permute-done.6.got0, ...), custom_call_target="tpu_custom_call" | custom-call | flops 20000000 | bytes 20000 | tf_op jit(solution)/shard_map/pallas_call | solution.py:49
  21.9 5.9 %all-to-all-start = ((f32[32,1,128]{2,1,0:T(1,128)}), f32[32,1,128]{2,1,0:T(1,128)S(1)}, u32[]{:S(2)}, u32[]{:S(2)}) async-start(f32[32,1,128]{2,1,0:T(1,128)} %get-tuple-element.29), calls=%async_computation | async-start | bytes 32768 | tf_op jit(solution)/shard_map/all_to_all | solution.py:568
  27.8 0.3 shard_map.87
  28.1 6.8 %all-to-all-done.total = f32[32,1,128]{2,1,0:T(1,128)S(1)} async-done(((f32[32,1,128]{2,1,0:T(1,128)}), f32[32,1,128]{2,1,0:T(1,128)S(1)}, u32[]{:S(2)}, u32[]{:S(2)}) %all-to-all-start) | async-done | bytes 16416 | tf_op jit(solution)/shard_map/all_to_all | solution.py:568
  34.8 0.0 copy-done
  34.8 4.8 %shard_map.88 = (f32[3,8,16,128]{3,2,1,0:T(8,128)}, f32[3,8,16,128]{3,2,1,0:T(8,128)}, f32[3,8,16,128]{3,2,1,0:T(8,128)}, f32[8,16,128]{2,1,0:T(8,128)}) custom-call(f32[7,16,24,128]{3,2,1,0:T(8,128)S(1)} %get-tuple-element.24.ext, f32[7,24,128]{2,1,0:T(8,128)S(1)} %get-tuple-element.25.ends, f32[7,24,128]{2,1,0:T(8,128)S(1)} %get-tuple-element.28.around, ...), custom_call_target="tpu_custom_call" | custom-call | flops 20000000 | bytes 20000 | tf_op jit(solution)/shard_map/pallas_call | solution.py:49
Async XLA Ops:
  0.6 18.5 %copy-start.2 = (s32[8,16,128]{2,1,0:T(8,128)S(1)}, s32[8,16,128]{2,1,0:T(8,128)}, u32[]{:S(2)}) copy-start(s32[8,16,128]{2,1,0:T(8,128)} %lab.1) | copy-start | bytes 196612
  0.6 18.5 %copy-start.1 = (f32[3,8,16,128]{3,2,1,0:T(8,128)S(1)}, f32[3,8,16,128]{3,2,1,0:T(8,128)}, u32[]{:S(2)}) copy-start(f32[3,8,16,128]{3,2,1,0:T(8,128)} %res.3) | copy-start | bytes 589828
  1.9 9.6 %collective-permute-start = (f32[7,4,16,128]{3,2,1,0:T(8,128)S(1)}, f32[7,4,16,128]{3,2,1,0:T(8,128)S(1)}, u32[]{:S(2)}, u32[]{:S(2)}) collective-permute-start(f32[7,4,16,128]{3,2,1,0:T(8,128)S(1)} %get-tuple-element.19.half0), channel_id=1, source_target_pairs={{0,8},{4,12},{8,0},{12,4},{16,24},{20,28},{24,16},{28,20},{1,9},{5... | collective-permute-start | bytes 688136 | tf_op jit(solution)/shard_map/ppermute | solution.py:546
  2.4 9.0 %collective-permute-start.1 = (f32[7,4,16,128]{3,2,1,0:T(8,128)S(1)}, f32[7,4,16,128]{3,2,1,0:T(8,128)S(1)}, u32[]{:S(2)}, u32[]{:S(2)}) collective-permute-start(f32[7,4,16,128]{3,2,1,0:T(8,128)S(1)} %get-tuple-element.20.half1), channel_id=1, source_target_pairs={{8,16},{12,20},{16,8},{20,12},{9,17},{13,21},{17,9},{21,13},{10,18... | collective-permute-start | bytes 688136 | tf_op jit(solution)/shard_map/ppermute | solution.py:546
  3.0 8.4 %collective-permute-start.2 = (f32[7,4,8,128]{3,2,1,0:T(8,128)S(1)}, f32[7,4,8,128]{3,2,1,0:T(8,128)S(1)}, u32[]{:S(2)}, u32[]{:S(2)}) collective-permute-start(f32[7,4,8,128]{3,2,1,0:T(8,128)S(1)} %get-tuple-element.21), channel_id=1, source_target_pairs={{0,4},{4,0},{8,12},{12,8},{16,20},{20,16},{24,28},{28,24},{1,5},{5... | collective-permute-start | bytes 344072 | tf_op jit(solution)/shard_map/ppermute | solution.py:550
  5.6 5.8 %collective-permute-start.3 = (f32[7,2,8,128]{3,2,1,0:T(8,128)S(1)}, f32[7,2,8,128]{3,2,1,0:T(8,128)S(1)}, u32[]{:S(2)}, u32[]{:S(2)}) collective-permute-start(f32[7,2,8,128]{3,2,1,0:T(8,128)S(1)} %get-tuple-element.22), channel_id=1, source_target_pairs={{0,12},{4,8},{8,4},{12,0},{16,28},{20,24},{24,20},{28,16},{1,13},{... | collective-permute-start | bytes 172040 | tf_op jit(solution)/shard_map/ppermute | solution.py:550
  8.3 26.5 %copy-start = (f32[3,8,16,128]{3,2,1,0:T(8,128)S(1)}, f32[3,8,16,128]{3,2,1,0:T(8,128)}, u32[]{:S(2)}) copy-start(f32[3,8,16,128]{3,2,1,0:T(8,128)} %dire.1) | copy-start | bytes 589828
  8.3 3.1 %collective-permute-start.4 = (f32[7,2,8,128]{3,2,1,0:T(8,128)S(1)}, f32[7,2,8,128]{3,2,1,0:T(8,128)S(1)}, u32[]{:S(2)}, u32[]{:S(2)}) collective-permute-start(f32[7,2,8,128]{3,2,1,0:T(8,128)S(1)} %get-tuple-element.23), channel_id=1, source_target_pairs={{8,20},{12,16},{16,12},{20,8},{9,21},{13,17},{17,13},{21,9},{10,22... | collective-permute-start | bytes 172040 | tf_op jit(solution)/shard_map/ppermute | solution.py:550
  12.0 5.1 %collective-permute-start.5 = (f32[11,8,128]{2,1,0:T(8,128)S(1)}, f32[11,8,128]{2,1,0:T(8,128)S(1)}, u32[]{:S(2)}, u32[]{:S(2)}) collective-permute-start(f32[11,8,128]{2,1,0:T(8,128)S(1)} %get-tuple-element.26), channel_id=1, source_target_pairs={{1,2},{2,1},{5,6},{6,5},{9,10},{10,9},{13,14},{14,13},{17,18},{18,... | collective-permute-start | bytes 135176 | tf_op jit(solution)/shard_map/ppermute | solution.py:558
  12.6 6.5 %collective-permute-start.6 = (f32[11,8,128]{2,1,0:T(8,128)S(1)}, f32[11,8,128]{2,1,0:T(8,128)S(1)}, u32[]{:S(2)}, u32[]{:S(2)}) collective-permute-start(f32[11,8,128]{2,1,0:T(8,128)S(1)} %get-tuple-element.27), channel_id=1, source_target_pairs={{0,1},{1,0},{2,3},{3,2},{4,5},{5,4},{6,7},{7,6},{8,9},{9,8},{10,11... | collective-permute-start | bytes 135176 | tf_op jit(solution)/shard_map/ppermute | solution.py:559
  21.9 13.0 %all-to-all-start = ((f32[32,1,128]{2,1,0:T(1,128)}), f32[32,1,128]{2,1,0:T(1,128)S(1)}, u32[]{:S(2)}, u32[]{:S(2)}) async-start(f32[32,1,128]{2,1,0:T(1,128)} %get-tuple-element.29), calls=%async_computation | async-start | bytes 32768 | tf_op jit(solution)/shard_map/all_to_all | solution.py:568
